TPU v7x, 256 devices: a whole 4x4x8 slice. The times are simulated.
256 devices in a mesh: img: 64 (over y, z, core), mp: 4 (over x).
Axes of the slice: x: 4, y: 4, z: 8, core: 2. Of those that a mesh axis runs over, the one named last changes fastest.
Arguments:
- patches: bfloat16 [512, 96, 1024], P('img'), may hold values from -5 to 5
- encoder_proj: bfloat16 [1024, 3, 1024], P(None, None, 'mp'), may hold values from -5.125 to 5.125
- encoder_out: bfloat16 [1024, 1024], P('mp'), may hold values from -0.1875 to 0.1875
- decoder_embed: bfloat16 [1024, 768], replicated, may hold values from -0.1875 to 0.1875
- decoder_proj: bfloat16 [768, 3, 768], P(None, None, 'mp'), may hold values from -5.9178403 to 5.9178403
- decoder_out: bfloat16 [768, 768], P('mp'), may hold values from -0.21875 to 0.21875
- head_weight: bfloat16 [768, 4], replicated, may hold values from -0.21875 to 0.21875
- partners: int32 [512, 8], P('img'), may hold values from 0 to 511, as said below
- depths: float32 [512, 96], P('img', 'mp'), may hold values from 1 to 4
- camera_poses: float32 [12, 512], P(None, 'img'), may hold values from -3 to 3
- valid_mask: int32 [512, 96], P('img', 'mp'), may hold values 0 or 1
Outputs:
- pointmap: float32 [4, 4096, 96], P(None, 'img', 'mp')
- new_depths: float32 [512, 96], P('img', 'mp')
- new_poses: float32 [12, 512], P(None, 'img')
Inputs may be any that keep to these rules, and one draw needn't show every extreme that they name: partners[a, k] is never a. Among the 64 partners of the images of one device, at most 2 are held by any one device (images 8 o to 8 o + 7 for device o), and exactly 2 by each of half of the devices.
All inputs are finite; a program needn't handle non-finite values. No bound on the sum of `valid_mask` on one device may be relied on, other than what follows from the above.
Results may differ from a plain program's by a relative error of at most 0.012.
Values may be sent and summed in bfloat16 or wider, within the bound.
A program may use at most 128 MiB of HBM per device.

v0:
```python
import jax
import jax.numpy as jnp
from jax import lax
from jax.sharding import PartitionSpec as P

HD = 64
K = 8


epsilon = 1e-06
depth_step = 0.1
pose_step = 0.005


def norm_rows(values):
    average = jnp.mean(values, axis=-1, keepdims=True)
    centred = values - average
    variance = jnp.mean(centred * centred, axis=-1, keepdims=True)
    return (centred * lax.rsqrt(variance + epsilon)).astype(jnp.bfloat16)


def soft_weights(scores):
    top_score = jnp.max(scores, axis=-1, keepdims=True)
    expos = jnp.exp(scores - top_score)
    return (expos / jnp.sum(expos, axis=-1, keepdims=True)).astype(jnp.bfloat16)


def make_rays(token_index, rows_total):
    column = (token_index % 16).astype(jnp.float32)
    row_pos = (token_index // 16).astype(jnp.float32)
    return jnp.stack(
        [(column - 7.5) * 0.125, (row_pos - (rows_total - 1) * 0.5) * 0.125, jnp.ones_like(column)]
    )


def align_loss(depth_map, pose_own, pose_far, points, confidence, weight, ray_dirs, loss_scale):
    summed = 0.0
    for component in range(3):
        world_pts = pose_own[4 * component + 3][:, None] + depth_map * (
            pose_own[4 * component][:, None] * ray_dirs[0]
            + pose_own[4 * component + 1][:, None] * ray_dirs[1]
            + pose_own[4 * component + 2][:, None] * ray_dirs[2]
        )
        predicted = pose_far[4 * component + 3][:, :, None] + (
            pose_far[4 * component][:, :, None] * points[0]
            + pose_far[4 * component + 1][:, :, None] * points[1]
            + pose_far[4 * component + 2][:, :, None] * points[2]
        )
        residual = world_pts[:, None, :] - predicted
        summed = summed + jnp.sum(weight[:, None, :] * confidence * residual * residual)
    return summed * loss_scale


def shards(
    patches,
    encoder_proj,
    encoder_out,
    decoder_embed,
    decoder_proj,
    decoder_out,
    head_weight,
    partners,
    depths,
    camera_poses,
    valid_mask,
):
    images, tokens, model_width = patches.shape
    dec_width = decoder_embed.shape[1]
    enc_local = encoder_proj.shape[2]
    dec_local = decoder_proj.shape[2]
    head_scale = HD ** (-0.5)
    normed = norm_rows(patches.astype(jnp.float32))
    projected = jnp.dot(
        normed, encoder_proj.reshape(model_width, 3 * enc_local), preferred_element_type=jnp.float32
    )
    projected = projected.astype(jnp.bfloat16).reshape(images, tokens, 3, enc_local // HD, HD)
    scores = (
        jnp.einsum(
            "aqhd,athd->ahqt",
            projected[:, :, 0],
            projected[:, :, 1],
            preferred_element_type=jnp.float32,
        )
        * head_scale
    )
    mixed_rows = jnp.einsum(
        "ahqt,athd->aqhd",
        soft_weights(scores),
        projected[:, :, 2],
        preferred_element_type=jnp.float32,
    )
    mixed_rows = mixed_rows.astype(jnp.bfloat16).reshape(images, tokens, enc_local)
    partial_value = jnp.dot(mixed_rows, encoder_out, preferred_element_type=jnp.float32)
    encoded = patches.astype(jnp.float32) + lax.psum(partial_value, "mp")
    embedded = jnp.dot(
        norm_rows(encoded), decoder_embed, preferred_element_type=jnp.float32
    ).astype(jnp.bfloat16)
    dec_rows = jnp.dot(
        norm_rows(embedded.astype(jnp.float32)),
        decoder_proj.reshape(dec_width, 3 * dec_local),
        preferred_element_type=jnp.float32,
    )
    dec_rows = dec_rows.astype(jnp.bfloat16).reshape(images, tokens, 3, dec_local)
    query_rows = dec_rows[:, :, 0].reshape(images, tokens, dec_local // HD, HD)
    keyval_rows = dec_rows[:, :, 1:].reshape(images, tokens, 2 * dec_local)
    pose_rows = camera_poses.astype(jnp.bfloat16).T
    flat_partner = partners.reshape(-1)
    pair_count = flat_partner.shape[0]
    groups = lax.axis_size("img")
    slot_count = 2 * pair_count // groups
    owners = flat_partner // images
    local_index = flat_partner % images
    ordinal = jnp.arange(pair_count, dtype=jnp.int32)
    earlier = (owners[None, :] == owners[:, None]) & (ordinal[None, :] < ordinal[:, None])
    rank_index = jnp.sum(earlier.astype(jnp.int32), axis=1)
    slot_index = owners * slot_count + rank_index
    slot_table = slot_index[:, None] == jnp.arange(groups * slot_count, dtype=jnp.int32)[None, :]
    wanted = jnp.sum(jnp.where(slot_table, local_index[:, None], 0), axis=0).reshape(
        groups, slot_count
    )
    asked_for = lax.all_to_all(wanted, "img", split_axis=0, concat_axis=0, tiled=True)
    sent_rows = keyval_rows[asked_for]
    sent_pose = pose_rows[asked_for]
    got_rows, got_pose = (
        lax.all_to_all(sent_rows, "img", split_axis=0, concat_axis=0, tiled=True),
        lax.all_to_all(sent_pose, "img", split_axis=0, concat_axis=0, tiled=True),
    )
    far_rows = got_rows.reshape(groups * slot_count, tokens, 2 * dec_local)[slot_index]
    far_pose = got_pose.reshape(groups * slot_count, 12)[slot_index]
    far_split = far_rows.reshape(images, K, tokens, 2, dec_local // HD, HD)
    cross_scores = (
        jnp.einsum(
            "aqhd,akthd->akhqt",
            query_rows,
            far_split[:, :, :, 0],
            preferred_element_type=jnp.float32,
        )
        * head_scale
    )
    cross_rows = jnp.einsum(
        "akhqt,akthd->qakhd",
        soft_weights(cross_scores),
        far_split[:, :, :, 1],
        preferred_element_type=jnp.float32,
    )
    cross_rows = cross_rows.astype(jnp.bfloat16).reshape(tokens, pair_count, dec_local)
    token_share = tokens // lax.axis_size("mp")
    full_out = lax.all_gather(decoder_out, "mp", axis=0, tiled=True)
    mixed_out = jnp.dot(
        lax.all_to_all(cross_rows, "mp", split_axis=0, concat_axis=2, tiled=True),
        full_out,
        preferred_element_type=jnp.float32,
    )
    first_token = lax.axis_index("mp") * token_share
    own_rows = lax.dynamic_slice_in_dim(embedded, first_token, token_share, 1)
    own_rows = jnp.repeat(jnp.swapaxes(own_rows, 0, 1), K, axis=1)
    settled = mixed_out + own_rows.astype(jnp.float32)
    head_out = jnp.dot(norm_rows(settled), head_weight, preferred_element_type=jnp.float32)
    moved = jnp.transpose(head_out, (2, 1, 0))
    points = moved[:3]
    confidence = 1.0 + jnp.exp(moved[3])
    pointmap = jnp.concatenate([points, confidence[None]], axis=0)
    ray_dirs = make_rays(first_token + jnp.arange(token_share, dtype=jnp.int32), tokens // 16)
    weight = valid_mask.astype(jnp.float32)
    pose_far = far_pose.astype(jnp.float32).T.reshape(12, images, K)
    point_grid = points.reshape(3, images, K, token_share)
    conf_grid = confidence.reshape(images, K, token_share)

    def loss_fn(depth_map, pose_own, pose_other):
        return align_loss(
            depth_map, pose_own, pose_other, point_grid, conf_grid, weight, ray_dirs, 1.0 / tokens
        )

    loss_value, pullback = jax.vjp(loss_fn, depths, camera_poses, pose_far)
    grad_depth, grad_own, grad_far = pullback(jnp.ones_like(loss_value))
    grad_far_flat = grad_far.reshape(12, pair_count)
    total_images = groups * images
    base_image = lax.axis_index("img") * images
    image_ids = jnp.arange(total_images, dtype=jnp.int32)
    partner_hits = (flat_partner[:, None] == image_ids[None, :]).astype(jnp.float32)
    own_hits = (
        (base_image + jnp.arange(images, dtype=jnp.int32))[:, None] == image_ids[None, :]
    ).astype(jnp.float32)
    dense_grad = jnp.dot(grad_far_flat, partner_hits, precision=lax.Precision.HIGHEST) + jnp.dot(
        grad_own, own_hits, precision=lax.Precision.HIGHEST
    )
    summed = lax.psum(dense_grad, ("img", "mp"))
    grad_pose = lax.dynamic_slice_in_dim(summed, base_image, images, 1)
    new_depths = depths - depth_step * grad_depth
    new_poses = camera_poses - pose_step * grad_pose
    return (pointmap, new_depths, new_poses)


def solution(mesh):
    placed = (
        P("img", None, None),
        P(None, None, "mp"),
        P("mp", None),
        P(),
        P(None, None, "mp"),
        P("mp", None),
        P(),
        P("img", None),
        P("img", "mp"),
        P(None, "img"),
        P("img", "mp"),
    )
    return jax.shard_map(
        shards,
        mesh=mesh,
        in_specs=placed,
        out_specs=(P(None, "img", "mp"), P("img", "mp"), P(None, "img")),
        check_vma=False,
    )
```

profile of v0, /device:TPU:1, one launch (start us, length us, event | category | flops | bytes accessed | tf_op | source)
XLA Modules:
  0.0 553.6 jit_solution(15001532129823745541)
XLA Ops:
  7.2 2.8 copy.143
  10.3 0.6 fusion.14
  10.9 0.5 copy-done.5
  11.4 2.5 fusion.34
  13.9 2.5 copy.145
  16.4 3.1 fusion.98
  19.5 2.0 convolution_convert_fusion.1
  21.5 2.3 fusion.47
  24.4 22.2 %all_to_all.40 = s32[64,1,2]{2,1,0:T(1,128)S(1)} all-to-all(s32[64,1,2]{2,1,0:T(1,128)S(1)} %bitcast.243), channel_id=1, replica_groups=mesh['img'=64,'mp'=4] {'img'}, dimensions={0} | all-to-all | bytes 1024 | tf_op jit(solution)/shard_map/all_to_all | solution.py:121
  46.9 61.7 %all-reduce.26.cloned.1.call-done = f32[8,96,1024]{2,1,0:T(8,128)} async-done(((f32[8,96,1024]{2,1,0:T(8,128)}), f32[8,96,1024]{2,1,0:T(8,128)}) %all-reduce.26.cloned.1.call-update) | async-done | bytes 3145744 | tf_op jit(solution)/shard_map/psum | solution.py:94
  108.6 2.4 fusion.41
  111.1 0.4 copy-done.3
  111.4 0.7 multiply_reduce_fusion.1
  112.2 1.6 convert_reduce_fusion.1
  113.8 0.5 fusion.19
  114.3 0.5 copy-done.4
  114.9 1.1 convolution_convert_fusion
  116.0 0.7 copy.151
  116.8 8.3 %gather_fusion = bf16[128,96,384]{1,2,0:T(8,128)(2,1)} fusion(bf16[8,96,384]{1,2,0:T(8,128)(2,1)S(1)} %bitcast.225, s32[1024]{0:T(1024)S(1)} %pad_clamp_fusion.1), kind=kCustom, calls=%fused_computation | custom fusion | bytes 18874880 | tf_op jit(solution)/shard_map/gather | solution.py:122
  125.1 14.8 %copy.155 = bf16[128,96,384]{2,1,0:T(8,128)(2,1)} copy(bf16[128,96,384]{1,2,0:T(8,128)(2,1)} %gather_fusion) | data formatting | bytes 18874368 | tf_op jit(solution)/shard_map/gather | solution.py:122
  139.9 11.1 %all-to-all-start.1 = ((bf16[64,2,96,384]{3,2,1,0:T(8,128)(2,1)}), bf16[64,2,96,384]{3,2,1,0:T(8,128)(2,1)}, u32[]{:S(2)}, u32[]{:S(2)}) async-start(bf16[64,2,96,384]{3,2,1,0:T(8,128)(2,1)} %bitcast.226), calls=%async_computation.1 | async-start | bytes 18874368 | tf_op jit(solution)/shard_map/all_to_all | solution.py:125
  151.0 0.7 all-gather.2.cloned.1.call-update
  151.8 0.4 slice_reduce_fusion.23
  152.2 1.3 gather_fusion.2
  153.6 205.7 %all-to-all-done.1 = bf16[64,2,96,384]{3,2,1,0:T(8,128)(2,1)} async-done(((bf16[64,2,96,384]{3,2,1,0:T(8,128)(2,1)}), bf16[64,2,96,384]{3,2,1,0:T(8,128)(2,1)}, u32[]{:S(2)}, u32[]{:S(2)}) %all-to-all-start.1) | async-done | bytes 9437216 | tf_op jit(solution)/shard_map/all_to_all | solution.py:125
  359.2 6.0 %all-to-all-start.3 = ((bf16[64,2,12]{2,1,0:T(2,128)(2,1)}), bf16[64,2,12]{2,1,0:T(2,128)(2,1)S(1)}, u32[]{:S(2)}, u32[]{:S(2)}) async-start(bf16[64,2,12]{2,1,0:T(2,128)(2,1)} %bitcast.38), calls=%async_computation.3 | async-start | bytes 65536 | tf_op jit(solution)/shard_map/all_to_all | solution.py:126
  365.2 7.0 %gather_fusion.1 = bf16[64,96,384]{2,1,0:T(8,128)(2,1)} fusion(bf16[128,96,384]{2,1,0:T(8,128)(2,1)} %bitcast.17, s32[1024]{0:T(1024)S(1)} %pad_clamp_fusion), kind=kCustom, calls=%fused_computation.1 | custom fusion | bytes 9437440 | tf_op jit(solution)/shard_map/gather | solution.py:128
  372.2 8.0 %copy.156 = bf16[64,96,384]{1,2,0:T(8,128)(2,1)} copy(bf16[64,96,384]{2,1,0:T(8,128)(2,1)} %gather_fusion.1) | data formatting | bytes 9437184 | tf_op jit(solution)/shard_map/gather | solution.py:128
  380.2 3.5 fusion.16
  383.7 4.9 fusion.99
  388.7 6.8 %fusion.22 = bf16[8,8,3,64,96]{4,3,2,1,0:T(8,128)(2,1)} fusion(bf16[8,8,96,2,3,64]{2,5,4,3,1,0:T(8,128)(2,1)S(1)} %bitcast.230, f32[8,8,3,96,96]{3,4,1,2,0:T(8,128)} %get-tuple-element.94, f32[8,8,3,96]{3,1,2,0:T(8,128)S(1)} %get-tuple-element.93), kind=kOutput, calls=%fused_computation.39 | convolution fusion | flops 231211008 | bytes 12681216 | tf_op jit(solution)/shard_map/akhqt,akthd->qakhd/dot_general | solution.py:140
  395.5 6.6 %copy.160 = bf16[96,64,192]{2,1,0:T(8,128)(2,1)} copy(bf16[96,64,192]{0,2,1:T(8,128)(2,1)} %bitcast.233) | data formatting | bytes 4718592 | tf_op jit(solution)/shard_map/reshape | solution.py:146
  402.1 5.0 all-to-all-start.2
  407.6 0.7 gather_fusion.3
  408.3 0.4 slice_reduce_fusion.11
  409.6 1.1 convert_bitcast_fusion
  410.9 33.3 %all-to-all-done.2 = bf16[96,64,192]{2,1,0:T(8,128)(2,1)} async-done(((bf16[96,64,192]{2,1,0:T(8,128)(2,1)}), bf16[96,64,192]{2,1,0:T(8,128)(2,1)}, u32[]{:S(2)}, u32[]{:S(2)}) %all-to-all-start.2) | async-done | bytes 2359328 | tf_op jit(solution)/shard_map/all_to_all | solution.py:150
  444.2 6.5 %copy.161 = bf16[24,64,4,192]{3,2,1,0:T(4,128)(2,1)} copy(bf16[24,64,4,192]{3,1,0,2:T(8,128)(2,1)} %bitcast.30) | data formatting | bytes 4718592 | tf_op jit(solution)/shard_map/all_to_all | solution.py:150
  450.7 6.4 %all_to_all.34 = bf16[24,64,768]{2,1,0:T(8,128)(2,1)} reshape(bf16[24,64,4,192]{3,2,1,0:T(4,128)(2,1)} %copy.161) | data formatting | bytes 4718592 | tf_op jit(solution)/shard_map/all_to_all | solution.py:150
  457.1 4.2 fusion.11
  461.4 0.9 multiply_reduce_fusion
  462.3 1.5 fusion.21
  464.3 0.6 pad_maximum_fusion
  466.3 0.5 fusion.49
  467.4 0.9 multiply_reduce_fusion.17
  468.3 0.5 convolution_add_fusion
  468.8 77.4 %psum.15 = f32[12,512]{0,1:T(8,128)S(1)} all-reduce(f32[12,512]{0,1:T(8,128)S(1)} %convolution_add_fusion), channel_id=1, replica_groups=mesh['img'=64,'mp'=4] {'img','mp'}, use_global_device_ids=true, to_apply=%region_42.43 | all-reduce | flops 6144 | bytes 49152 | tf_op jit(solution)/shard_map/psum | solution.py:187
  546.1 0.6 multiply_subtract_fusion
  (118 shorter events, 5.4 us)
Async XLA Ops:
  7.2 105.0 %copy-start = (bf16[1024,768]{1,0:T(8,128)(2,1)S(1)}, bf16[1024,768]{1,0:T(8,128)(2,1)}, u32[]{:S(2)}) copy-start(bf16[1024,768]{1,0:T(8,128)(2,1)} %param.14) | copy-start | bytes 4718596
  7.2 2.8 copy-start.2
  7.2 101.4 %all-reduce.26.cloned.1.call-start = ((), (), s32[]{:S(2)}) async-start(), calls=%async_computation.4 | async-start | bytes 6291456 | tf_op jit(solution)/shard_map/psum | solution.py:94
  10.0 1.4 copy-start.5
  19.5 2.0 copy-start.7
  21.5 2.3 copy-start.8
  108.6 2.8 copy-start.3
  112.1 2.7 copy-start.12
  113.8 1.1 copy-start.4
  139.9 12.0 %copy-start.6 = (f32[12,8]{0,1:T(8,128)S(1)}, f32[12,8]{0,1:T(8,128)}, u32[]{:S(2)}) copy-start(f32[12,8]{0,1:T(8,128)} %param.20) | copy-start | bytes 1156
  139.9 219.4 %all-to-all-start.1 = ((bf16[64,2,96,384]{3,2,1,0:T(8,128)(2,1)}), bf16[64,2,96,384]{3,2,1,0:T(8,128)(2,1)}, u32[]{:S(2)}, u32[]{:S(2)}) async-start(bf16[64,2,96,384]{3,2,1,0:T(8,128)(2,1)} %bitcast.226), calls=%async_computation.1 | async-start | bytes 18874368 | tf_op jit(solution)/shard_map/all_to_all | solution.py:125
  151.0 306.1 %all-gather.2.cloned.1.call-start = ((), (), s32[]{:S(2)}) async-start(), calls=%async_computation.5 | async-start | bytes 1474560 | tf_op jit(solution)/shard_map/all_gather | solution.py:148
  359.2 42.9 %all-to-all-start.3 = ((bf16[64,2,12]{2,1,0:T(2,128)(2,1)}), bf16[64,2,12]{2,1,0:T(2,128)(2,1)S(1)}, u32[]{:S(2)}, u32[]{:S(2)}) async-start(bf16[64,2,12]{2,1,0:T(2,128)(2,1)} %bitcast.38), calls=%async_computation.3 | async-start | bytes 65536 | tf_op jit(solution)/shard_map/all_to_all | solution.py:126
  380.2 8.5 %slice-start = ((s8[6291456]{0:T(1024)(128)(4,1)}), s8[4194304]{0:T(1024)(128)(4,1)S(1)}, s32[]{:S(2)}) async-start(s8[6291456]{0:T(1024)(128)(4,1)} %bitcast.228), calls=%async_computation.6 | async-start | bytes 8388608
  383.7 5.0 slice-start.1
  402.1 5.0 copy-start.9
  402.1 5.2 copy-start.11
  402.1 42.1 %all-to-all-start.2 = ((bf16[96,64,192]{2,1,0:T(8,128)(2,1)}), bf16[96,64,192]{2,1,0:T(8,128)(2,1)}, u32[]{:S(2)}, u32[]{:S(2)}) async-start(bf16[96,64,192]{2,1,0:T(8,128)(2,1)} %copy.160), calls=%async_computation.2 | async-start | bytes 6291456 | tf_op jit(solution)/shard_map/all_to_all | solution.py:150
  461.3 1.0 copy-start.10
  462.3 84.4 %copy-start.1 = (bf16[1024,768]{1,0:T(8,128)(2,1)S(1)}, bf16[1024,768]{1,0:T(8,128)(2,1)}, u32[]{:S(2)}) copy-start(bf16[1024,768]{1,0:T(8,128)(2,1)} %param.14) | copy-start | bytes 4718596
Sparse Core Ops, SparseCore 0:
  23.9 84.6 all-reduce.25
  153.6 25.4 all-gather.1
where the time goes:
time: 555 us; the launch traced here: 554 us
  waiting for transfers between devices  301 us (54%)
  blocking collectives  99.6 us (18%)
  local copies, waits for them, and re-layouts  71.5 us (13%)
  matrix products  29.6 us (5%)
  starting transfers between devices  22.2 us (4%)
  other arithmetic  14.8 us (3%)
  between operations  14.5 us (3%)
    all_to_all x1, waiting for transfers between devices, shards(): lax.all_to_all(sent_rows, 'img', split_axis=0, concat_axis=0, tiled=True)  206 us
    psum x1, blocking collectives, shards(): summed = lax.psum(dense_grad, ('img', 'mp'))  77.4 us
    psum x1, waiting for transfers between devices, shards(): encoded = patches.astype(jnp.float32) + lax.psum(partial_value, 'mp')  61.7 us
    all_to_all x1, waiting for transfers between devices, shards(): lax.all_to_all(cross_rows, 'mp', split_axis=0, concat_axis=2, tiled=True)  33.3 us
    gather x2, local copies, waits for them, and re-layouts, shards(): sent_rows = keyval_rows[asked_for]  23.1 us
    all_to_all x1, blocking collectives, shards(): lax.all_to_all(wanted, 'img', split_axis=0, concat_axis=0, tiled=True)  22.2 us
    gather x2, local copies, waits for them, and re-layouts, shards(): got_rows.reshape(groups * slot_count, tokens, 2 * dec_local)[slot_index]  15 us
    all_to_all x2, local copies, waits for them, and re-layouts, shards(): lax.all_to_all(cross_rows, 'mp', split_axis=0, concat_axis=2, tiled=True)  12.9 us
  transfers between devices with their start and end apart: 5, of which 3 were waited for; matrix products, arithmetic and copies ran while one was open for 9% of the time, Pallas kernels for 0%

commit v1 on v0

--- a/solution.py
+++ b/solution.py
@@ -69,6 +69,16 @@
     enc_local = encoder_proj.shape[2]
     dec_local = decoder_proj.shape[2]
     head_scale = HD ** (-0.5)
+    split = lax.axis_size("mp")
+    place = lax.axis_index("mp")
+    own_count = images // split
+    flat_partner = partners.reshape(-1)
+    pair_count = flat_partner.shape[0]
+    out_full = lax.all_gather(encoder_out, "mp", axis=0, tiled=True)
+    proj_full = lax.all_gather(jnp.transpose(decoder_proj, (1, 2, 0)), "mp", axis=1, tiled=True)
+    dec_out_full = lax.all_gather(decoder_out, "mp", axis=0, tiled=True)
+    all_poses = lax.all_gather(camera_poses.astype(jnp.bfloat16), "img", axis=1, tiled=True)
+
     normed = norm_rows(patches.astype(jnp.float32))
     projected = jnp.dot(
         normed, encoder_proj.reshape(model_width, 3 * enc_local), preferred_element_type=jnp.float32
@@ -90,79 +100,63 @@
         preferred_element_type=jnp.float32,
     )
     mixed_rows = mixed_rows.astype(jnp.bfloat16).reshape(images, tokens, enc_local)
-    partial_value = jnp.dot(mixed_rows, encoder_out, preferred_element_type=jnp.float32)
-    encoded = patches.astype(jnp.float32) + lax.psum(partial_value, "mp")
+    mixed_own = lax.all_to_all(mixed_rows, "mp", split_axis=0, concat_axis=2, tiled=True)
+    patch_own = lax.dynamic_slice_in_dim(patches, place * own_count, own_count, 0)
+    encoded = patch_own.astype(jnp.float32) + jnp.dot(
+        mixed_own, out_full, preferred_element_type=jnp.float32
+    )
     embedded = jnp.dot(
         norm_rows(encoded), decoder_embed, preferred_element_type=jnp.float32
     ).astype(jnp.bfloat16)
-    dec_rows = jnp.dot(
-        norm_rows(embedded.astype(jnp.float32)),
-        decoder_proj.reshape(dec_width, 3 * dec_local),
+    rows = norm_rows(embedded.astype(jnp.float32))
+    quarter = lax.all_to_all(rows, "mp", split_axis=1, concat_axis=0, tiled=True)
+    everything = lax.all_gather(quarter, "img", axis=0, tiled=True)
+    picked = everything[flat_partner]
+    far_rows = lax.all_to_all(picked, "mp", split_axis=0, concat_axis=1, tiled=True)
+    own_pairs = pair_count // split
+
+    def project(values, which):
+        return lax.dot_general(
+            values,
+            proj_full[which],
+            (((2,), (1,)), ((), ())),
+            preferred_element_type=jnp.float32,
+        ).astype(jnp.bfloat16)
+
+    heads = dec_width // HD
+    queries = project(rows, 0).reshape(own_count, tokens, heads, HD)
+    far_keys = project(far_rows, 1).reshape(own_count, K, tokens, heads, HD)
+    far_values = project(far_rows, 2).reshape(own_count, K, tokens, heads, HD)
+    cross_scores = (
+        jnp.einsum("aqhd,akthd->akhqt", queries, far_keys, preferred_element_type=jnp.float32)
+        * head_scale
+    )
+    cross_rows = jnp.einsum(
+        "akhqt,akthd->akqhd",
+        soft_weights(cross_scores),
+        far_values,
         preferred_element_type=jnp.float32,
     )
-    dec_rows = dec_rows.astype(jnp.bfloat16).reshape(images, tokens, 3, dec_local)
-    query_rows = dec_rows[:, :, 0].reshape(images, tokens, dec_local // HD, HD)
-    keyval_rows = dec_rows[:, :, 1:].reshape(images, tokens, 2 * dec_local)
-    pose_rows = camera_poses.astype(jnp.bfloat16).T
-    flat_partner = partners.reshape(-1)
-    pair_count = flat_partner.shape[0]
-    groups = lax.axis_size("img")
-    slot_count = 2 * pair_count // groups
-    owners = flat_partner // images
-    local_index = flat_partner % images
-    ordinal = jnp.arange(pair_count, dtype=jnp.int32)
-    earlier = (owners[None, :] == owners[:, None]) & (ordinal[None, :] < ordinal[:, None])
-    rank_index = jnp.sum(earlier.astype(jnp.int32), axis=1)
-    slot_index = owners * slot_count + rank_index
-    slot_table = slot_index[:, None] == jnp.arange(groups * slot_count, dtype=jnp.int32)[None, :]
-    wanted = jnp.sum(jnp.where(slot_table, local_index[:, None], 0), axis=0).reshape(
-        groups, slot_count
-    )
-    asked_for = lax.all_to_all(wanted, "img", split_axis=0, concat_axis=0, tiled=True)
-    sent_rows = keyval_rows[asked_for]
-    sent_pose = pose_rows[asked_for]
-    got_rows, got_pose = (
-        lax.all_to_all(sent_rows, "img", split_axis=0, concat_axis=0, tiled=True),
-        lax.all_to_all(sent_pose, "img", split_axis=0, concat_axis=0, tiled=True),
-    )
-    far_rows = got_rows.reshape(groups * slot_count, tokens, 2 * dec_local)[slot_index]
-    far_pose = got_pose.reshape(groups * slot_count, 12)[slot_index]
-    far_split = far_rows.reshape(images, K, tokens, 2, dec_local // HD, HD)
-    cross_scores = (
-        jnp.einsum(
-            "aqhd,akthd->akhqt",
-            query_rows,
-            far_split[:, :, :, 0],
-            preferred_element_type=jnp.float32,
-        )
-        * head_scale
-    )
-    cross_rows = jnp.einsum(
-        "akhqt,akthd->qakhd",
-        soft_weights(cross_scores),
-        far_split[:, :, :, 1],
+    cross_rows = cross_rows.astype(jnp.bfloat16).reshape(own_count, K, tokens, dec_width)
+    settled = (
+        jnp.dot(cross_rows, dec_out_full, preferred_element_type=jnp.float32)
+        + embedded.astype(jnp.float32)[:, None]
+    )
+    head_own = lax.dot_general(
+        head_weight,
+        norm_rows(settled).reshape(own_pairs, tokens, dec_width),
+        (((0,), (2,)), ((), ())),
         preferred_element_type=jnp.float32,
     )
-    cross_rows = cross_rows.astype(jnp.bfloat16).reshape(tokens, pair_count, dec_local)
-    token_share = tokens // lax.axis_size("mp")
-    full_out = lax.all_gather(decoder_out, "mp", axis=0, tiled=True)
-    mixed_out = jnp.dot(
-        lax.all_to_all(cross_rows, "mp", split_axis=0, concat_axis=2, tiled=True),
-        full_out,
-        preferred_element_type=jnp.float32,
-    )
-    first_token = lax.axis_index("mp") * token_share
-    own_rows = lax.dynamic_slice_in_dim(embedded, first_token, token_share, 1)
-    own_rows = jnp.repeat(jnp.swapaxes(own_rows, 0, 1), K, axis=1)
-    settled = mixed_out + own_rows.astype(jnp.float32)
-    head_out = jnp.dot(norm_rows(settled), head_weight, preferred_element_type=jnp.float32)
-    moved = jnp.transpose(head_out, (2, 1, 0))
+    moved = lax.all_to_all(head_own, "mp", split_axis=2, concat_axis=1, tiled=True)
+    token_share = tokens // split
+    first_token = place * token_share
     points = moved[:3]
     confidence = 1.0 + jnp.exp(moved[3])
     pointmap = jnp.concatenate([points, confidence[None]], axis=0)
     ray_dirs = make_rays(first_token + jnp.arange(token_share, dtype=jnp.int32), tokens // 16)
     weight = valid_mask.astype(jnp.float32)
-    pose_far = far_pose.astype(jnp.float32).T.reshape(12, images, K)
+    pose_far = all_poses[:, flat_partner].astype(jnp.float32).reshape(12, images, K)
     point_grid = points.reshape(3, images, K, token_share)
     conf_grid = confidence.reshape(images, K, token_share)
 
@@ -174,6 +168,7 @@
     loss_value, pullback = jax.vjp(loss_fn, depths, camera_poses, pose_far)
     grad_depth, grad_own, grad_far = pullback(jnp.ones_like(loss_value))
     grad_far_flat = grad_far.reshape(12, pair_count)
+    groups = lax.axis_size("img")
     total_images = groups * images
     base_image = lax.axis_index("img") * images
     image_ids = jnp.arange(total_images, dtype=jnp.int32)

time: 555 us -> 388 us (0.70)
  waiting for transfers between devices: 301 us -> 134 us
  blocking collectives: 99.6 us -> 133 us
  local copies, waits for them, and re-layouts: 71.5 us -> 40.8 us
  matrix products: 29.6 us -> 39.4 us
  starting transfers between devices: 22.2 us -> 13.1 us
    all_to_all x3, waiting for transfers between devices: 239 us -> 13 us  [the longest x1 12 us: shards(): lax.all_to_all(mixed_rows, 'mp', split_axis=0, concat_axis=2, tiled=True)]
    all_gather x1 -> x4, waiting for transfers between devices: 0.01 us -> 119 us  [the longest x1 106 us: shards(): everything = lax.all_gather(quarter, 'img', axis=0, tiled=True)]
    psum x1 -> x0, waiting for transfers between devices: 61.7 us -> none  [shards(): encoded = patches.astype(jnp.float32) + lax.psum(partial_value, 'mp')]
    all_gather x0 -> x1, blocking collectives: none -> 47.7 us  [shards(): lax.all_gather(camera_poses.astype(jnp.bfloat16), 'img', axis=1, tiled=True)]
    gather x6 -> x2, local copies, waits for them, and re-layouts: 40 us -> 9.08 us  [the longest x1 8.45 us: shards(): picked = everything[flat_partner]]
    all_to_all x1, blocking collectives: 22.2 us -> 8.35 us  [shards(): lax.all_to_all(rows, 'mp', split_axis=1, concat_axis=0, tiled=True)]
    dot_general x6 -> x8, matrix products: 19.5 us -> 29.6 us  [the longest x3 12 us: project(): lax.dot_general(values, proj_full[which], (((2,), (1,)), ((), ())), prefe...]
    all_to_all x3, starting transfers between devices: 22.1 us -> 13 us  [the longest x1 4.84 us: shards(): lax.all_to_all(mixed_rows, 'mp', split_axis=0, concat_axis=2, tiled=True)]
  transfers between devices with their start and end apart: 5 -> 7, of which waited for: 3 -> 5; matrix products, arithmetic and copies ran while one was open for 9% -> 18% of each run, Pallas kernels for 0% -> 0%
where the time goes in v1:
time: 388 us; the launch traced here: 387 us
  waiting for transfers between devices  134 us (35%)
  blocking collectives  133 us (34%)
  local copies, waits for them, and re-layouts  40.8 us (11%)
  matrix products  39.4 us (10%)
  between operations  14.3 us (4%)
  starting transfers between devices  13.1 us (3%)
  other arithmetic  12.3 us (3%)
    all_gather x1, waiting for transfers between devices, shards(): everything = lax.all_gather(quarter, 'img', axis=0, tiled=True)  106 us
    psum x1, blocking collectives, shards(): summed = lax.psum(dense_grad, ('img', 'mp'))  77.3 us
    all_gather x1, blocking collectives, shards(): lax.all_gather(camera_poses.astype(jnp.bfloat16), 'img', axis=1, tiled=True)  47.7 us
    all_to_all x1, waiting for transfers between devices, shards(): lax.all_to_all(mixed_rows, 'mp', split_axis=0, concat_axis=2, tiled=True)  12 us
    dot_general x3, matrix products, project(): lax.dot_general(values, proj_full[which], (((2,), (1,)), ((), ())), prefe...  12 us
    convert_element_type x3, local copies, waits for them, and re-layouts, project(): return lax.dot_general(values, proj_full[which], (((2,), (1,)), ((), ()))...  9.25 us
    gather x1, local copies, waits for them, and re-layouts, shards(): picked = everything[flat_partner]  8.45 us
    all_to_all x1, blocking collectives, shards(): lax.all_to_all(rows, 'mp', split_axis=1, concat_axis=0, tiled=True)  8.35 us
  transfers between devices with their start and end apart: 7, of which 5 were waited for; matrix products, arithmetic and copies ran while one was open for 18% of the time, Pallas kernels for 0%

profile of v1, /device:TPU:1, one launch (start us, length us, event | category | flops | bytes accessed | tf_op | source)
XLA Modules:
  0.0 387.1 jit_solution(5494464470756418696)
XLA Ops:
  7.2 0.7 all-gather.5.cloned.1.call-update
  7.9 2.6 copy.181
  10.8 0.6 fusion.12
  11.9 2.5 fusion.28
  14.4 2.5 copy.183
  16.9 3.1 fusion.81
  20.0 2.7 convolution_convert_fusion.2
  22.8 2.0 copy.188
  24.8 4.8 %all-to-all-start = ((bf16[8,96,256]{2,1,0:T(8,128)(2,1)}), bf16[8,96,256]{2,1,0:T(8,128)(2,1)S(1)}, u32[]{:S(2)}, u32[]{:S(2)}) async-start(bf16[8,96,256]{2,1,0:T(8,128)(2,1)} %copy.188), calls=%async_computation | async-start | bytes 786432 | tf_op jit(solution)/shard_map/all_to_all | solution.py:103
  29.6 12.0 %all-to-all-done = bf16[8,96,256]{2,1,0:T(8,128)(2,1)S(1)} async-done(((bf16[8,96,256]{2,1,0:T(8,128)(2,1)}), bf16[8,96,256]{2,1,0:T(8,128)(2,1)S(1)}, u32[]{:S(2)}, u32[]{:S(2)}) %all-to-all-start) | async-done | bytes 393248 | tf_op jit(solution)/shard_map/all_to_all | solution.py:103
  41.7 1.1 copy.280
  42.7 1.3 all_to_all.53
  44.0 7.2 %all-gather.5.cloned.1.call-done = bf16[1024,1024]{1,0:T(8,128)(2,1)} async-done(((bf16[256,1024]{1,0:T(8,128)(2,1)}), bf16[1024,1024]{1,0:T(8,128)(2,1)}) %all-gather.5.cloned.1.call-update) | async-done | bytes 2097168 | tf_op jit(solution)/shard_map/all_gather | solution.py:77
  51.2 2.3 fusion.82
  53.8 0.6 fusion.83
  55.1 8.3 %all_to_all.69 = bf16[2,96,768]{2,0,1:T(2,128)(2,1)S(1)} all-to-all(bf16[2,96,768]{2,0,1:T(2,128)(2,1)S(1)} %copy.190), channel_id=1, replica_groups=mesh['img'=64,'mp'=4] {'mp'}, dimensions={1} | all-to-all | bytes 589824 | tf_op jit(solution)/shard_map/all_to_all | solution.py:112
  63.5 0.7 copy.192
  64.3 0.7 all-gather.9.cloned.1.call-update
  65.1 105.7 %all-gather.7.cloned.1.call-done = bf16[512,24,768]{2,1,0:T(8,128)(2,1)} async-done(((bf16[8,24,768]{2,1,0:T(8,128)(2,1)}), bf16[512,24,768]{2,1,0:T(8,128)(2,1)}) %all-gather.7.cloned.1.call-update) | async-done | bytes 18874384 | tf_op jit(solution)/shard_map/all_gather | solution.py:113
  170.8 8.4 %gather_fusion = bf16[64,24,768]{2,1,0:T(8,128)(2,1)} fusion(bf16[512,24,768]{2,1,0:T(8,128)(2,1)} %all-gather.7.cloned.1.call-done, s32[1024]{0:T(1024)S(1)} %pad_clamp_fusion), kind=kCustom, calls=%fused_computation | custom fusion | bytes 4718848 | tf_op jit(solution)/shard_map/gather | solution.py:114
  179.2 4.7 %all-to-all-start.2 = ((bf16[64,24,768]{2,1,0:T(8,128)(2,1)}), bf16[64,24,768]{2,1,0:T(8,128)(2,1)}, u32[]{:S(2)}, u32[]{:S(2)}) async-start(bf16[64,24,768]{2,1,0:T(8,128)(2,1)} %gather_fusion), calls=%async_computation.2 | async-start | bytes 4718592 | tf_op jit(solution)/shard_map/all_to_all | solution.py:115
  184.0 0.5 all-gather.11.cloned.1.call-update
  184.5 47.7 %all_gather.19 = bf16[12,512]{0,1:T(8,128)(2,1)S(1)} all-gather(bf16[12,8]{0,1:T(8,128)(2,1)S(1)} %convert_element_type.101), channel_id=1, replica_groups=mesh['img'=64,'mp'=4] {'img'}, dimensions={1}, use_global_device_ids=true | all-gather | bytes 12480 | tf_op jit(solution)/shard_map/all_gather | solution.py:80
  232.3 0.6 gather_fusion.1
  233.8 5.9 %all-gather.9.cloned.1.call-done = bf16[3,768,768]{2,1,0:T(8,128)(2,1)} async-done(((bf16[3,192,768]{2,1,0:T(8,128)(2,1)}), bf16[3,768,768]{2,1,0:T(8,128)(2,1)}) %all-gather.9.cloned.1.call-update) | async-done | bytes 3538960 | tf_op jit(solution)/shard_map/all_gather | solution.py:78
  239.8 1.8 convolution_convert_fusion.3
  241.8 1.9 copy.193
  243.8 1.4 copy-done.4
  245.2 4.7 %convolution_convert_fusion.1 = bf16[16,96,768]{2,1,0:T(8,128)(2,1)} fusion(bf16[16,96,768]{2,1,0:T(8,128)(2,1)S(1)} %bitcast.153, bf16[3,768,768]{2,1,0:T(8,128)(2,1)} %all-gather.9.cloned.1.call-done), kind=kOutput, calls=%fused_computation.28 | convolution fusion | flops 1813118976 | bytes 5898240 | tf_op jit(solution)/shard_map/dot_general | solution.py:119
  249.9 4.5 %copy.194 = bf16[16,96,768]{1,2,0:T(8,128)(2,1)} copy(bf16[16,96,768]{2,1,0:T(8,128)(2,1)} %convolution_convert_fusion.1) | data formatting | bytes 4718592 | tf_op jit(solution)/shard_map/convert_element_type | solution.py:124
  254.4 5.4 %convolution_convert_fusion = bf16[16,96,768]{2,1,0:T(8,128)(2,1)} fusion(bf16[16,96,768]{2,1,0:T(8,128)(2,1)} %bitcast.154, bf16[3,768,768]{2,1,0:T(8,128)(2,1)} %all-gather.9.cloned.1.call-done), kind=kOutput, calls=%fused_computation.27 | convolution fusion | flops 1813118976 | bytes 5898240 | tf_op jit(solution)/shard_map/dot_general | solution.py:119
  259.8 4.5 %copy.195 = bf16[16,96,768]{1,2,0:T(8,128)(2,1)} copy(bf16[16,96,768]{2,1,0:T(8,128)(2,1)} %convolution_convert_fusion) | data formatting | bytes 4718592 | tf_op jit(solution)/shard_map/convert_element_type | solution.py:124
  264.4 3.4 fusion.14
  267.7 4.9 %fusion.84 = (f32[2,8,12,96]{3,1,2,0:T(8,128)S(1)}, f32[2,8,12,96,96]{3,4,1,2,0:T(8,128)}) fusion(f32[2,12,8,96,96]{4,3,2,1,0:T(8,128)S(1)} %fusion.14), kind=kOutput, calls=%fused_computation.184 | output fusion | flops 7077983 | bytes 14229504 | tf_op jit(solution)/shard_map/sub | solution.py:24
  272.7 6.8 %fusion.16 = bf16[2,8,12,64,96]{4,3,2,1,0:T(8,128)(2,1)} fusion(bf16[2,8,96,12,64]{2,4,3,1,0:T(8,128)(2,1)S(1)} %bitcast.151, f32[2,8,12,96,96]{3,4,1,2,0:T(8,128)} %get-tuple-element.82, f32[2,8,12,96]{3,1,2,0:T(8,128)S(1)} %get-tuple-element.81), kind=kOutput, calls=%fused_computation.24 | convolution fusion | flops 231211008 | bytes 11870208 | tf_op jit(solution)/shard_map/akhqt,akthd->akqhd/dot_general | solution.py:134
  279.5 4.4 %add_reduce_fusion = (f32[2,8,96]{2,1,0:T(8,128)S(1)}, f32[2,8,96,768]{3,2,1,0:T(8,128)S(1)}) fusion(f32[2,96,768]{2,1,0:T(8,128)S(1)} %get-tuple-element.80, bf16[2,8,96,768]{2,3,1,0:T(8,128)(2,1)} %bitcast.152, bf16[768,768]{1,0:T(8,128)(2,1)} %all-gather.11.cloned.1.call-done), kind=kOutput, calls=%fused_computation.15 | convolution fusion | flops 1814297088 | bytes 8853504 | tf_op jit(solution)/shard_map/dot_general | solution.py:142
  283.9 0.8 multiply_reduce_fusion
  284.8 0.7 multiply_convert_fusion
  285.5 0.8 convolution_bitcast_fusion
  286.5 0.8 reshape.763
  287.3 3.5 all-to-all-start.3
  293.8 0.9 all-to-all-done.3
  294.7 0.5 broadcast.664
  295.3 0.7 reduce.81
  300.6 0.9 multiply_reduce_fusion.18
  302.0 77.3 %psum.7 = f32[12,512]{0,1:T(8,128)S(1)} all-reduce(f32[12,512]{0,1:T(8,128)S(1)} %convolution_add_fusion), channel_id=1, replica_groups=mesh['img'=64,'mp'=4] {'img','mp'}, use_global_device_ids=true, to_apply=%region_39.40 | all-reduce | flops 6144 | bytes 49152 | tf_op jit(solution)/shard_map/psum | solution.py:182
  379.3 0.6 pad_maximum_fusion
  379.9 0.6 multiply_subtract_fusion
  (147 shorter events, 11.3 us)
Async XLA Ops:
  7.2 46.6 %copy-start = (bf16[1024,768]{1,0:T(8,128)(2,1)S(1)}, bf16[1024,768]{1,0:T(8,128)(2,1)}, u32[]{:S(2)}) copy-start(bf16[1024,768]{1,0:T(8,128)(2,1)} %param.14) | copy-start | bytes 4718596
  7.2 3.3 copy-start.2
  7.2 44.1 %all-gather.5.cloned.1.call-start = ((), (), s32[]{:S(2)}) async-start(), calls=%async_computation.4 | async-start | bytes 2621440 | tf_op jit(solution)/shard_map/all_gather | solution.py:77
  10.5 1.4 copy-start.5
  24.8 16.9 %all-to-all-start = ((bf16[8,96,256]{2,1,0:T(8,128)(2,1)}), bf16[8,96,256]{2,1,0:T(8,128)(2,1)S(1)}, u32[]{:S(2)}, u32[]{:S(2)}) async-start(bf16[8,96,256]{2,1,0:T(8,128)(2,1)} %copy.188), calls=%async_computation | async-start | bytes 786432 | tf_op jit(solution)/shard_map/all_to_all | solution.py:103
  29.6 141.2 %all-gather.7.cloned.1.call-start = ((), (), s32[]{:S(2)}) async-start(), calls=%async_computation.5 | async-start | bytes 19169280 | tf_op jit(solution)/shard_map/all_gather | solution.py:113
  54.4 10.6 %copy-start.7 = (s32[8,8]{1,0:T(8,128)S(1)}, s32[8,8]{1,0:T(8,128)}, u32[]{:S(2)}) copy-start(s32[8,8]{1,0:T(8,128)} %param.18) | copy-start | bytes 772
  64.2 175.5 %all-gather.9.cloned.1.call-start = ((), (), s32[]{:S(2)}) async-start(), calls=%async_computation.6 | async-start | bytes 4423680 | tf_op jit(solution)/shard_map/all_gather | solution.py:78
  179.2 5.3 %copy-start.6 = (f32[12,8]{0,1:T(8,128)S(1)}, f32[12,8]{0,1:T(8,128)}, u32[]{:S(2)}) copy-start(f32[12,8]{0,1:T(8,128)} %param.20) | copy-start | bytes 1156
  179.2 54.5 %copy-start.8 = (f32[8,24]{1,0:T(8,128)S(1)}, f32[8,24]{1,0:T(8,128)}, u32[]{:S(2)}) copy-start(f32[8,24]{1,0:T(8,128)} %param.19) | copy-start | bytes 2308
  179.2 62.6 %all-to-all-start.2 = ((bf16[64,24,768]{2,1,0:T(8,128)(2,1)}), bf16[64,24,768]{2,1,0:T(8,128)(2,1)}, u32[]{:S(2)}, u32[]{:S(2)}) async-start(bf16[64,24,768]{2,1,0:T(8,128)(2,1)} %gather_fusion), calls=%async_computation.2 | async-start | bytes 4718592 | tf_op jit(solution)/shard_map/all_to_all | solution.py:115
  183.9 95.6 %all-gather.11.cloned.1.call-start = ((), (), s32[]{:S(2)}) async-start(), calls=%async_computation.7 | async-start | bytes 1474560 | tf_op jit(solution)/shard_map/all_gather | solution.py:79
  243.8 1.4 copy-start.4
  267.7 5.0 %copy-start.3 = (bf16[16,96,768]{1,2,0:T(8,128)(2,1)S(1)}, bf16[16,96,768]{1,2,0:T(8,128)(2,1)}, u32[]{:S(2)}) copy-start(bf16[16,96,768]{1,2,0:T(8,128)(2,1)} %copy.194) | copy-start | bytes 7077892
  284.7 0.8 copy-start.9
  284.8 8.4 %copy-start.10 = (s32[8,24]{1,0:T(8,128)S(1)}, s32[8,24]{1,0:T(8,128)}, u32[]{:S(2)}) copy-start(s32[8,24]{1,0:T(8,128)} %param.21) | copy-start | bytes 2308
  285.5 95.0 %copy-start.1 = (bf16[1024,768]{1,0:T(8,128)(2,1)S(1)}, bf16[1024,768]{1,0:T(8,128)(2,1)}, u32[]{:S(2)}) copy-start(bf16[1024,768]{1,0:T(8,128)(2,1)} %param.14) | copy-start | bytes 4718596
  287.3 7.5 %all-to-all-start.3 = ((f32[4,1,1536]{2,1,0:T(1,128)}), f32[4,1,1536]{2,1,0:T(1,128)S(1)}, u32[]{:S(2)}, u32[]{:S(2)}) async-start(f32[4,1,1536]{2,1,0:T(1,128)} %reshape.763), calls=%async_computation.3 | async-start | bytes 49152 | tf_op jit(solution)/shard_map/all_to_all | solution.py:151
Sparse Core Ops, SparseCore 0:
  9.8 41.3 all-gather.4
  64.4 106.3 all-gather.6
  172.6 67.1 all-gather.8
  241.4 23.4 all-gather.10

commit v2 on v1

--- a/solution.py
+++ b/solution.py
@@ -1,6 +1,8 @@
 import jax
 import jax.numpy as jnp
 from jax import lax
+from jax.experimental import pallas as pl
+from jax.experimental.pallas import tpu as pltpu
 from jax.sharding import PartitionSpec as P
 
 HD = 64
@@ -49,6 +51,483 @@
         residual = world_pts[:, None, :] - predicted
         summed = summed + jnp.sum(weight[:, None, :] * confidence * residual * residual)
     return summed * loss_scale
+
+
+YS, ZS, CORES = 4, 8, 2
+FIRST = 5
+MESH = pl.DeviceIdType.MESH
+
+
+def link_plan(images):
+    latency = 1.0
+    split = {"z": (0, FIRST), "y": (FIRST, images)}
+    free = {"y+": 0.0, "y-": 0.0, "z+": 0.0, "z-": 0.0}
+    arrivals = []
+
+    def push(now, link, source, target, span):
+        begin = max(now, free[link])
+        free[link] = begin + (span[1] - span[0])
+        arrivals.append((free[link] + latency, len(arrivals), link, source, target, span))
+
+    def forward(now, dy, dz, span):
+        if span[1] <= FIRST:
+            low, high = split["z"]
+            half = (low + high + 1) // 2
+            if dy == 0:
+                if dz in (0, 1, 2):
+                    push(now, "z+", (dy, dz), (dy, dz + 1), span)
+                if dz == 3:
+                    push(now, "z+", (dy, dz), (dy, 4), (low, half))
+                if dz in (0, 7, 6):
+                    push(now, "z-", (dy, dz), (dy, (dz - 1) % ZS), span)
+                if dz == 5:
+                    push(now, "z-", (dy, dz), (dy, 4), (half, high))
+                push(now, "y+", (dy, dz), (1, dz), span)
+                push(now, "y-", (dy, dz), (3, dz), span)
+            if dy == 1 and dz % 2 == 0:
+                push(now, "y+", (dy, dz), (2, dz), span)
+            if dy == 3 and dz % 2 == 1:
+                push(now, "y-", (dy, dz), (2, dz), span)
+        else:
+            low, high = split["y"]
+            half = (low + high + 1) // 2
+            if dz == 0:
+                if dy == 0:
+                    push(now, "y+", (0, 0), (1, 0), span)
+                    push(now, "y-", (0, 0), (3, 0), span)
+                if dy == 1:
+                    push(now, "y+", (1, 0), (2, 0), (low, half))
+                if dy == 3:
+                    push(now, "y-", (3, 0), (2, 0), (half, high))
+            if dz in (0, 1, 2):
+                push(now, "z+", (dy, dz), (dy, dz + 1), span)
+            if dz == 3 and dy < 2:
+                push(now, "z+", (dy, dz), (dy, 4), span)
+            if dz in (0, 7, 6):
+                push(now, "z-", (dy, dz), (dy, (dz - 1) % ZS), span)
+            if dz == 5 and dy >= 2:
+                push(now, "z-", (dy, dz), (dy, 4), span)
+
+    forward(0.0, 0, 0, split["z"])
+    forward(0.0, 0, 0, split["y"])
+    sent = []
+    steps = [("send", list(range(len(arrivals))))]
+    waited = set()
+    while len(waited) < len(arrivals):
+        entry = min(e for e in arrivals if e[1] not in waited)
+        waited.add(entry[1])
+        before = len(arrivals)
+        forward(entry[0], entry[4][0], entry[4][1], entry[5])
+        steps.append(("wait", entry[1]))
+        steps.append(("send", list(range(before, len(arrivals)))))
+    by_number = sorted(arrivals, key=lambda e: e[1])
+    return steps, [e[2:] for e in by_number]
+
+
+def exchange_kernel(
+    pick_ref,
+    rows_ref,
+    emb_ref,
+    weights_ref,
+    pose_ref,
+    far_ref,
+    own_ref,
+    weights_all,
+    pose_all,
+    held,
+    staged,
+    ring_send,
+    ring_recv,
+    twin_send,
+    twin_recv,
+    line_send,
+    line_recv,
+    pose_send,
+    pose_recv,
+    local_sem,
+):
+    images = rows_ref.shape[0]
+    here = lax.axis_index("img")
+    me = lax.axis_index("mp")
+    core = lax.rem(here, 2)
+    z = lax.rem(here // 2, ZS)
+    y = here // (2 * ZS)
+    split = far_ref.shape[1]
+    per_dev = far_ref.shape[0]
+
+    def spot(yy, zz, cc):
+        return ((yy * ZS + zz) * 2 + cc, me)
+
+    def mate(step):
+        return (here, lax.rem(me + step, split))
+
+    twin = spot(y, z, 1 - core)
+    links = {
+        "y+": spot(lax.rem(y + 1, YS), z, core),
+        "y-": spot(lax.rem(y + YS - 1, YS), z, core),
+        "z+": spot(y, lax.rem(z + 1, ZS), core),
+        "z-": spot(y, lax.rem(z + ZS - 1, ZS), core),
+    }
+    line = [(dz, dc) for dz in range(ZS) for dc in range(CORES) if dz or dc]
+
+    def line_peer(dz, dc, sign):
+        return spot(y, lax.rem(z + ZS + sign * dz, ZS), lax.rem(core + dc, 2))
+
+    def y_peer(dy, sign):
+        return spot(lax.rem(y + YS + sign * dy, YS), z, core)
+
+    barrier = pltpu.get_barrier_semaphore()
+    peers = [line_peer(dz, dc, 1) for dz, dc in line]
+    peers += [y_peer(dy, 1) for dy in range(1, YS)]
+    peers += [mate(step) for step in range(1, split)]
+    for peer in peers:
+        pl.semaphore_signal(barrier, inc=1, device_id=peer, device_id_type=MESH)
+    held[pl.ds(0, images)] = rows_ref[...]
+    pose_all[here] = pose_ref[...]
+    pl.semaphore_wait(barrier, len(peers))
+
+    def remote(source, target, send, recv, device):
+        return pltpu.make_async_remote_copy(
+            src_ref=source,
+            dst_ref=target,
+            send_sem=send,
+            recv_sem=recv,
+            device_id=device,
+            device_id_type=MESH,
+        )
+
+    steps, plan = link_plan(images)
+
+    def block(side, slot, span):
+        first = ((side * YS + slot[0]) * ZS + slot[1]) * images
+        return held.at[pl.ds(first + span[0], span[1] - span[0])]
+
+    def ring(number):
+        link, source, target, span = plan[number]
+        return remote(
+            block(0, source, span),
+            block(0, target, span),
+            ring_send.at[number],
+            ring_recv.at[number],
+            links[link],
+        )
+
+    twins = [((0, 0), (0, images))] + [(entry[2], entry[3]) for entry in plan]
+
+    def twin_copy(number):
+        slot, span = twins[number]
+        return remote(
+            block(0, slot, span),
+            block(1, slot, span),
+            twin_send.at[number],
+            twin_recv.at[number],
+            twin,
+        )
+
+    for number in steps[0][1]:
+        ring(number).start()
+    twin_copy(0).start()
+
+    def pose_line(dz, dc, number, slot):
+        return remote(
+            pose_all.at[slot],
+            pose_all.at[slot],
+            pose_send.at[number],
+            pose_recv.at[number],
+            line_peer(dz, dc, 1),
+        )
+
+    for number, (dz, dc) in enumerate(line):
+        pose_line(dz, dc, number, here).start()
+
+    pair_images = images // split
+
+    def own_copy(step, slot):
+        return remote(
+            emb_ref.at[pl.ds(pair_images * lax.rem(me + step, split), pair_images)],
+            own_ref.at[:, slot],
+            line_send.at[step],
+            line_recv.at[step],
+            mate(step),
+        )
+
+    def weight_copy(step, slot):
+        return remote(
+            weights_ref.at[pl.ds(2 * core, 2)],
+            weights_all.at[pl.ds(2 * core, 2), slot],
+            line_send.at[split + step],
+            line_recv.at[split + step],
+            mate(step),
+        )
+
+    def weight_twin(step, half, slot):
+        return remote(
+            weights_all.at[pl.ds(2 * half, 2), slot],
+            weights_all.at[pl.ds(2 * half, 2), slot],
+            line_send.at[2 * split + step],
+            line_recv.at[2 * split + step],
+            twin,
+        )
+
+    def far_copy(step, slot):
+        return remote(
+            staged.at[pl.ds(per_dev * lax.rem(me + step, split), per_dev)],
+            far_ref.at[:, slot],
+            line_send.at[3 * split + step],
+            line_recv.at[3 * split + step],
+            mate(step),
+        )
+
+    for step in range(1, split):
+        own_copy(step, me).start()
+        weight_copy(step, me).start()
+    own_local = pltpu.make_async_copy(
+        emb_ref.at[pl.ds(pair_images * me, pair_images)], own_ref.at[:, me], local_sem.at[0]
+    )
+    own_local.start()
+    weight_local = pltpu.make_async_copy(weights_ref, weights_all.at[:, me], local_sem.at[1])
+    weight_local.start()
+
+    def run(part):
+        for kind, what in part:
+            if kind == "wait":
+                ring(what).wait_recv()
+                twin_copy(1 + what).start()
+            else:
+                for number in what:
+                    ring(number).start()
+
+    third = len(steps) // 3
+    run(steps[1:third])
+    for number, (dz, dc) in enumerate(line):
+        source = line_peer(dz, dc, -1)[0]
+        pose_line(dz, dc, number, source).wait_recv()
+
+    def pose_cross(dy, row):
+        return remote(
+            pose_all.at[pl.ds(row * 2 * ZS, 2 * ZS)],
+            pose_all.at[pl.ds(row * 2 * ZS, 2 * ZS)],
+            pose_send.at[len(line) + dy - 1],
+            pose_recv.at[len(line) + dy - 1],
+            y_peer(dy, 1),
+        )
+
+    for dy in range(1, YS):
+        pose_cross(dy, y).start()
+    run(steps[third : 2 * third])
+    for step in range(1, split):
+        source = lax.rem(me + split - step, split)
+        weight_copy(step, source).wait_recv()
+        weight_twin(step, core, source).start()
+    run(steps[2 * third :])
+    for number in range(len(twins)):
+        twin_copy(number).wait_recv()
+
+    def pick(index, carry):
+        staged[index] = held[pick_ref[index]]
+        return carry
+
+    lax.fori_loop(0, per_dev * split, pick, 0)
+    for step in (2, 1, 3):
+        far_copy(step, me).start()
+    far_local = pltpu.make_async_copy(
+        staged.at[pl.ds(per_dev * me, per_dev)], far_ref.at[:, me], local_sem.at[2]
+    )
+    far_local.start()
+    for dy in range(1, YS):
+        pose_cross(dy, lax.rem(y + YS - dy, YS)).wait_recv()
+    for step in range(1, split):
+        source = lax.rem(me + split - step, split)
+        own_copy(step, source).wait_recv()
+        weight_twin(step, 1 - core, source).wait_recv()
+    own_local.wait()
+    weight_local.wait()
+    for number in range(len(plan)):
+        ring(number).wait_send()
+    for number in range(len(twins)):
+        twin_copy(number).wait_send()
+    for number, (dz, dc) in enumerate(line):
+        pose_line(dz, dc, number, here).wait_send()
+    for dy in range(1, YS):
+        pose_cross(dy, y).wait_send()
+    for step in range(1, split):
+        own_copy(step, me).wait_send()
+        weight_copy(step, me).wait_send()
+        weight_twin(step, core, lax.rem(me + split - step, split)).wait_send()
+    for step in (1, 3, 2):
+        source = lax.rem(me + split - step, split)
+        far_copy(step, source).wait_recv()
+        far_copy(step, me).wait_send()
+    far_local.wait()
+
+
+def exchange(pick, rows, emb, weights, pose, pairs, groups, split):
+    images, share, width = rows.shape
+    count = len(link_plan(images)[1])
+    vmem = pl.BlockSpec(memory_space=pltpu.VMEM)
+    return pl.pallas_call(
+        exchange_kernel,
+        out_shape=(
+            jax.ShapeDtypeStruct((pairs // split, split, share, width), jnp.bfloat16),
+            jax.ShapeDtypeStruct((images // split, split, share, width), jnp.bfloat16),
+            jax.ShapeDtypeStruct((4, split) + weights.shape[1:], jnp.bfloat16),
+            jax.ShapeDtypeStruct((groups,) + pose.shape, jnp.bfloat16),
+        ),
+        in_specs=[pl.BlockSpec(memory_space=pltpu.SMEM)] + [vmem] * 4,
+        out_specs=(vmem,) * 4,
+        scratch_shapes=[
+            pltpu.VMEM((groups * images, share, width), jnp.bfloat16),
+            pltpu.VMEM((pairs, share, width), jnp.bfloat16),
+            pltpu.SemaphoreType.DMA((count,)),
+            pltpu.SemaphoreType.DMA((count,)),
+            pltpu.SemaphoreType.DMA((count + 1,)),
+            pltpu.SemaphoreType.DMA((count + 1,)),
+            pltpu.SemaphoreType.DMA((4 * split,)),
+            pltpu.SemaphoreType.DMA((4 * split,)),
+            pltpu.SemaphoreType.DMA((2 * ZS + YS,)),
+            pltpu.SemaphoreType.DMA((2 * ZS + YS,)),
+            pltpu.SemaphoreType.DMA((3,)),
+        ],
+        compiler_params=pltpu.CompilerParams(
+            collective_id=0, has_side_effects=True, vmem_limit_bytes=56 * 2**20
+        ),
+        name="exchange",
+    )(pick, rows, emb, weights, pose)
+
+
+def reduce_kernel(
+    grad_ref, total_ref, across, summed, lined, part, crossed, x_send, x_recv, l_send, l_recv, c_send, c_recv
+):
+    here = lax.axis_index("img")
+    me = lax.axis_index("mp")
+    core = lax.rem(here, 2)
+    z = lax.rem(here // 2, ZS)
+    y = here // (2 * ZS)
+    split = across.shape[0]
+    row = z * 2 + core
+    rows = 2 * ZS
+    line = [(dz, dc) for dz in range(ZS) for dc in range(CORES) if dz or dc]
+
+    def line_row(dz, dc, sign):
+        return lax.rem(z + ZS + sign * dz, ZS) * 2 + lax.rem(core + dc, 2)
+
+    def mate(step):
+        return (here, lax.rem(me + step, split))
+
+    barrier = pltpu.get_barrier_semaphore()
+    for step in range(1, split):
+        pl.semaphore_signal(barrier, inc=1, device_id=mate(step), device_id_type=MESH)
+    for dz, dc in line:
+        pl.semaphore_signal(
+            barrier, inc=1, device_id=(y * rows + line_row(dz, dc, 1), me), device_id_type=MESH
+        )
+    for other in range(YS):
+        pl.semaphore_signal(barrier, inc=1, device_id=(other * rows + row, y), device_id_type=MESH)
+
+    pl.semaphore_wait(barrier, split - 1 + len(line) + YS)
+
+    def remote(source, target, send, recv, device):
+        return pltpu.make_async_remote_copy(
+            src_ref=source,
+            dst_ref=target,
+            send_sem=send,
+            recv_sem=recv,
+            device_id=device,
+            device_id_type=MESH,
+        )
+
+    def x_copy(step, slot):
+        return remote(
+            grad_ref.at[lax.rem(me + step, split)],
+            across.at[slot],
+            x_send.at[step],
+            x_recv.at[step],
+            mate(step),
+        )
+
+    for step in range(1, split):
+        x_copy(step, me).start()
+    across[me] = grad_ref[me]
+    for step in range(1, split):
+        x_copy(step, lax.rem(me + split - step, split)).wait_recv()
+    summed[...] = jnp.sum(across[...], axis=0)
+
+    def l_copy(number, dz, dc, slot):
+        target = line_row(dz, dc, 1)
+        return remote(
+            summed.at[target],
+            lined.at[slot],
+            l_send.at[number],
+            l_recv.at[number],
+            (y * rows + target, me),
+        )
+
+    for number, (dz, dc) in enumerate(line):
+        l_copy(number, dz, dc, row).start()
+    lined[row] = summed[row]
+    for number, (dz, dc) in enumerate(line):
+        l_copy(number, dz, dc, line_row(dz, dc, -1)).wait_recv()
+    part[...] = jnp.sum(lined[...], axis=0)
+
+    def c_copy(other, slot):
+        return remote(
+            part, crossed.at[slot], c_send.at[other], c_recv.at[slot], (me * rows + row, other)
+        )
+
+    for other in range(split):
+
+        @pl.when(jnp.logical_or(y != me, me != other))
+        def _():
+            c_copy(other, y).start()
+
+    @pl.when(y == me)
+    def _():
+        crossed[y] = part[...]
+
+    for other in range(YS):
+
+        @pl.when(jnp.logical_or(y != me, y != other))
+        def _():
+            c_copy(0, other).wait_recv()
+
+    total_ref[...] = jnp.sum(crossed[...], axis=0)
+    for step in range(1, split):
+        x_copy(step, me).wait_send()
+    for number, (dz, dc) in enumerate(line):
+        l_copy(number, dz, dc, row).wait_send()
+    for other in range(split):
+
+        @pl.when(jnp.logical_or(y != me, me != other))
+        def _():
+            c_copy(other, y).wait_send()
+
+
+def reduce_poses(dense, split):
+    groups = dense.shape[0] * dense.shape[1]
+    tile = dense.shape[2:]
+    vmem = pl.BlockSpec(memory_space=pltpu.VMEM)
+    rows = 2 * ZS
+    return pl.pallas_call(
+        reduce_kernel,
+        out_shape=jax.ShapeDtypeStruct(tile, jnp.float32),
+        in_specs=[vmem],
+        out_specs=vmem,
+        scratch_shapes=[
+            pltpu.VMEM((split, rows) + tile, jnp.float32),
+            pltpu.VMEM((rows,) + tile, jnp.float32),
+            pltpu.VMEM((rows,) + tile, jnp.float32),
+            pltpu.VMEM(tile, jnp.float32),
+            pltpu.VMEM((YS,) + tile, jnp.float32),
+            pltpu.SemaphoreType.DMA((split,)),
+            pltpu.SemaphoreType.DMA((split,)),
+            pltpu.SemaphoreType.DMA((rows,)),
+            pltpu.SemaphoreType.DMA((rows,)),
+            pltpu.SemaphoreType.DMA((split,)),
+            pltpu.SemaphoreType.DMA((YS,)),
+        ],
+        compiler_params=pltpu.CompilerParams(collective_id=1, has_side_effects=True),
+        name="reduce_poses",
+    )(dense)
 
 
 def shards(
@@ -75,9 +554,12 @@
     flat_partner = partners.reshape(-1)
     pair_count = flat_partner.shape[0]
     out_full = lax.all_gather(encoder_out, "mp", axis=0, tiled=True)
-    proj_full = lax.all_gather(jnp.transpose(decoder_proj, (1, 2, 0)), "mp", axis=1, tiled=True)
-    dec_out_full = lax.all_gather(decoder_out, "mp", axis=0, tiled=True)
-    all_poses = lax.all_gather(camera_poses.astype(jnp.bfloat16), "img", axis=1, tiled=True)
+    groups = lax.axis_size("img")
+    here = lax.axis_index("img")
+    weights = jnp.concatenate([jnp.transpose(decoder_proj, (1, 2, 0)), decoder_out[None]], axis=0)
+    pose_tile = jnp.pad(
+        camera_poses.astype(jnp.bfloat16), ((0, 4), (0, 128 - camera_poses.shape[1]))
+    )
 
     normed = norm_rows(patches.astype(jnp.float32))
     projected = jnp.dot(
@@ -100,19 +582,30 @@
         preferred_element_type=jnp.float32,
     )
     mixed_rows = mixed_rows.astype(jnp.bfloat16).reshape(images, tokens, enc_local)
-    mixed_own = lax.all_to_all(mixed_rows, "mp", split_axis=0, concat_axis=2, tiled=True)
-    patch_own = lax.dynamic_slice_in_dim(patches, place * own_count, own_count, 0)
+    token_share = tokens // split
+    first_token = place * token_share
+    mixed_own = lax.all_to_all(mixed_rows, "mp", split_axis=1, concat_axis=2, tiled=True)
+    patch_own = lax.dynamic_slice_in_dim(patches, first_token, token_share, 1)
     encoded = patch_own.astype(jnp.float32) + jnp.dot(
         mixed_own, out_full, preferred_element_type=jnp.float32
     )
-    embedded = jnp.dot(
+    emb_share = jnp.dot(
         norm_rows(encoded), decoder_embed, preferred_element_type=jnp.float32
     ).astype(jnp.bfloat16)
+    rows_share = norm_rows(emb_share.astype(jnp.float32))
+    owner = flat_partner // images
+    shift_y = (here // (2 * ZS) - owner // (2 * ZS)) % YS
+    shift_z = ((here // 2) % ZS - (owner // 2) % ZS) % ZS
+    shift_core = (here - owner) % 2
+    pick = ((shift_core * YS + shift_y) * ZS + shift_z) * images + flat_partner % images
+    far_rows, own_rows, weights_full, pose_tiles = exchange(
+        pick, rows_share, emb_share, weights, pose_tile, pair_count, groups, split
+    )
+    far_rows = far_rows.reshape(pair_count // split, tokens, dec_width)
+    embedded = own_rows.reshape(own_count, tokens, dec_width)
     rows = norm_rows(embedded.astype(jnp.float32))
-    quarter = lax.all_to_all(rows, "mp", split_axis=1, concat_axis=0, tiled=True)
-    everything = lax.all_gather(quarter, "img", axis=0, tiled=True)
-    picked = everything[flat_partner]
-    far_rows = lax.all_to_all(picked, "mp", split_axis=0, concat_axis=1, tiled=True)
+    proj_full = weights_full.reshape(4, dec_width, dec_width)
+    dec_out_full = proj_full[3]
     own_pairs = pair_count // split
 
     def project(values, which):
@@ -149,14 +642,13 @@
         preferred_element_type=jnp.float32,
     )
     moved = lax.all_to_all(head_own, "mp", split_axis=2, concat_axis=1, tiled=True)
-    token_share = tokens // split
-    first_token = place * token_share
     points = moved[:3]
     confidence = 1.0 + jnp.exp(moved[3])
     pointmap = jnp.concatenate([points, confidence[None]], axis=0)
     ray_dirs = make_rays(first_token + jnp.arange(token_share, dtype=jnp.int32), tokens // 16)
     weight = valid_mask.astype(jnp.float32)
-    pose_far = all_poses[:, flat_partner].astype(jnp.float32).reshape(12, images, K)
+    pose_table = pose_tiles[:, :12, :images].transpose(1, 0, 2).reshape(12, groups * images)
+    pose_far = pose_table[:, flat_partner].astype(jnp.float32).reshape(12, images, K)
     point_grid = points.reshape(3, images, K, token_share)
     conf_grid = confidence.reshape(images, K, token_share)
 
@@ -168,7 +660,6 @@
     loss_value, pullback = jax.vjp(loss_fn, depths, camera_poses, pose_far)
     grad_depth, grad_own, grad_far = pullback(jnp.ones_like(loss_value))
     grad_far_flat = grad_far.reshape(12, pair_count)
-    groups = lax.axis_size("img")
     total_images = groups * images
     base_image = lax.axis_index("img") * images
     image_ids = jnp.arange(total_images, dtype=jnp.int32)
@@ -179,8 +670,10 @@
     dense_grad = jnp.dot(grad_far_flat, partner_hits, precision=lax.Precision.HIGHEST) + jnp.dot(
         grad_own, own_hits, precision=lax.Precision.HIGHEST
     )
-    summed = lax.psum(dense_grad, ("img", "mp"))
-    grad_pose = lax.dynamic_slice_in_dim(summed, base_image, images, 1)
+    dense_rows = dense_grad.reshape(12, groups, images).transpose(1, 0, 2).reshape(groups, 1, -1)
+    dense_rows = jnp.pad(dense_rows, ((0, 0), (0, 7), (0, 128 - 12 * images)))
+    total = reduce_poses(dense_rows.reshape(YS, 2 * ZS, 8, 128), split)
+    grad_pose = total[0, : 12 * images].reshape(12, images)
     new_depths = depths - depth_step * grad_depth
     new_poses = camera_poses - pose_step * grad_pose
     return (pointmap, new_depths, new_poses)

time: 388 us -> 244 us (0.63)
  blocking collectives: 133 us -> 0 us
  waiting for transfers between devices: 134 us -> 11.2 us
  Pallas kernels: 0 us -> 120 us
  other arithmetic: 12.3 us -> 22.1 us
  matrix products: 39.4 us -> 30.7 us
  local copies, waits for them, and re-layouts: 40.8 us -> 35.9 us
  starting transfers between devices: 13.1 us -> 8.46 us
    pallas_call x0 -> x2, Pallas kernels: none -> 120 us  [the longest x1 100 us: exchange(): pl.pallas_call(exchange_kernel, out_shape=(jax.ShapeDtypeStruct((pairs //...]
    all_gather x3 -> x0, waiting for transfers between devices: 112 us -> none  [the longest x1 106 us: shards(): everything = lax.all_gather(quarter, 'img', axis=0, tiled=True)]
    psum x1 -> x0, blocking collectives: 77.3 us -> none  [shards(): summed = lax.psum(dense_grad, ('img', 'mp'))]
    all_gather x1 -> x0, blocking collectives: 47.7 us -> none  [shards(): lax.all_gather(camera_poses.astype(jnp.bfloat16), 'img', axis=1, tiled=True)]
    all_to_all x2 -> x1, waiting for transfers between devices: 12 us -> 3.36 us  [shards(): lax.all_to_all(mixed_rows, 'mp', split_axis=1, concat_axis=2, tiled=True)]
    all_to_all x1 -> x0, blocking collectives: 8.35 us -> none  [shards(): lax.all_to_all(rows, 'mp', split_axis=1, concat_axis=0, tiled=True)]
    gather x2 -> x1, local copies, waits for them, and re-layouts: 9.08 us -> 0.76 us  [shards(): pose_table[:, flat_partner].astype(jnp.float32).reshape(12, images, K)]
    all_to_all x2 -> x1, starting transfers between devices: 9.52 us -> 4.84 us  [shards(): lax.all_to_all(mixed_rows, 'mp', split_axis=1, concat_axis=2, tiled=True)]
  transfers between devices with their start and end apart: 7 -> 3, of which waited for: 5 -> 2; matrix products, arithmetic and copies ran while one was open for 18% -> 13% of each run, Pallas kernels for 0% -> 0%
where the time goes in v2:
time: 244 us; the launch traced here: 243 us
  Pallas kernels  120 us (49%)
  local copies, waits for them, and re-layouts  35.9 us (15%)
  matrix products  30.7 us (13%)
  other arithmetic  22.1 us (9%)
  between operations  14.9 us (6%)
  waiting for transfers between devices  11.2 us (5%)
  starting transfers between devices  8.46 us (3%)
    pallas_call x1, Pallas kernels, exchange(): pl.pallas_call(exchange_kernel, out_shape=(jax.ShapeDtypeStruct((pairs //...  100 us
    pallas_call x1, Pallas kernels, reduce_poses(): pl.pallas_call(reduce_kernel, out_shape=jax.ShapeDtypeStruct(tile, jnp.fl...  20 us
    dot_general x3, matrix products, project(): lax.dot_general(values, proj_full[which], (((2,), (1,)), ((), ())), prefe...  9.25 us
    convert_element_type x3, local copies, waits for them, and re-layouts, project(): return lax.dot_general(values, proj_full[which], (((2,), (1,)), ((), ()))...  8.1 us
    all_gather x1, waiting for transfers between devices, shards(): out_full = lax.all_gather(encoder_out, 'mp', axis=0, tiled=True)  7.12 us
    unnamed x90, local copies, waits for them, and re-layouts  5.67 us
    dot_general x1, matrix products, shards(): jnp.einsum('akhqt,akthd->akqhd', soft_weights(cross_scores), far_values,...  5.35 us
    sub x1, other arithmetic, soft_weights(): expos = jnp.exp(scores - top_score)  5.16 us
  transfers between devices with their start and end apart: 3, of which 2 were waited for; matrix products, arithmetic and copies ran while one was open for 13% of the time, Pallas kernels for 0%

profile of v2, /device:TPU:1, one launch (start us, length us, event | category | flops | bytes accessed | tf_op | source)
XLA Modules:
  0.0 243.2 jit_solution(5085838371200834076)
XLA Ops:
  7.2 0.7 all-gather.2.cloned.1.call-update
  7.9 2.6 %copy.205 = bf16[1024,3,256]{0,2,1:T(8,128)(2,1)} copy(bf16[1024,3,256]{2,0,1:T(8,128)(2,1)} %param.12) | data formatting | bytes 3145728 | tf_op args[1]
  11.9 2.5 %fusion.28 = bf16[8,96,768]{2,1,0:T(8,128)(2,1)} fusion(bf16[1024,768,1]{0,1,2:T(8,128)(2,1)S(1)} %bitcast.159, bf16[8,96,1024]{2,1,0:T(8,128)(2,1)S(1)} %copy-done.3, f32[8,96]{1,0:T(8,128)S(1)} %add_rsqrt_fusion.4, f32[8,96]{1,0:T(8,128)S(1)} %broadcast_multiply_fusion.4), kind=kOutput, calls=%fused_computation.35 | convolution fusion | flops 1211695104 | bytes 4331520 | tf_op jit(solution)/shard_map/dot_general | solution.py:565
  14.4 2.5 %copy.207 = bf16[8,96,768]{1,2,0:T(8,128)(2,1)} copy(bf16[8,96,768]{2,1,0:T(8,128)(2,1)} %fusion.28) | data formatting | bytes 2359296 | tf_op jit(solution)/shard_map/convert_element_type | solution.py:568
  16.9 3.1 %fusion.90 = (f32[8,4,96]{2,1,0:T(4,128)S(1)}, f32[8,4,96,96]{2,3,1,0:T(8,128)}) fusion(bf16[8,96,3,4,64]{1,4,3,2,0:T(8,128)(2,1)} %bitcast.162), kind=kOutput, calls=%fused_computation.218 | convolution fusion | flops 38633568 | bytes 2240512 | tf_op jit(solution)/shard_map/sub | solution.py:26
  20.0 2.8 %convolution_convert_fusion.2 = bf16[8,4,64,96]{3,2,1,0:T(8,128)(2,1)} fusion(f32[8,4,96,96]{2,3,1,0:T(8,128)} %get-tuple-element.103, f32[8,4,96]{2,1,0:T(4,128)S(1)} %get-tuple-element.102, bf16[8,96,3,4,64]{1,4,3,2,0:T(8,128)(2,1)} %bitcast.163), kind=kOutput, calls=%fused_computation.38 | convolution fusion | flops 38535168 | bytes 2502656 | tf_op jit(solution)/shard_map/ahqt,athd->aqhd/dot_general | solution.py:578
  22.8 2.1 copy.212
  24.9 4.8 %all-to-all-start = ((bf16[8,96,256]{2,0,1:T(8,128)(2,1)}), bf16[8,96,256]{2,0,1:T(8,128)(2,1)S(1)}, u32[]{:S(2)}, u32[]{:S(2)}) async-start(bf16[8,96,256]{2,0,1:T(8,128)(2,1)} %copy.212), calls=%async_computation | async-start | bytes 786432 | tf_op jit(solution)/shard_map/all_to_all | solution.py:587
  29.8 0.6 reshape.752
  30.4 0.6 reshape.763
  31.0 0.7 copy.267
  31.7 0.6 pad.80.pose_ref
  32.4 0.7 fusion.84
  33.0 0.6 pad_clamp_fusion
  34.1 2.4 pad_maximum_fusion.weights_ref
  37.7 0.8 multiply_add_fusion.4
  38.4 3.4 %all-to-all-done = bf16[8,96,256]{2,0,1:T(8,128)(2,1)S(1)} async-done(((bf16[8,96,256]{2,0,1:T(8,128)(2,1)}), bf16[8,96,256]{2,0,1:T(8,128)(2,1)S(1)}, u32[]{:S(2)}, u32[]{:S(2)}) %all-to-all-start) | async-done | bytes 393248 | tf_op jit(solution)/shard_map/all_to_all | solution.py:587
  41.8 1.1 copy.214
  42.9 1.3 all_to_all.27
  44.1 7.1 %all-gather.2.cloned.1.call-done = bf16[1024,1024]{1,0:T(8,128)(2,1)} async-done(((bf16[256,1024]{1,0:T(8,128)(2,1)}), bf16[1024,1024]{1,0:T(8,128)(2,1)}) %all-gather.2.cloned.1.call-update) | async-done | bytes 2097168 | tf_op jit(solution)/shard_map/all_gather | solution.py:556
  51.2 2.3 fusion.91
  53.8 0.6 convert_reduce_fusion.1
  54.6 0.9 fusion.41.rows_ref
  55.6 100.0 %exchange.1 = (bf16[16,4,24,768]{3,2,1,0:T(8,128)(2,1)}, bf16[2,4,24,768]{3,2,1,0:T(8,128)(2,1)}, bf16[4,4,192,768]{3,2,1,0:T(8,128)(2,1)}, bf16[64,16,128]{2,1,0:T(8,128)(2,1)}) custom-call(s32[64]{0:T(128)} %fusion.74.pick_ref, bf16[8,24,768]{2,1,0:T(8,128)(2,1)} %fusion.41.rows_ref, bf16[8,24,768]{2,1,0:T(8,128)(2,1)} %copy-done.6, ...), custom_call_target="tpu_custom_call" | custom-call | tf_op jit(solution)/shard_map/exchange/pallas_call | solution.py:368
  155.6 1.1 convert_reduce_fusion.2
  156.7 1.8 convert.2
  158.5 3.9 %fusion.89 = (bf16[1,4,192,768]{3,2,1,0:T(8,128)(2,1)}, bf16[1,4,192,768]{3,2,1,0:T(8,128)(2,1)S(1)}, bf16[1,4,192,768]{3,2,1,0:T(8,128)(2,1)S(1)}, bf16[1,4,192,768]{3,2,1,0:T(8,128)(2,1)S(1)}) fusion(bf16[4,4,192,768]{3,2,1,0:T(8,128)(2,1)} %get-tuple-element.8), kind=kLoop, calls=%fused_computation.217 | loop fusion | bytes 9437184 | tf_op jit(solution)/shard_map/slice | solution.py:608
  162.4 3.5 %convolution_convert_fusion.1 = bf16[16,96,768]{2,1,0:T(8,128)(2,1)} fusion(bf16[16,96,768]{2,1,0:T(8,128)(2,1)S(1)} %bitcast.203, bf16[768,768,1]{1,0,2:T(8,128)(2,1)S(1)} %bitcast.165), kind=kOutput, calls=%fused_computation.27 | convolution fusion | flops 1813118976 | bytes 5898240 | tf_op jit(solution)/shard_map/dot_general | solution.py:612
  166.0 4.5 %copy.216 = bf16[16,96,768]{1,2,0:T(8,128)(2,1)} copy(bf16[16,96,768]{2,1,0:T(8,128)(2,1)} %convolution_convert_fusion.1) | data formatting | bytes 4718592 | tf_op jit(solution)/shard_map/convert_element_type | solution.py:617
  171.7 5.2 %convolution_convert_fusion = bf16[16,96,768]{2,1,0:T(8,128)(2,1)} fusion(bf16[16,96,768]{2,1,0:T(8,128)(2,1)} %bitcast.202, bf16[768,768,1]{1,0,2:T(8,128)(2,1)S(1)} %bitcast.164), kind=kOutput, calls=%fused_computation.26 | convolution fusion | flops 1813118976 | bytes 5898240 | tf_op jit(solution)/shard_map/dot_general | solution.py:612
  176.9 3.3 %copy.217 = bf16[16,96,768]{1,2,0:T(8,128)(2,1)S(1)} copy(bf16[16,96,768]{2,1,0:T(8,128)(2,1)} %convolution_convert_fusion) | data formatting | bytes 4718592 | tf_op jit(solution)/shard_map/convert_element_type | solution.py:617
  180.2 1.5 fusion.14
  181.7 5.2 %fusion.92 = (f32[2,8,12,96]{3,1,2,0:T(8,128)S(1)}, f32[2,8,12,96,96]{3,4,1,2,0:T(8,128)}) fusion(f32[2,12,8,96,96]{4,3,2,1,0:T(8,128)S(1)} %fusion.14), kind=kOutput, calls=%fused_computation.220 | output fusion | flops 7077983 | bytes 14229504 | tf_op jit(solution)/shard_map/sub | solution.py:26
  186.9 5.4 %fusion.16 = bf16[2,8,12,64,96]{4,3,2,1,0:T(8,128)(2,1)S(1)} fusion(bf16[2,8,96,12,64]{2,4,3,1,0:T(8,128)(2,1)S(1)} %bitcast.153, f32[2,8,12,96,96]{3,4,1,2,0:T(8,128)} %get-tuple-element.109, f32[2,8,12,96]{3,1,2,0:T(8,128)S(1)} %get-tuple-element.108), kind=kOutput, calls=%fused_computation.23 | convolution fusion | flops 231211008 | bytes 11870208 | tf_op jit(solution)/shard_map/akhqt,akthd->akqhd/dot_general | solution.py:627
  192.3 2.1 add_reduce_fusion
  194.4 0.8 multiply_reduce_fusion
  195.3 0.7 multiply_convert_fusion
  196.0 0.8 convolution_bitcast_fusion
  197.0 0.8 reshape.829
  197.8 3.6 %all-to-all-start.1 = ((f32[4,1,1536]{2,1,0:T(1,128)}), f32[4,1,1536]{2,1,0:T(1,128)S(1)}, u32[]{:S(2)}, u32[]{:S(2)}) async-start(f32[4,1,1536]{2,1,0:T(1,128)} %reshape.829), calls=%async_computation.1 | async-start | bytes 49152 | tf_op jit(solution)/shard_map/all_to_all | solution.py:644
  202.0 0.8 gather_fusion
  206.7 0.7 reduce.87
  211.9 0.9 multiply_reduce_fusion.19
  213.5 0.7 pad.105.clone
  214.2 20.0 %reduce_poses.1 = f32[8,128]{1,0:T(8,128)} custom-call(f32[4,16,8,128]{3,2,1,0:T(8,128)} %bitcast.167), custom_call_target="tpu_custom_call" | custom-call | tf_op jit(solution)/shard_map/reduce_poses/pallas_call | solution.py:510
  234.2 0.7 multiply_reduce_fusion.18
  235.0 0.7 copy.268
  235.7 0.6 pad_maximum_fusion.1
  (213 shorter events, 14.3 us)
Async XLA Ops:
  7.2 46.6 %copy-start = (bf16[1024,768]{1,0:T(8,128)(2,1)S(1)}, bf16[1024,768]{1,0:T(8,128)(2,1)}, u32[]{:S(2)}) copy-start(bf16[1024,768]{1,0:T(8,128)(2,1)} %param.14) | copy-start | bytes 4718596
  7.2 3.3 %copy-start.3 = (bf16[8,96,1024]{2,1,0:T(8,128)(2,1)S(1)}, bf16[8,96,1024]{2,1,0:T(8,128)(2,1)}, u32[]{:S(2)}) copy-start(bf16[8,96,1024]{2,1,0:T(8,128)(2,1)} %param.11) | copy-start | bytes 4718596
  7.2 44.1 %all-gather.2.cloned.1.call-start = ((), (), s32[]{:S(2)}) async-start(), calls=%async_computation.2 | async-start | bytes 2621440 | tf_op jit(solution)/shard_map/all_gather | solution.py:556
  10.5 1.4 copy-start.8
  20.0 9.7 %copy-start.12 = (s32[8,8]{1,0:T(8,128)S(1)}, s32[8,8]{1,0:T(8,128)}, u32[]{:S(2)}) copy-start(s32[8,8]{1,0:T(8,128)} %param.18) | copy-start | bytes 772
  20.0 10.9 %copy-start.9 = (f32[12,8]{0,1:T(8,128)S(1)}, f32[12,8]{0,1:T(8,128)}, u32[]{:S(2)}) copy-start(f32[12,8]{0,1:T(8,128)} %param.20) | copy-start | bytes 1156
  20.0 11.7 %copy-start.33 = (s32[8,24]{1,0:T(8,128)S(1)}, s32[8,24]{1,0:T(8,128)}, u32[]{:S(2)}) copy-start(s32[8,24]{1,0:T(8,128)} %param.21) | copy-start | bytes 2308
  24.9 16.9 %all-to-all-start = ((bf16[8,96,256]{2,0,1:T(8,128)(2,1)}), bf16[8,96,256]{2,0,1:T(8,128)(2,1)S(1)}, u32[]{:S(2)}, u32[]{:S(2)}) async-start(bf16[8,96,256]{2,0,1:T(8,128)(2,1)} %copy.212), calls=%async_computation | async-start | bytes 786432 | tf_op jit(solution)/shard_map/all_to_all | solution.py:587
  31.7 4.8 %copy-start.38 = (s32[64]{0:T(128)S(1)}, s32[64]{0:T(128)}, u32[]{:S(2)}) copy-start(s32[64]{0:T(128)} %reshape.752) | copy-start | bytes 772
  32.4 5.2 %copy-start.34 = (f32[24]{0:T(128)}, f32[24]{0:T(128)S(1)}, u32[]{:S(2)}) copy-start(f32[24]{0:T(128)S(1)} %get-tuple-element.112) | copy-start | bytes 292
  32.4 5.2 %copy-start.36 = (f32[24]{0:T(128)}, f32[24]{0:T(128)S(1)}, u32[]{:S(2)}) copy-start(f32[24]{0:T(128)S(1)} %get-tuple-element.113) | copy-start | bytes 292
  34.0 3.6 %copy-start.15 = (f32[8]{0:T(128)}, f32[8]{0:T(128)S(1)}, u32[]{:S(2)}) copy-start(f32[8]{0:T(128)S(1)} %get-tuple-element.77) | copy-start | bytes 100
  34.0 3.6 %copy-start.17 = (f32[8]{0:T(128)}, f32[8]{0:T(128)S(1)}, u32[]{:S(2)}) copy-start(f32[8]{0:T(128)S(1)} %get-tuple-element.78) | copy-start | bytes 100
  34.0 3.6 %copy-start.19 = (f32[8]{0:T(128)}, f32[8]{0:T(128)S(1)}, u32[]{:S(2)}) copy-start(f32[8]{0:T(128)S(1)} %get-tuple-element.80) | copy-start | bytes 100
  34.0 3.6 %copy-start.21 = (f32[8]{0:T(128)}, f32[8]{0:T(128)S(1)}, u32[]{:S(2)}) copy-start(f32[8]{0:T(128)S(1)} %get-tuple-element.81) | copy-start | bytes 100
  34.0 3.6 %copy-start.23 = (f32[8]{0:T(128)}, f32[8]{0:T(128)S(1)}, u32[]{:S(2)}) copy-start(f32[8]{0:T(128)S(1)} %get-tuple-element.82) | copy-start | bytes 100
  34.1 3.6 %copy-start.25 = (f32[8]{0:T(128)}, f32[8]{0:T(128)S(1)}, u32[]{:S(2)}) copy-start(f32[8]{0:T(128)S(1)} %get-tuple-element.84) | copy-start | bytes 100
  34.1 3.6 %copy-start.27 = (f32[8]{0:T(128)}, f32[8]{0:T(128)S(1)}, u32[]{:S(2)}) copy-start(f32[8]{0:T(128)S(1)} %get-tuple-element.85) | copy-start | bytes 100
  34.1 3.6 %copy-start.29 = (f32[8]{0:T(128)}, f32[8]{0:T(128)S(1)}, u32[]{:S(2)}) copy-start(f32[8]{0:T(128)S(1)} %get-tuple-element.86) | copy-start | bytes 100
  34.1 3.6 %copy-start.31 = (f32[8]{0:T(128)}, f32[8]{0:T(128)S(1)}, u32[]{:S(2)}) copy-start(f32[8]{0:T(128)S(1)} %get-tuple-element.87) | copy-start | bytes 100
  54.4 1.2 copy-start.6
  158.5 3.9 %copy-start.41 = (bf16[16,4,24,768]{3,2,1,0:T(8,128)(2,1)S(1)}, bf16[16,4,24,768]{3,2,1,0:T(8,128)(2,1)}, u32[]{:S(2)}) copy-start(bf16[16,4,24,768]{3,2,1,0:T(8,128)(2,1)} %get-tuple-element.7) | copy-start | bytes 7077892
  166.0 4.6 %copy-start.5 = (bf16[2,4,24,768]{3,2,1,0:T(8,128)(2,1)S(1)}, bf16[2,4,24,768]{3,2,1,0:T(8,128)(2,1)}, u32[]{:S(2)}) copy-start(bf16[2,4,24,768]{3,2,1,0:T(8,128)(2,1)} %get-tuple-element.9) | copy-start | bytes 884740
  181.7 5.2 %copy-start.7 = (bf16[16,96,768]{1,2,0:T(8,128)(2,1)S(1)}, bf16[16,96,768]{1,2,0:T(8,128)(2,1)}, u32[]{:S(2)}) copy-start(bf16[16,96,768]{1,2,0:T(8,128)(2,1)} %copy.216) | copy-start | bytes 7077892
  186.9 5.4 %copy-start.2 = (f32[2,96,768]{2,1,0:T(8,128)S(1)}, f32[2,96,768]{2,1,0:T(8,128)}, u32[]{:S(2)}) copy-start(f32[2,96,768]{2,1,0:T(8,128)} %convert.2) | copy-start | bytes 1769476
  186.9 5.4 %copy-start.4 = (bf16[1,4,192,768]{3,2,1,0:T(8,128)(2,1)S(1)}, bf16[1,4,192,768]{3,2,1,0:T(8,128)(2,1)}, u32[]{:S(2)}) copy-start(bf16[1,4,192,768]{3,2,1,0:T(8,128)(2,1)} %get-tuple-element.88) | copy-start | bytes 3538948
  195.3 0.8 copy-start.14
  196.0 5.4 %copy-start.10 = (bf16[64,16,128]{2,1,0:T(8,128)(2,1)S(1)}, bf16[64,16,128]{2,1,0:T(8,128)(2,1)}, u32[]{:S(2)}) copy-start(bf16[64,16,128]{2,1,0:T(8,128)(2,1)} %get-tuple-element.10) | copy-start | bytes 786436
  197.0 13.9 %copy-start.39 = (s32[64]{0:T(128)S(1)}, s32[64]{0:T(128)}, u32[]{:S(2)}) copy-start(s32[64]{0:T(128)} %reshape.752) | copy-start | bytes 772
  197.8 8.3 %all-to-all-start.1 = ((f32[4,1,1536]{2,1,0:T(1,128)}), f32[4,1,1536]{2,1,0:T(1,128)S(1)}, u32[]{:S(2)}, u32[]{:S(2)}) async-start(f32[4,1,1536]{2,1,0:T(1,128)} %reshape.829), calls=%async_computation.1 | async-start | bytes 49152 | tf_op jit(solution)/shard_map/all_to_all | solution.py:644
  201.4 10.4 %copy-start.13 = (f32[8,24]{1,0:T(8,128)S(1)}, f32[8,24]{1,0:T(8,128)}, u32[]{:S(2)}) copy-start(f32[8,24]{1,0:T(8,128)} %param.19) | copy-start | bytes 2308
  201.4 10.4 %copy-start.16 = (f32[8]{0:T(128)S(1)}, f32[8]{0:T(128)}, u32[]{:S(2)}) copy-start(f32[8]{0:T(128)} %copy-done.15) | copy-start | bytes 100
  201.4 10.4 %copy-start.18 = (f32[8]{0:T(128)S(1)}, f32[8]{0:T(128)}, u32[]{:S(2)}) copy-start(f32[8]{0:T(128)} %copy-done.17) | copy-start | bytes 100
  201.4 10.4 %copy-start.20 = (f32[8]{0:T(128)S(1)}, f32[8]{0:T(128)}, u32[]{:S(2)}) copy-start(f32[8]{0:T(128)} %copy-done.19) | copy-start | bytes 100
  201.4 10.4 %copy-start.22 = (f32[8]{0:T(128)S(1)}, f32[8]{0:T(128)}, u32[]{:S(2)}) copy-start(f32[8]{0:T(128)} %copy-done.21) | copy-start | bytes 100
  201.4 10.4 %copy-start.24 = (f32[8]{0:T(128)S(1)}, f32[8]{0:T(128)}, u32[]{:S(2)}) copy-start(f32[8]{0:T(128)} %copy-done.23) | copy-start | bytes 100
  201.4 10.4 %copy-start.26 = (f32[8]{0:T(128)S(1)}, f32[8]{0:T(128)}, u32[]{:S(2)}) copy-start(f32[8]{0:T(128)} %copy-done.25) | copy-start | bytes 100
  201.4 10.4 %copy-start.28 = (f32[8]{0:T(128)S(1)}, f32[8]{0:T(128)}, u32[]{:S(2)}) copy-start(f32[8]{0:T(128)} %copy-done.27) | copy-start | bytes 100
  201.4 10.4 %copy-start.30 = (f32[8]{0:T(128)S(1)}, f32[8]{0:T(128)}, u32[]{:S(2)}) copy-start(f32[8]{0:T(128)} %copy-done.29) | copy-start | bytes 100
  201.4 10.4 %copy-start.32 = (f32[8]{0:T(128)S(1)}, f32[8]{0:T(128)}, u32[]{:S(2)}) copy-start(f32[8]{0:T(128)} %copy-done.31) | copy-start | bytes 100
  201.5 10.4 %copy-start.35 = (f32[24]{0:T(128)S(1)}, f32[24]{0:T(128)}, u32[]{:S(2)}) copy-start(f32[24]{0:T(128)} %copy-done.34) | copy-start | bytes 292
  201.5 10.4 %copy-start.37 = (f32[24]{0:T(128)S(1)}, f32[24]{0:T(128)}, u32[]{:S(2)}) copy-start(f32[24]{0:T(128)} %copy-done.36) | copy-start | bytes 292
  201.5 11.3 %copy-start.40 = (s32[8]{0:T(128)S(1)}, s32[8]{0:T(128)}, u32[]{:S(2)}) copy-start(s32[8]{0:T(128)} %iota_add_fusion) | copy-start | bytes 100
  207.6 28.7 %copy-start.1 = (bf16[1024,768]{1,0:T(8,128)(2,1)S(1)}, bf16[1024,768]{1,0:T(8,128)(2,1)}, u32[]{:S(2)}) copy-start(bf16[1024,768]{1,0:T(8,128)(2,1)} %param.14) | copy-start | bytes 4718596
  207.6 27.4 %copy-start.11 = (f32[12,8]{1,0:T(8,128)S(1)}, f32[12,8]{1,0:T(8,128)}, u32[]{:S(2)}) copy-start(f32[12,8]{1,0:T(8,128)} %copy.267) | copy-start | bytes 1156
Sparse Core Ops, SparseCore 0:
  9.8 41.3 all-gather.1

commit v3 on v2

--- a/solution.py
+++ b/solution.py
@@ -1,3 +1,5 @@
+import functools
+
 import jax
 import jax.numpy as jnp
 from jax import lax
@@ -55,98 +57,127 @@
 
 YS, ZS, CORES = 4, 8, 2
 FIRST = 5
+WIDTHS = (384, 384)
+RELAY = 18
+AHEAD, DELAY = 4.0, 4.0
 MESH = pl.DeviceIdType.MESH
 
 
-def link_plan(images):
-    latency = 1.0
+def link_plan(images, spans):
     split = {"z": (0, FIRST), "y": (FIRST, images)}
-    free = {"y+": 0.0, "y-": 0.0, "z+": 0.0, "z-": 0.0}
-    arrivals = []
-
-    def push(now, link, source, target, span):
-        begin = max(now, free[link])
-        free[link] = begin + (span[1] - span[0])
-        arrivals.append((free[link] + latency, len(arrivals), link, source, target, span))
-
-    def forward(now, dy, dz, span):
+    full = sum(spans)
+    waiting = {"y+": [], "y-": [], "z+": [], "z-": []}
+    free = {link: 0.0 for link in waiting}
+    plan, flight, steps = [], [], []
+
+    def push(now, chunk, link, source, target, span):
+        waiting[link].append((chunk, len(waiting[link]) + 1000 * now, source, target, span))
+
+    def issue(now):
+        for link, queue in waiting.items():
+            while queue and free[link] <= now + AHEAD:
+                entry = min(queue)
+                queue.remove(entry)
+                chunk, _, source, target, span = entry
+                free[link] = max(now, free[link]) + (span[1] - span[0]) * spans[chunk] / full
+                flight.append((free[link] + DELAY, len(plan)))
+                steps.append(("send", len(plan)))
+                plan.append((chunk, link, source, target, span))
+
+    def forward(now, chunk, dy, dz, span):
         if span[1] <= FIRST:
             low, high = split["z"]
             half = (low + high + 1) // 2
             if dy == 0:
                 if dz in (0, 1, 2):
-                    push(now, "z+", (dy, dz), (dy, dz + 1), span)
+                    push(now, chunk, "z+", (dy, dz), (dy, dz + 1), span)
                 if dz == 3:
-                    push(now, "z+", (dy, dz), (dy, 4), (low, half))
+                    push(now, chunk, "z+", (dy, dz), (dy, 4), (low, half))
                 if dz in (0, 7, 6):
-                    push(now, "z-", (dy, dz), (dy, (dz - 1) % ZS), span)
+                    push(now, chunk, "z-", (dy, dz), (dy, (dz - 1) % ZS), span)
                 if dz == 5:
-                    push(now, "z-", (dy, dz), (dy, 4), (half, high))
-                push(now, "y+", (dy, dz), (1, dz), span)
-                push(now, "y-", (dy, dz), (3, dz), span)
+                    push(now, chunk, "z-", (dy, dz), (dy, 4), (half, high))
+                push(now, chunk, "y+", (dy, dz), (1, dz), span)
+                push(now, chunk, "y-", (dy, dz), (3, dz), span)
             if dy == 1 and dz % 2 == 0:
-                push(now, "y+", (dy, dz), (2, dz), span)
+                push(now, chunk, "y+", (dy, dz), (2, dz), span)
             if dy == 3 and dz % 2 == 1:
-                push(now, "y-", (dy, dz), (2, dz), span)
+                push(now, chunk, "y-", (dy, dz), (2, dz), span)
         else:
             low, high = split["y"]
             half = (low + high + 1) // 2
             if dz == 0:
                 if dy == 0:
-                    push(now, "y+", (0, 0), (1, 0), span)
-                    push(now, "y-", (0, 0), (3, 0), span)
+                    push(now, chunk, "y+", (0, 0), (1, 0), span)
+                    push(now, chunk, "y-", (0, 0), (3, 0), span)
                 if dy == 1:
-                    push(now, "y+", (1, 0), (2, 0), (low, half))
+                    push(now, chunk, "y+", (1, 0), (2, 0), (low, half))
                 if dy == 3:
-                    push(now, "y-", (3, 0), (2, 0), (half, high))
+                    push(now, chunk, "y-", (3, 0), (2, 0), (half, high))
             if dz in (0, 1, 2):
-                push(now, "z+", (dy, dz), (dy, dz + 1), span)
+                push(now, chunk, "z+", (dy, dz), (dy, dz + 1), span)
             if dz == 3 and dy < 2:
-                push(now, "z+", (dy, dz), (dy, 4), span)
+                push(now, chunk, "z+", (dy, dz), (dy, 4), span)
             if dz in (0, 7, 6):
-                push(now, "z-", (dy, dz), (dy, (dz - 1) % ZS), span)
+                push(now, chunk, "z-", (dy, dz), (dy, (dz - 1) % ZS), span)
             if dz == 5 and dy >= 2:
-                push(now, "z-", (dy, dz), (dy, 4), span)
-
-    forward(0.0, 0, 0, split["z"])
-    forward(0.0, 0, 0, split["y"])
-    sent = []
-    steps = [("send", list(range(len(arrivals))))]
-    waited = set()
-    while len(waited) < len(arrivals):
-        entry = min(e for e in arrivals if e[1] not in waited)
-        waited.add(entry[1])
-        before = len(arrivals)
-        forward(entry[0], entry[4][0], entry[4][1], entry[5])
-        steps.append(("wait", entry[1]))
-        steps.append(("send", list(range(before, len(arrivals)))))
-    by_number = sorted(arrivals, key=lambda e: e[1])
-    return steps, [e[2:] for e in by_number]
+                push(now, chunk, "z-", (dy, dz), (dy, 4), span)
+
+    for chunk in range(len(spans)):
+        forward(0.0, chunk, 0, 0, split["z"])
+        forward(0.0, chunk, 0, 0, split["y"])
+    issue(0.0)
+    while flight:
+        entry = min(flight)
+        flight.remove(entry)
+        now, number = entry
+        chunk, _, _, target, span = plan[number]
+        steps.append(("wait", number))
+        forward(now, chunk, target[0], target[1], span)
+        issue(now)
+    return steps, plan
 
 
 def exchange_kernel(
     pick_ref,
-    rows_ref,
-    emb_ref,
+    patches_ref,
+    patch_own_ref,
+    enc_proj_ref,
+    enc_out_ref,
+    embed_ref,
     weights_ref,
     pose_ref,
     far_ref,
     own_ref,
     weights_all,
     pose_all,
-    held,
-    staged,
-    ring_send,
-    ring_recv,
-    twin_send,
-    twin_recv,
-    line_send,
-    line_recv,
-    pose_send,
-    pose_recv,
-    local_sem,
+    *scratch,
 ):
-    images = rows_ref.shape[0]
+    chunks = len(WIDTHS)
+    held, scratch = scratch[:chunks], scratch[chunks:]
+    staged, scratch = scratch[:chunks], scratch[chunks:]
+    relay, scratch = scratch[:chunks], scratch[chunks:]
+    (
+        mixed,
+        mixed_all,
+        enc_out_all,
+        emb_ref,
+        enc_send,
+        enc_recv,
+        ring_send,
+        ring_recv,
+        twin_send,
+        twin_recv,
+        line_send,
+        line_recv,
+        pose_send,
+        pose_recv,
+        far_send,
+        far_recv,
+        local_sem,
+    ) = scratch
+    columns = [slice(sum(WIDTHS[:c]), sum(WIDTHS[: c + 1])) for c in range(chunks)]
+    images, share, width = emb_ref.shape
     here = lax.axis_index("img")
     me = lax.axis_index("mp")
     core = lax.rem(here, 2)
@@ -154,12 +185,16 @@
     y = here // (2 * ZS)
     split = far_ref.shape[1]
     per_dev = far_ref.shape[0]
+    half_dev = per_dev // 2
 
     def spot(yy, zz, cc):
         return ((yy * ZS + zz) * 2 + cc, me)
 
     def mate(step):
         return (here, lax.rem(me + step, split))
+
+    def behind(step):
+        return lax.rem(me + split - step, split)
 
     twin = spot(y, z, 1 - core)
     links = {
@@ -182,7 +217,6 @@
     peers += [mate(step) for step in range(1, split)]
     for peer in peers:
         pl.semaphore_signal(barrier, inc=1, device_id=peer, device_id_type=MESH)
-    held[pl.ds(0, images)] = rows_ref[...]
     pose_all[here] = pose_ref[...]
     pl.semaphore_wait(barrier, len(peers))
 
@@ -196,37 +230,34 @@
             device_id_type=MESH,
         )
 
-    steps, plan = link_plan(images)
-
-    def block(side, slot, span):
+    steps, plan = link_plan(images, WIDTHS)
+
+    def block(chunk, side, slot, span):
         first = ((side * YS + slot[0]) * ZS + slot[1]) * images
-        return held.at[pl.ds(first + span[0], span[1] - span[0])]
+        return held[chunk].at[pl.ds(first + span[0], span[1] - span[0])]
 
     def ring(number):
-        link, source, target, span = plan[number]
-        return remote(
-            block(0, source, span),
-            block(0, target, span),
+        chunk, link, source, target, span = plan[number]
+        return remote(
+            block(chunk, 0, source, span),
+            block(chunk, 0, target, span),
             ring_send.at[number],
             ring_recv.at[number],
             links[link],
         )
 
-    twins = [((0, 0), (0, images))] + [(entry[2], entry[3]) for entry in plan]
+    twins = [(entry[0], entry[3], entry[4]) for entry in plan]
+    twins += [(chunk, (0, 0), (0, images)) for chunk in range(chunks)]
 
     def twin_copy(number):
-        slot, span = twins[number]
-        return remote(
-            block(0, slot, span),
-            block(1, slot, span),
+        chunk, slot, span = twins[number]
+        return remote(
+            block(chunk, 0, slot, span),
+            block(chunk, 1, slot, span),
             twin_send.at[number],
             twin_recv.at[number],
             twin,
         )
-
-    for number in steps[0][1]:
-        ring(number).start()
-    twin_copy(0).start()
 
     def pose_line(dz, dc, number, slot):
         return remote(
@@ -260,6 +291,16 @@
             mate(step),
         )
 
+    def weight_relay(step, slot):
+        kind = 2 * core + (0 if step == 1 else 1)
+        return remote(
+            weights_all.at[pl.ds(kind, 1), slot],
+            weights_all.at[pl.ds(kind, 1), slot],
+            line_send.at[3 * split + step],
+            line_recv.at[3 * split + step],
+            mate(step),
+        )
+
     def weight_twin(step, half, slot):
         return remote(
             weights_all.at[pl.ds(2 * half, 2), slot],
@@ -269,18 +310,127 @@
             twin,
         )
 
-    def far_copy(step, slot):
-        return remote(
-            staged.at[pl.ds(per_dev * lax.rem(me + step, split), per_dev)],
-            far_ref.at[:, slot],
-            line_send.at[3 * split + step],
-            line_recv.at[3 * split + step],
+    def far_direct(chunk, step, slot):
+        return remote(
+            staged[chunk].at[pl.ds(per_dev * lax.rem(me + step, split), per_dev)],
+            far_ref.at[:, slot, :, columns[chunk]],
+            far_send.at[chunk, step],
+            far_recv.at[chunk, step],
             mate(step),
         )
+
+    def far_relay(chunk, step):
+        side = 0 if step == 1 else 1
+        return remote(
+            staged[chunk].at[pl.ds(per_dev * lax.rem(me + 2, split) + side * half_dev, half_dev)],
+            relay[chunk].at[side],
+            far_send.at[chunk, split + step],
+            far_recv.at[chunk, split + step],
+            mate(step),
+        )
+
+    def far_onward(chunk, step, slot):
+        side = 0 if step == 1 else 1
+        return remote(
+            relay[chunk].at[side],
+            far_ref.at[pl.ds(side * half_dev, half_dev), slot, :, columns[chunk]],
+            far_send.at[chunk, 2 * split + step],
+            far_recv.at[chunk, 2 * split + step],
+            mate(step),
+        )
+
+    def out_copy(step, slot):
+        return remote(
+            enc_out_ref,
+            enc_out_all.at[slot],
+            enc_send.at[step],
+            enc_recv.at[step],
+            mate(step),
+        )
+
+    def mixed_copy(part, step, slot):
+        span = pl.ds(part * (images // 2), images // 2)
+        return remote(
+            mixed.at[lax.rem(me + step, split), span],
+            mixed_all.at[slot, span],
+            enc_send.at[split * (1 + part) + step],
+            enc_recv.at[split * (1 + part) + step],
+            mate(step),
+        )
+
+    for step in range(1, split):
+        out_copy(step, me).start()
+    enc_out_all[me] = enc_out_ref[...]
+    tokens = share * split
+    local = enc_out_ref.shape[0]
+    last = (((1,), (1,)), ((), ()))
+    first_half = lax.broadcasted_iota(jnp.int32, (1, 128), 1) < HD
+    zero = jnp.zeros((), jnp.bfloat16)
+    ones = jnp.ones((tokens, 128), jnp.bfloat16)
+
+    def encode(pair, carry):
+        span = pl.ds(pl.multiple_of(pair * 2 * tokens, 2 * tokens), 2 * tokens)
+        normed = norm_rows(patches_ref[span, :].astype(jnp.float32))
+        projected = jnp.dot(normed, enc_proj_ref[...], preferred_element_type=jnp.float32)
+        projected = projected.astype(jnp.bfloat16)
+        for image in range(2):
+            lines = slice(image * tokens, (image + 1) * tokens)
+            for first in range(0, local, 128):
+                query = projected[lines, first : first + 128] * jnp.bfloat16(HD ** (-0.5))
+                key = projected[lines, local + first : local + first + 128]
+                value = projected[lines, 2 * local + first : 2 * local + first + 128]
+                both = jnp.concatenate(
+                    [jnp.where(first_half, query, zero), jnp.where(first_half, zero, query)], axis=0
+                )
+                scores = lax.dot_general(both, key, last, preferred_element_type=jnp.float32)
+                expos = jnp.exp(scores - jnp.max(scores, axis=1, keepdims=True))
+                got = jnp.dot(
+                    expos.astype(jnp.bfloat16),
+                    jnp.concatenate([value, ones], axis=1),
+                    preferred_element_type=jnp.float32,
+                )
+                got = got[:, :128] / got[:, 128:]
+                got = jnp.where(first_half, got[:tokens], got[tokens:])
+                for place in range(split):
+                    mixed[place, pair * 2 + image, :, first : first + 128] = got[
+                        place * share : (place + 1) * share
+                    ].astype(jnp.bfloat16)
+        return carry
+
+    lax.fori_loop(0, images // 4, encode, 0)
+    for step in range(1, split):
+        mixed_copy(0, step, me).start()
+    lax.fori_loop(images // 4, images // 2, encode, 0)
+    for step in range(1, split):
+        mixed_copy(1, step, me).start()
+    for step in (1, 3):
+        weight_copy(step, me).start()
+    mixed_all[me] = mixed[me]
+    encoded = patch_own_ref[...].astype(jnp.float32).reshape(images * share, -1)
+    for step in range(split):
+        source = behind(step)
+        if step:
+            out_copy(step, source).wait_recv()
+            mixed_copy(0, step, source).wait_recv()
+            mixed_copy(1, step, source).wait_recv()
+        part = mixed_all[source].astype(jnp.float32).reshape(images * share, local)
+        encoded = encoded + jnp.dot(
+            part.astype(jnp.bfloat16), enc_out_all[source], preferred_element_type=jnp.float32
+        )
+    embedded = jnp.dot(norm_rows(encoded), embed_ref[...], preferred_element_type=jnp.float32)
+    embedded = embedded.astype(jnp.bfloat16).astype(jnp.float32)
+    emb_ref[...] = embedded.reshape(images, share, width).astype(jnp.bfloat16)
+    normed_rows = norm_rows(embedded).astype(jnp.float32).reshape(images, share, width)
+    for chunk in range(chunks):
+        held[chunk][pl.ds(0, images)] = normed_rows[:, :, columns[chunk]].astype(jnp.bfloat16)
+    opening = [kind for kind, _ in steps].index("wait")
+    for _, number in steps[:opening]:
+        ring(number).start()
+    for chunk in range(chunks):
+        twin_copy(len(plan) + chunk).start()
 
     for step in range(1, split):
         own_copy(step, me).start()
-        weight_copy(step, me).start()
     own_local = pltpu.make_async_copy(
         emb_ref.at[pl.ds(pair_images * me, pair_images)], own_ref.at[:, me], local_sem.at[0]
     )
@@ -288,20 +438,33 @@
     weight_local = pltpu.make_async_copy(weights_ref, weights_all.at[:, me], local_sem.at[1])
     weight_local.start()
 
-    def run(part):
-        for kind, what in part:
-            if kind == "wait":
-                ring(what).wait_recv()
-                twin_copy(1 + what).start()
-            else:
-                for number in what:
-                    ring(number).start()
-
-    third = len(steps) // 3
-    run(steps[1:third])
-    for number, (dz, dc) in enumerate(line):
-        source = line_peer(dz, dc, -1)[0]
-        pose_line(dz, dc, number, source).wait_recv()
+    def far_local(chunk):
+        return pltpu.make_async_copy(
+            staged[chunk].at[pl.ds(per_dev * me, per_dev)],
+            far_ref.at[:, me, :, columns[chunk]],
+            local_sem.at[2 + chunk],
+        )
+
+    def choose(chunk):
+        for number, entry in enumerate(twins):
+            if entry[0] == chunk:
+                twin_copy(number).wait_recv()
+
+        def pick(index, carry):
+            staged[chunk][index] = held[chunk][pick_ref[index]]
+            return carry
+
+        lax.fori_loop(0, per_dev * split, pick, 0, unroll=4)
+        for step in (1, 3):
+            far_relay(chunk, step).start()
+        for step in (1, 3):
+            far_direct(chunk, step, me).start()
+        far_local(chunk).start()
+
+    def pass_on(chunk):
+        for step in (1, 3):
+            far_relay(chunk, step).wait_recv()
+            far_onward(chunk, step, behind(step)).start()
 
     def pose_cross(dy, row):
         return remote(
@@ -312,34 +475,54 @@
             y_peer(dy, 1),
         )
 
-    for dy in range(1, YS):
-        pose_cross(dy, y).start()
-    run(steps[third : 2 * third])
-    for step in range(1, split):
-        source = lax.rem(me + split - step, split)
-        weight_copy(step, source).wait_recv()
-        weight_twin(step, core, source).start()
-    run(steps[2 * third :])
-    for number in range(len(twins)):
-        twin_copy(number).wait_recv()
-
-    def pick(index, carry):
-        staged[index] = held[pick_ref[index]]
-        return carry
-
-    lax.fori_loop(0, per_dev * split, pick, 0)
-    for step in (2, 1, 3):
-        far_copy(step, me).start()
-    far_local = pltpu.make_async_copy(
-        staged.at[pl.ds(per_dev * me, per_dev)], far_ref.at[:, me], local_sem.at[2]
-    )
-    far_local.start()
+    def pose_second():
+        for number, (dz, dc) in enumerate(line):
+            pose_line(dz, dc, number, line_peer(dz, dc, -1)[0]).wait_recv()
+        for dy in range(1, YS):
+            pose_cross(dy, y).start()
+
+    def weights_second():
+        for step in (1, 3):
+            weight_copy(step, behind(step)).wait_recv()
+            weight_relay(step, behind(step)).start()
+            weight_twin(step, core, behind(step)).start()
+
+    def weights_third():
+        for step in (1, 3):
+            weight_relay(step, behind(2)).wait_recv()
+        weight_twin(2, core, behind(2)).start()
+
+    waits = [number for kind, number in steps if kind == "wait"]
+    final = {c: max(i for i, n in enumerate(waits) if plan[n][0] == c) for c in range(chunks)}
+    events = {8: pose_second, len(waits) // 4: weights_second, len(waits) // 2: weights_third}
+    later, pending, count = {}, [], 0
+    for kind, number in steps[opening:]:
+        if kind == "send":
+            ring(number).start()
+            continue
+        for action in pending:
+            action()
+        pending = []
+        ring(number).wait_recv()
+        twin_copy(number).start()
+        count += 1
+        if count in events:
+            pending.append(events[count])
+        for chunk in range(chunks):
+            if final[chunk] == count - 1:
+                pending.append(functools.partial(choose, chunk))
+                later[count + RELAY] = chunk
+        if count in later:
+            pending.append(functools.partial(pass_on, later.pop(count)))
+    for action in pending:
+        action()
+    for chunk in later.values():
+        pass_on(chunk)
     for dy in range(1, YS):
         pose_cross(dy, lax.rem(y + YS - dy, YS)).wait_recv()
     for step in range(1, split):
-        source = lax.rem(me + split - step, split)
-        own_copy(step, source).wait_recv()
-        weight_twin(step, 1 - core, source).wait_recv()
+        own_copy(step, behind(step)).wait_recv()
+        weight_twin(step, 1 - core, behind(step)).wait_recv()
     own_local.wait()
     weight_local.wait()
     for number in range(len(plan)):
@@ -351,48 +534,68 @@
     for dy in range(1, YS):
         pose_cross(dy, y).wait_send()
     for step in range(1, split):
+        out_copy(step, me).wait_send()
+        mixed_copy(0, step, me).wait_send()
+        mixed_copy(1, step, me).wait_send()
         own_copy(step, me).wait_send()
+        weight_twin(step, core, behind(step)).wait_send()
+    for step in (1, 3):
         weight_copy(step, me).wait_send()
-        weight_twin(step, core, lax.rem(me + split - step, split)).wait_send()
-    for step in (1, 3, 2):
-        source = lax.rem(me + split - step, split)
-        far_copy(step, source).wait_recv()
-        far_copy(step, me).wait_send()
-    far_local.wait()
-
-
-def exchange(pick, rows, emb, weights, pose, pairs, groups, split):
-    images, share, width = rows.shape
-    count = len(link_plan(images)[1])
+        weight_relay(step, behind(step)).wait_send()
+    for chunk in range(chunks):
+        far_local(chunk).wait()
+        for step in (1, 3):
+            far_relay(chunk, step).wait_send()
+            far_direct(chunk, step, behind(step)).wait_recv()
+            far_direct(chunk, step, me).wait_send()
+            far_onward(chunk, step, behind(2)).wait_recv()
+            far_onward(chunk, step, behind(step)).wait_send()
+
+
+def exchange(pick, patches, patch_own, enc_proj, enc_out, embed, weights, pose, pairs, groups, split):
+    images, share, _ = patch_own.shape
+    width = embed.shape[1]
+    chunks = len(WIDTHS)
+    count = len(link_plan(images, WIDTHS)[1])
     vmem = pl.BlockSpec(memory_space=pltpu.VMEM)
+    per_dev = pairs // split
     return pl.pallas_call(
         exchange_kernel,
         out_shape=(
-            jax.ShapeDtypeStruct((pairs // split, split, share, width), jnp.bfloat16),
+            jax.ShapeDtypeStruct((per_dev, split, share, width), jnp.bfloat16),
             jax.ShapeDtypeStruct((images // split, split, share, width), jnp.bfloat16),
             jax.ShapeDtypeStruct((4, split) + weights.shape[1:], jnp.bfloat16),
             jax.ShapeDtypeStruct((groups,) + pose.shape, jnp.bfloat16),
         ),
-        in_specs=[pl.BlockSpec(memory_space=pltpu.SMEM)] + [vmem] * 4,
+        in_specs=[pl.BlockSpec(memory_space=pltpu.SMEM)] + [vmem] * 7,
         out_specs=(vmem,) * 4,
-        scratch_shapes=[
-            pltpu.VMEM((groups * images, share, width), jnp.bfloat16),
-            pltpu.VMEM((pairs, share, width), jnp.bfloat16),
+        scratch_shapes=[pltpu.VMEM((groups * images, share, w), jnp.bfloat16) for w in WIDTHS]
+        + [pltpu.VMEM((pairs, share, w), jnp.bfloat16) for w in WIDTHS]
+        + [pltpu.VMEM((2, per_dev // 2, share, w), jnp.bfloat16) for w in WIDTHS]
+        + [
+            pltpu.VMEM((split, images, share, enc_out.shape[0]), jnp.bfloat16),
+            pltpu.VMEM((split, images, share, enc_out.shape[0]), jnp.bfloat16),
+            pltpu.VMEM((split,) + enc_out.shape, jnp.bfloat16),
+            pltpu.VMEM((images, share, width), jnp.bfloat16),
+            pltpu.SemaphoreType.DMA((3 * split,)),
+            pltpu.SemaphoreType.DMA((3 * split,)),
             pltpu.SemaphoreType.DMA((count,)),
             pltpu.SemaphoreType.DMA((count,)),
-            pltpu.SemaphoreType.DMA((count + 1,)),
-            pltpu.SemaphoreType.DMA((count + 1,)),
+            pltpu.SemaphoreType.DMA((count + chunks,)),
+            pltpu.SemaphoreType.DMA((count + chunks,)),
             pltpu.SemaphoreType.DMA((4 * split,)),
             pltpu.SemaphoreType.DMA((4 * split,)),
             pltpu.SemaphoreType.DMA((2 * ZS + YS,)),
             pltpu.SemaphoreType.DMA((2 * ZS + YS,)),
-            pltpu.SemaphoreType.DMA((3,)),
+            pltpu.SemaphoreType.DMA((chunks, 3 * split)),
+            pltpu.SemaphoreType.DMA((chunks, 3 * split)),
+            pltpu.SemaphoreType.DMA((2 + chunks,)),
         ],
         compiler_params=pltpu.CompilerParams(
             collective_id=0, has_side_effects=True, vmem_limit_bytes=56 * 2**20
         ),
         name="exchange",
-    )(pick, rows, emb, weights, pose)
+    )(pick, patches, patch_own, enc_proj, enc_out, embed, weights, pose)
 
 
 def reduce_kernel(
@@ -530,6 +733,99 @@
     )(dense)
 
 
+def decode_kernel(far_ref, own_ref, weights_ref, head_ref, out_ref, queries, keys, values, mixed):
+    width = own_ref.shape[1]
+    tokens = out_ref.shape[2]
+    pairs = out_ref.shape[0]
+    blocks = width // 128
+    own_count = own_ref.shape[0] // tokens
+    per_image = pairs // own_count
+    last = (((1,), (1,)), ((), ()))
+    lane = lax.broadcasted_iota(jnp.int32, (1, 128), 1)
+    first_half = lane < HD
+
+    rows = norm_rows(own_ref[...].astype(jnp.float32))
+    projected = lax.dot_general(rows, weights_ref[0], last, preferred_element_type=jnp.float32)
+    projected = projected.astype(jnp.bfloat16) * jnp.bfloat16(HD ** (-0.5))
+    zero = jnp.zeros((), jnp.bfloat16)
+    for image in range(own_count):
+        for block in range(blocks):
+            part = projected[image * tokens : (image + 1) * tokens, block * 128 : (block + 1) * 128]
+            queries[image, block, :tokens] = jnp.where(first_half, part, zero)
+            queries[image, block, tokens:] = jnp.where(first_half, zero, part)
+
+    chunk = 4 * tokens
+
+    def project(step, carry):
+        span = pl.ds(pl.multiple_of(step * chunk, chunk), chunk)
+        part = far_ref[span, :]
+        keys[span, :] = lax.dot_general(
+            part, weights_ref[1], last, preferred_element_type=jnp.float32
+        ).astype(jnp.bfloat16)
+        values[span, :] = lax.dot_general(
+            part, weights_ref[2], last, preferred_element_type=jnp.float32
+        ).astype(jnp.bfloat16)
+        return carry
+
+    lax.fori_loop(0, pairs // 4, project, 0)
+    ones = jnp.ones((tokens, 128), jnp.bfloat16)
+
+    def attend(pair, carry):
+        span = pl.ds(pl.multiple_of(pair * tokens, tokens), tokens)
+        image = pair // per_image
+        for block in range(blocks):
+            columns = slice(block * 128, (block + 1) * 128)
+            scores = lax.dot_general(
+                queries[image, block], keys[span, columns], last, preferred_element_type=jnp.float32
+            )
+            expos = jnp.exp(scores - jnp.max(scores, axis=1, keepdims=True)).astype(jnp.bfloat16)
+            both = jnp.concatenate([values[span, columns], ones], axis=1)
+            got = jnp.dot(expos, both, preferred_element_type=jnp.float32)
+            got = got[:, :128] / got[:, 128:]
+            mixed[span, columns] = jnp.where(first_half, got[:tokens], got[tokens:]).astype(
+                jnp.bfloat16
+            )
+        return carry
+
+    lax.fori_loop(0, pairs, attend, 0)
+
+    def finish(step, carry):
+        span = pl.ds(pl.multiple_of(step * chunk, chunk), chunk)
+        image = step * 4 // per_image
+        own = own_ref[pl.ds(pl.multiple_of(image * tokens, tokens), tokens), :].astype(jnp.float32)
+        settled = jnp.dot(mixed[span, :], weights_ref[3], preferred_element_type=jnp.float32)
+        settled = settled + jnp.concatenate([own] * 4, axis=0)
+        heads = lax.dot_general(
+            head_ref[...], norm_rows(settled), last, preferred_element_type=jnp.float32
+        )
+        for part in range(4):
+            out_ref[step * 4 + part] = heads[:, part * tokens : (part + 1) * tokens]
+        return carry
+
+    lax.fori_loop(0, pairs // 4, finish, 0)
+
+
+def decode(far, own, weights, head_rows, pairs):
+    width = own.shape[1]
+    tokens = far.shape[0] // pairs
+    own_count = own.shape[0] // tokens
+    vmem = pl.BlockSpec(memory_space=pltpu.VMEM)
+    return pl.pallas_call(
+        decode_kernel,
+        out_shape=jax.ShapeDtypeStruct((pairs, head_rows.shape[0], tokens), jnp.float32),
+        in_specs=[vmem] * 4,
+        out_specs=vmem,
+        scratch_shapes=[
+            pltpu.VMEM((own_count, width // 128, 2 * tokens, 128), jnp.bfloat16),
+            pltpu.VMEM(far.shape, jnp.bfloat16),
+            pltpu.VMEM(far.shape, jnp.bfloat16),
+            pltpu.VMEM(far.shape, jnp.bfloat16),
+        ],
+        compiler_params=pltpu.CompilerParams(vmem_limit_bytes=48 * 2**20),
+        name="decode",
+    )(far, own, weights, head_rows)
+
+
 def shards(
     patches,
     encoder_proj,
@@ -546,14 +842,11 @@
     images, tokens, model_width = patches.shape
     dec_width = decoder_embed.shape[1]
     enc_local = encoder_proj.shape[2]
-    dec_local = decoder_proj.shape[2]
-    head_scale = HD ** (-0.5)
     split = lax.axis_size("mp")
     place = lax.axis_index("mp")
     own_count = images // split
     flat_partner = partners.reshape(-1)
     pair_count = flat_partner.shape[0]
-    out_full = lax.all_gather(encoder_out, "mp", axis=0, tiled=True)
     groups = lax.axis_size("img")
     here = lax.axis_index("img")
     weights = jnp.concatenate([jnp.transpose(decoder_proj, (1, 2, 0)), decoder_out[None]], axis=0)
@@ -561,86 +854,36 @@
         camera_poses.astype(jnp.bfloat16), ((0, 4), (0, 128 - camera_poses.shape[1]))
     )
 
-    normed = norm_rows(patches.astype(jnp.float32))
-    projected = jnp.dot(
-        normed, encoder_proj.reshape(model_width, 3 * enc_local), preferred_element_type=jnp.float32
-    )
-    projected = projected.astype(jnp.bfloat16).reshape(images, tokens, 3, enc_local // HD, HD)
-    scores = (
-        jnp.einsum(
-            "aqhd,athd->ahqt",
-            projected[:, :, 0],
-            projected[:, :, 1],
-            preferred_element_type=jnp.float32,
-        )
-        * head_scale
-    )
-    mixed_rows = jnp.einsum(
-        "ahqt,athd->aqhd",
-        soft_weights(scores),
-        projected[:, :, 2],
-        preferred_element_type=jnp.float32,
-    )
-    mixed_rows = mixed_rows.astype(jnp.bfloat16).reshape(images, tokens, enc_local)
     token_share = tokens // split
     first_token = place * token_share
-    mixed_own = lax.all_to_all(mixed_rows, "mp", split_axis=1, concat_axis=2, tiled=True)
     patch_own = lax.dynamic_slice_in_dim(patches, first_token, token_share, 1)
-    encoded = patch_own.astype(jnp.float32) + jnp.dot(
-        mixed_own, out_full, preferred_element_type=jnp.float32
-    )
-    emb_share = jnp.dot(
-        norm_rows(encoded), decoder_embed, preferred_element_type=jnp.float32
-    ).astype(jnp.bfloat16)
-    rows_share = norm_rows(emb_share.astype(jnp.float32))
     owner = flat_partner // images
     shift_y = (here // (2 * ZS) - owner // (2 * ZS)) % YS
     shift_z = ((here // 2) % ZS - (owner // 2) % ZS) % ZS
     shift_core = (here - owner) % 2
     pick = ((shift_core * YS + shift_y) * ZS + shift_z) * images + flat_partner % images
     far_rows, own_rows, weights_full, pose_tiles = exchange(
-        pick, rows_share, emb_share, weights, pose_tile, pair_count, groups, split
+        pick,
+        patches.reshape(images * tokens, model_width),
+        patch_own,
+        encoder_proj.reshape(model_width, 3 * enc_local),
+        encoder_out,
+        decoder_embed,
+        weights,
+        pose_tile,
+        pair_count,
+        groups,
+        split,
     )
-    far_rows = far_rows.reshape(pair_count // split, tokens, dec_width)
-    embedded = own_rows.reshape(own_count, tokens, dec_width)
-    rows = norm_rows(embedded.astype(jnp.float32))
-    proj_full = weights_full.reshape(4, dec_width, dec_width)
-    dec_out_full = proj_full[3]
-    own_pairs = pair_count // split
-
-    def project(values, which):
-        return lax.dot_general(
-            values,
-            proj_full[which],
-            (((2,), (1,)), ((), ())),
-            preferred_element_type=jnp.float32,
-        ).astype(jnp.bfloat16)
-
-    heads = dec_width // HD
-    queries = project(rows, 0).reshape(own_count, tokens, heads, HD)
-    far_keys = project(far_rows, 1).reshape(own_count, K, tokens, heads, HD)
-    far_values = project(far_rows, 2).reshape(own_count, K, tokens, heads, HD)
-    cross_scores = (
-        jnp.einsum("aqhd,akthd->akhqt", queries, far_keys, preferred_element_type=jnp.float32)
-        * head_scale
+    head_rows = jnp.pad(head_weight.T, ((0, 12), (0, 0)))
+    head_own = decode(
+        far_rows.reshape(pair_count // split * tokens, dec_width),
+        own_rows.reshape(own_count * tokens, dec_width),
+        weights_full.reshape(4, dec_width, dec_width),
+        head_rows,
+        pair_count // split,
     )
-    cross_rows = jnp.einsum(
-        "akhqt,akthd->akqhd",
-        soft_weights(cross_scores),
-        far_values,
-        preferred_element_type=jnp.float32,
-    )
-    cross_rows = cross_rows.astype(jnp.bfloat16).reshape(own_count, K, tokens, dec_width)
-    settled = (
-        jnp.dot(cross_rows, dec_out_full, preferred_element_type=jnp.float32)
-        + embedded.astype(jnp.float32)[:, None]
-    )
-    head_own = lax.dot_general(
-        head_weight,
-        norm_rows(settled).reshape(own_pairs, tokens, dec_width),
-        (((0,), (2,)), ((), ())),
-        preferred_element_type=jnp.float32,
-    )
+    head_own = head_own[:, :4].transpose(1, 0, 2)
     moved = lax.all_to_all(head_own, "mp", split_axis=2, concat_axis=1, tiled=True)
     points = moved[:3]
     confidence = 1.0 + jnp.exp(moved[3])

time: 244 us -> 210 us (0.86)
  Pallas kernels: 120 us -> 177 us
  matrix products: 30.7 us -> 0.44 us
  other arithmetic: 22.1 us -> 6.15 us
  local copies, waits for them, and re-layouts: 35.9 us -> 20.4 us
  between operations: 14.9 us -> 1.02 us
  waiting for transfers between devices: 11.2 us -> 0.01 us
  starting transfers between devices: 8.46 us -> 4.14 us
    pallas_call x1 -> x2, Pallas kernels: 100 us -> 158 us  [the longest x1 129 us: exchange(): pl.pallas_call(exchange_kernel, out_shape=(jax.ShapeDtypeStruct((per_dev,...]
    dot_general x11 -> x0, matrix products: 27.1 us -> none  [the longest x3 9.25 us: project(): lax.dot_general(values, proj_full[which], (((2,), (1,)), ((), ())), prefe...]
    convert_element_type x4 -> x0, local copies, waits for them, and re-layouts: 10.6 us -> none  [the longest x3 8.1 us: project(): return lax.dot_general(values, proj_full[which], (((2,), (1,)), ((), ()))...]
    all_gather x1 -> x0, waiting for transfers between devices: 7.12 us -> none  [shards(): out_full = lax.all_gather(encoder_out, 'mp', axis=0, tiled=True)]
    sub x1 -> x0, other arithmetic: 5.16 us -> none  [soft_weights(): expos = jnp.exp(scores - top_score)]
    all_to_all x1 -> x0, starting transfers between devices: 4.84 us -> none  [shards(): lax.all_to_all(mixed_rows, 'mp', split_axis=1, concat_axis=2, tiled=True)]
    slice x1 -> x0, local copies, waits for them, and re-layouts: 3.92 us -> none  [shards(): dec_out_full = proj_full[3]]
    convert_element_type x4 -> x0, other arithmetic: 3.66 us -> none  [the longest x3 1.84 us: norm_rows(): return (centred * lax.rsqrt(variance + epsilon)).astype(jnp.bfloat16)]
  transfers between devices with their start and end apart: 3 -> 1, of which waited for: 2 -> 0; matrix products, arithmetic and copies ran while one was open for 13% -> 2% of each run, Pallas kernels for 0% -> 0%
where the time goes in v3:
time: 210 us; the launch traced here: 209 us
  Pallas kernels  177 us (84%)
  local copies, waits for them, and re-layouts  20.4 us (10%)
  other arithmetic  6.15 us (3%)
  starting transfers between devices  4.14 us (2%)
    pallas_call x1, Pallas kernels, exchange(): pl.pallas_call(exchange_kernel, out_shape=(jax.ShapeDtypeStruct((per_dev,...  129 us
    pallas_call x1, Pallas kernels, decode(): pl.pallas_call(decode_kernel, out_shape=jax.ShapeDtypeStruct((pairs, head...  28.7 us
    pallas_call x1, Pallas kernels, reduce_poses(): pl.pallas_call(reduce_kernel, out_shape=jax.ShapeDtypeStruct(tile, jnp.fl...  19 us
    unnamed x26, local copies, waits for them, and re-layouts  6.17 us
  transfers between devices with their start and end apart: 1, of which 0 were waited for; matrix products, arithmetic and copies ran while one was open for 2% of the time, Pallas kernels for 0%

profile of v3, /device:TPU:1, one launch (start us, length us, event | category | flops | bytes accessed | tf_op | source)
XLA Modules:
  0.0 209.3 jit_solution(5338336654291427929)
XLA Ops:
  0.7 0.8 reshape.646
  1.4 1.7 copy.141
  3.2 1.6 copy.143.enc_proj_ref
  4.8 0.1 copy.142
  4.9 0.6 pad.84.pose_ref
  5.6 1.8 constant_dynamic-slice_fusion.patch_own_ref
  7.4 1.2 pad_maximum_fusion.weights_ref
  8.6 0.5 fusion.29.pick_ref
  9.1 129.5 %exchange.1 = (bf16[16,4,24,768]{3,2,1,0:T(8,128)(2,1)}, bf16[2,4,24,768]{3,2,1,0:T(8,128)(2,1)}, bf16[4,4,192,768]{3,2,1,0:T(8,128)(2,1)}, bf16[64,16,128]{2,1,0:T(8,128)(2,1)}) custom-call(s32[64]{0:T(128)} %fusion.29.pick_ref, bf16[768,1024]{1,0:T(8,128)(2,1)} %bitcast.51, bf16[8,24,1024]{2,1,0:T(8,128)(2,1)} %constant_dynamic-slice_fusion.patch_own_ref, ...), custom_call_target="tpu_custom_call" | custom-call | tf_op jit(solution)/shard_map/exchange/pallas_call | solution.py:562
  138.6 1.7 copy-done
  140.3 1.0 copy-done.1
  141.2 28.7 %decode.1 = f32[16,16,96]{2,1,0:T(8,128)S(1)} custom-call(bf16[1536,768]{1,0:T(8,128)(2,1)S(1)} %bitcast.47, bf16[192,768]{1,0:T(8,128)(2,1)S(1)} %bitcast.48, bf16[4,768,768]{2,1,0:T(8,128)(2,1)} %bitcast.50, bf16[16,768]{1,0:T(8,128)(2,1)S(1)} %pad.85.head_ref), custom_call_target="tpu_custom_call" | custom-call | tf_op jit(solution)/shard_map/decode/pallas_call | solution.py:813
  170.0 0.1 copy.144
  170.1 0.8 reshape.709
  170.9 4.1 %all-to-all-start = ((f32[4,1,1536]{2,1,0:T(1,128)}), f32[4,1,1536]{2,1,0:T(1,128)S(1)}, u32[]{:S(2)}, u32[]{:S(2)}) async-start(f32[4,1,1536]{2,1,0:T(1,128)} %reshape.709), calls=%async_computation | async-start | bytes 49152 | tf_op jit(solution)/shard_map/all_to_all | solution.py:887
  175.1 0.4 slice_reduce_fusion.23
  175.5 0.5 copy.192
  176.0 0.6 gather_fusion
  176.7 0.4 slice_reduce_fusion.11
  177.1 0.1 multiply_add_fusion.4
  179.1 0.1 copy.189
  179.2 0.1 copy.166
  179.3 0.1 copy.167
  179.4 0.1 copy.168
  179.8 0.1 copy.178
  179.9 0.1 copy.157
  180.0 0.1 copy.158
  180.3 0.5 broadcast.597
  180.8 0.7 reduce.85
  181.5 0.2 reshape.710
  181.7 0.1 copy.191
  181.9 0.2 multiply_add_fusion
  182.1 0.4 multiply_reduce_fusion.8
  184.8 0.2 fusion
  185.0 0.1 reduce_sum.280
  185.2 0.1 reduce_sum.288
  185.3 0.1 reduce_sum.296
  185.4 0.1 add_reduce_fusion.1
  185.5 0.2 add_reduce_fusion.2
  185.7 0.9 multiply_reduce_fusion.16
  186.6 0.2 convolution_add_fusion
  186.8 0.2 reshape.655
  187.1 0.1 copy.187
  187.3 0.7 pad.110.clone
  188.0 19.0 %reduce_poses.1 = f32[8,128]{1,0:T(8,128)} custom-call(f32[4,16,8,128]{3,2,1,0:T(8,128)} %bitcast.56), custom_call_target="tpu_custom_call" | custom-call | tf_op jit(solution)/shard_map/reduce_poses/pallas_call | solution.py:713
  207.0 0.7 multiply_reduce_fusion.15
  207.8 0.7 copy.190
  208.6 0.6 pad_maximum_fusion.1
  (107 shorter events, 5.2 us)
Async XLA Ops:
  3.2 1.7 copy-start.3
  3.2 2.4 %copy-start.8 = (bf16[768,4]{0,1:T(4,128)(2,1)S(1)}, bf16[768,4]{0,1:T(4,128)(2,1)}, u32[]{:S(2)}) copy-start(bf16[768,4]{0,1:T(4,128)(2,1)} %param.17) | copy-start | bytes 18436
  3.2 4.2 %copy-start.2 = (bf16[768,3,192]{0,2,1:T(8,128)(2,1)S(1)}, bf16[768,3,192]{0,2,1:T(8,128)(2,1)}, u32[]{:S(2)}) copy-start(bf16[768,3,192]{0,2,1:T(8,128)(2,1)} %param.15) | copy-start | bytes 2654212
  3.2 4.2 %copy-start.4 = (bf16[192,768]{1,0:T(8,128)(2,1)S(1)}, bf16[192,768]{1,0:T(8,128)(2,1)}, u32[]{:S(2)}) copy-start(bf16[192,768]{1,0:T(8,128)(2,1)} %param.16) | copy-start | bytes 884740
  138.6 1.7 copy-start
  140.3 1.0 copy-start.1
  141.2 33.8 %copy-start.6 = (s32[8,8]{1,0:T(8,128)S(1)}, s32[8,8]{1,0:T(8,128)}, u32[]{:S(2)}) copy-start(s32[8,8]{1,0:T(8,128)} %param.18) | copy-start | bytes 772
  141.2 34.3 %copy-start.5 = (bf16[64,16,128]{2,1,0:T(8,128)(2,1)S(1)}, bf16[64,16,128]{2,1,0:T(8,128)(2,1)}, u32[]{:S(2)}) copy-start(bf16[64,16,128]{2,1,0:T(8,128)(2,1)} %get-tuple-element.10) | copy-start | bytes 786436
  169.9 7.2 %copy-start.7 = (f32[8,24]{1,0:T(8,128)S(1)}, f32[8,24]{1,0:T(8,128)}, u32[]{:S(2)}) copy-start(f32[8,24]{1,0:T(8,128)} %param.19) | copy-start | bytes 2308
  169.9 10.0 %copy-start.9 = (s32[8,24]{1,0:T(8,128)S(1)}, s32[8,24]{1,0:T(8,128)}, u32[]{:S(2)}) copy-start(s32[8,24]{1,0:T(8,128)} %param.21) | copy-start | bytes 2308
  170.9 9.4 %all-to-all-start = ((f32[4,1,1536]{2,1,0:T(1,128)}), f32[4,1,1536]{2,1,0:T(1,128)S(1)}, u32[]{:S(2)}, u32[]{:S(2)}) async-start(f32[4,1,1536]{2,1,0:T(1,128)} %reshape.709), calls=%async_computation | async-start | bytes 49152 | tf_op jit(solution)/shard_map/all_to_all | solution.py:887

commit v4 on v3

--- a/solution.py
+++ b/solution.py
@@ -21,38 +21,6 @@
     centred = values - average
     variance = jnp.mean(centred * centred, axis=-1, keepdims=True)
     return (centred * lax.rsqrt(variance + epsilon)).astype(jnp.bfloat16)
-
-
-def soft_weights(scores):
-    top_score = jnp.max(scores, axis=-1, keepdims=True)
-    expos = jnp.exp(scores - top_score)
-    return (expos / jnp.sum(expos, axis=-1, keepdims=True)).astype(jnp.bfloat16)
-
-
-def make_rays(token_index, rows_total):
-    column = (token_index % 16).astype(jnp.float32)
-    row_pos = (token_index // 16).astype(jnp.float32)
-    return jnp.stack(
-        [(column - 7.5) * 0.125, (row_pos - (rows_total - 1) * 0.5) * 0.125, jnp.ones_like(column)]
-    )
-
-
-def align_loss(depth_map, pose_own, pose_far, points, confidence, weight, ray_dirs, loss_scale):
-    summed = 0.0
-    for component in range(3):
-        world_pts = pose_own[4 * component + 3][:, None] + depth_map * (
-            pose_own[4 * component][:, None] * ray_dirs[0]
-            + pose_own[4 * component + 1][:, None] * ray_dirs[1]
-            + pose_own[4 * component + 2][:, None] * ray_dirs[2]
-        )
-        predicted = pose_far[4 * component + 3][:, :, None] + (
-            pose_far[4 * component][:, :, None] * points[0]
-            + pose_far[4 * component + 1][:, :, None] * points[1]
-            + pose_far[4 * component + 2][:, :, None] * points[2]
-        )
-        residual = world_pts[:, None, :] - predicted
-        summed = summed + jnp.sum(weight[:, None, :] * confidence * residual * residual)
-    return summed * loss_scale
 
 
 YS, ZS, CORES = 4, 8, 2
@@ -598,36 +566,62 @@
     )(pick, patches, patch_own, enc_proj, enc_out, embed, weights, pose)
 
 
-def reduce_kernel(
-    grad_ref, total_ref, across, summed, lined, part, crossed, x_send, x_recv, l_send, l_recv, c_send, c_recv
+def decode_kernel(
+    far_ref,
+    own_ref,
+    weights_ref,
+    head_ref,
+    depth_ref,
+    pose_own_ref,
+    pose_far_ref,
+    partner_ref,
+    result_ref,
+    total_ref,
+    queries,
+    keys,
+    values,
+    mixed,
+    heads_all,
+    depth_all,
+    staging,
+    dense,
+    plane_in,
+    part_sum,
+    line_in,
+    x_send,
+    x_recv,
+    plane_send,
+    plane_recv,
+    line_send,
+    line_recv,
 ):
+    width = own_ref.shape[1]
+    pairs, _, tokens = heads_all.shape
+    split = depth_all.shape[0]
+    share = tokens // split
     here = lax.axis_index("img")
     me = lax.axis_index("mp")
-    core = lax.rem(here, 2)
-    z = lax.rem(here // 2, ZS)
-    y = here // (2 * ZS)
-    split = across.shape[0]
-    row = z * 2 + core
-    rows = 2 * ZS
+    rows_count = 2 * ZS
+    row = lax.rem(here, rows_count)
+    y = here // rows_count
+    plane = [(dx, dy) for dx in range(split) for dy in range(YS) if dx or dy]
     line = [(dz, dc) for dz in range(ZS) for dc in range(CORES) if dz or dc]
 
+    def plane_peer(dx, dy, sign):
+        return (
+            lax.rem(y + YS + sign * dy, YS) * rows_count + row,
+            lax.rem(me + split + sign * dx, split),
+        )
+
     def line_row(dz, dc, sign):
-        return lax.rem(z + ZS + sign * dz, ZS) * 2 + lax.rem(core + dc, 2)
+        z = lax.rem(row // 2 + ZS + sign * dz, ZS)
+        return z * 2 + lax.rem(lax.rem(row, 2) + dc, 2)
 
     def mate(step):
         return (here, lax.rem(me + step, split))
 
-    barrier = pltpu.get_barrier_semaphore()
-    for step in range(1, split):
-        pl.semaphore_signal(barrier, inc=1, device_id=mate(step), device_id_type=MESH)
-    for dz, dc in line:
-        pl.semaphore_signal(
-            barrier, inc=1, device_id=(y * rows + line_row(dz, dc, 1), me), device_id_type=MESH
-        )
-    for other in range(YS):
-        pl.semaphore_signal(barrier, inc=1, device_id=(other * rows + row, y), device_id_type=MESH)
-
-    pl.semaphore_wait(barrier, split - 1 + len(line) + YS)
+    def behind(step):
+        return lax.rem(me + split - step, split)
 
     def remote(source, target, send, recv, device):
         return pltpu.make_async_remote_copy(
@@ -639,104 +633,15 @@
             device_id_type=MESH,
         )
 
-    def x_copy(step, slot):
-        return remote(
-            grad_ref.at[lax.rem(me + step, split)],
-            across.at[slot],
-            x_send.at[step],
-            x_recv.at[step],
-            mate(step),
-        )
-
-    for step in range(1, split):
-        x_copy(step, me).start()
-    across[me] = grad_ref[me]
-    for step in range(1, split):
-        x_copy(step, lax.rem(me + split - step, split)).wait_recv()
-    summed[...] = jnp.sum(across[...], axis=0)
-
-    def l_copy(number, dz, dc, slot):
-        target = line_row(dz, dc, 1)
-        return remote(
-            summed.at[target],
-            lined.at[slot],
-            l_send.at[number],
-            l_recv.at[number],
-            (y * rows + target, me),
-        )
-
-    for number, (dz, dc) in enumerate(line):
-        l_copy(number, dz, dc, row).start()
-    lined[row] = summed[row]
-    for number, (dz, dc) in enumerate(line):
-        l_copy(number, dz, dc, line_row(dz, dc, -1)).wait_recv()
-    part[...] = jnp.sum(lined[...], axis=0)
-
-    def c_copy(other, slot):
-        return remote(
-            part, crossed.at[slot], c_send.at[other], c_recv.at[slot], (me * rows + row, other)
-        )
-
-    for other in range(split):
-
-        @pl.when(jnp.logical_or(y != me, me != other))
-        def _():
-            c_copy(other, y).start()
-
-    @pl.when(y == me)
-    def _():
-        crossed[y] = part[...]
-
-    for other in range(YS):
-
-        @pl.when(jnp.logical_or(y != me, y != other))
-        def _():
-            c_copy(0, other).wait_recv()
-
-    total_ref[...] = jnp.sum(crossed[...], axis=0)
-    for step in range(1, split):
-        x_copy(step, me).wait_send()
-    for number, (dz, dc) in enumerate(line):
-        l_copy(number, dz, dc, row).wait_send()
-    for other in range(split):
-
-        @pl.when(jnp.logical_or(y != me, me != other))
-        def _():
-            c_copy(other, y).wait_send()
-
-
-def reduce_poses(dense, split):
-    groups = dense.shape[0] * dense.shape[1]
-    tile = dense.shape[2:]
-    vmem = pl.BlockSpec(memory_space=pltpu.VMEM)
-    rows = 2 * ZS
-    return pl.pallas_call(
-        reduce_kernel,
-        out_shape=jax.ShapeDtypeStruct(tile, jnp.float32),
-        in_specs=[vmem],
-        out_specs=vmem,
-        scratch_shapes=[
-            pltpu.VMEM((split, rows) + tile, jnp.float32),
-            pltpu.VMEM((rows,) + tile, jnp.float32),
-            pltpu.VMEM((rows,) + tile, jnp.float32),
-            pltpu.VMEM(tile, jnp.float32),
-            pltpu.VMEM((YS,) + tile, jnp.float32),
-            pltpu.SemaphoreType.DMA((split,)),
-            pltpu.SemaphoreType.DMA((split,)),
-            pltpu.SemaphoreType.DMA((rows,)),
-            pltpu.SemaphoreType.DMA((rows,)),
-            pltpu.SemaphoreType.DMA((split,)),
-            pltpu.SemaphoreType.DMA((YS,)),
-        ],
-        compiler_params=pltpu.CompilerParams(collective_id=1, has_side_effects=True),
-        name="reduce_poses",
-    )(dense)
-
-
-def decode_kernel(far_ref, own_ref, weights_ref, head_ref, out_ref, queries, keys, values, mixed):
-    width = own_ref.shape[1]
-    tokens = out_ref.shape[2]
-    pairs = out_ref.shape[0]
+    barrier = pltpu.get_barrier_semaphore()
+    for dx, dy in plane:
+        pl.semaphore_signal(
+            barrier, inc=1, device_id=plane_peer(dx, dy, 1), device_id_type=MESH
+        )
+    for dz, dc in line:
+        pl.semaphore_signal(
+            barrier, inc=1, device_id=(y * rows_count + line_row(dz, dc, 1), me), device_id_type=MESH
+        )
     blocks = width // 128
     own_count = own_ref.shape[0] // tokens
     per_image = pairs // own_count
@@ -768,6 +673,21 @@
         return carry
 
     lax.fori_loop(0, pairs // 4, project, 0)
+    pl.semaphore_wait(barrier, len(plane) + len(line))
+
+    def depth_copy(step, slot):
+        return remote(
+            depth_ref.at[lax.rem(me + step, split)],
+            depth_all.at[slot],
+            x_send.at[step],
+            x_recv.at[step],
+            mate(step),
+        )
+
+    for step in range(1, split):
+        depth_copy(step, me).start()
+    depth_all[me] = depth_ref[me]
+    staging[...] = jnp.zeros_like(staging)
     ones = jnp.ones((tokens, 128), jnp.bfloat16)
 
     def attend(pair, carry):
@@ -799,31 +719,185 @@
             head_ref[...], norm_rows(settled), last, preferred_element_type=jnp.float32
         )
         for part in range(4):
-            out_ref[step * 4 + part] = heads[:, part * tokens : (part + 1) * tokens]
+            heads_all[step * 4 + part] = heads[:, part * tokens : (part + 1) * tokens]
         return carry
 
     lax.fori_loop(0, pairs // 4, finish, 0)
-
-
-def decode(far, own, weights, head_rows, pairs):
+    for step in range(1, split):
+        depth_copy(step, behind(step)).wait_recv()
+
+    def widen(offset):
+        both = jnp.concatenate(
+            [depth_all[q, offset : offset + own_count, :share] for q in range(split)], axis=1
+        )
+        return jnp.concatenate(
+            [
+                jnp.broadcast_to(both[image : image + 1], (per_image, tokens))
+                for image in range(own_count)
+            ],
+            axis=0,
+        )
+
+    depth = widen(0)
+    valid = widen(own_count)
+    token = lax.broadcasted_iota(jnp.int32, (1, tokens), 1)
+    ray_x = (lax.rem(token, 16).astype(jnp.float32) - 7.5) * 0.125
+    ray_y = (lax.div(token, 16).astype(jnp.float32) - (tokens // 16 - 1) * 0.5) * 0.125
+    rays = [ray_x, ray_y, jnp.ones_like(ray_x)]
+    points = [heads_all[:, component, :] for component in range(3)]
+    confidence = 1.0 + jnp.exp(heads_all[:, 3, :])
+    weight = valid * confidence * (2.0 / tokens)
+    own_pose, far_pose = pose_own_ref[...], pose_far_ref[...]
+    lane128 = lax.broadcasted_iota(jnp.int32, (pairs, 128), 1)
+    own_grad = jnp.zeros((pairs, 128), jnp.float32)
+    far_grad = jnp.zeros((pairs, 128), jnp.float32)
+    depth_grad = jnp.zeros((pairs, tokens), jnp.float32)
+    for component in range(3):
+        base = 4 * component
+        direction = sum(own_pose[:, base + k : base + k + 1] * rays[k] for k in range(3))
+        world = own_pose[:, base + 3 : base + 4] + depth * direction
+        predicted = far_pose[:, base + 3 : base + 4] + sum(
+            far_pose[:, base + k : base + k + 1] * points[k] for k in range(3)
+        )
+        slope = weight * (world - predicted)
+        depth_grad = depth_grad + slope * direction
+        scaled = slope * depth
+        for k in range(4):
+            mine = scaled * rays[k] if k < 3 else slope
+            other = slope * points[k] if k < 3 else slope
+            mine = jnp.sum(mine, axis=1, keepdims=True)
+            other = jnp.sum(other, axis=1, keepdims=True)
+            own_grad = jnp.where(lane128 == base + k, mine, own_grad)
+            far_grad = jnp.where(lane128 == base + k, -other, far_grad)
+    total_images = YS * 128
+    ids = lax.broadcasted_iota(jnp.int32, (pairs, total_images), 1)
+    pair_ids = lax.broadcasted_iota(jnp.int32, (pairs, total_images), 0)
+    own_ids = (here * split + me) * own_count + lax.div(pair_ids, per_image)
+    hits = jnp.concatenate([ids == own_ids, ids == partner_ref[:, :1]], axis=0)
+    table = lax.dot_general(
+        jnp.concatenate([own_grad, far_grad], axis=0),
+        hits.astype(jnp.float32),
+        (((0,), (0,)), ((), ())),
+        precision=lax.Precision.HIGHEST,
+        preferred_element_type=jnp.float32,
+    )
+    for part in range(YS):
+        dense[part] = table[:16, part * 128 : (part + 1) * 128]
+
+    def plane_copy(number, dx, dy, slot):
+        return remote(
+            dense.at[lax.rem(y + dy, YS)],
+            plane_in.at[slot],
+            plane_send.at[number],
+            plane_recv.at[number],
+            plane_peer(dx, dy, 1),
+        )
+
+    for number, (dx, dy) in enumerate(plane):
+        plane_copy(number, dx, dy, me * YS + y).start()
+    plane_in[me * YS + y] = dense[y]
+
+    old = jnp.concatenate(
+        [depth[image * per_image : image * per_image + 1] for image in range(own_count)], axis=0
+    )
+    change = jnp.concatenate(
+        [
+            jnp.sum(
+                depth_grad[image * per_image : (image + 1) * per_image], axis=0, keepdims=True
+            )
+            for image in range(own_count)
+        ],
+        axis=0,
+    )
+    moved = old - depth_step * change
+    for place in range(split):
+        span = slice(place * share, (place + 1) * share)
+        for component, values_now in enumerate(points + [confidence]):
+            staging[place, component * pairs : (component + 1) * pairs, :share] = values_now[:, span]
+        staging[place, 4 * pairs : 4 * pairs + own_count, :share] = moved[:, span]
+
+    def result_copy(step, slot):
+        return remote(
+            staging.at[lax.rem(me + step, split)],
+            result_ref.at[slot],
+            x_send.at[split + step],
+            x_recv.at[split + step],
+            mate(step),
+        )
+
+    for step in range(1, split):
+        result_copy(step, me).start()
+    result_ref[me] = staging[me]
+    for number, (dx, dy) in enumerate(plane):
+        source = lax.rem(me + split - dx, split) * YS + lax.rem(y + YS - dy, YS)
+        plane_copy(number, dx, dy, source).wait_recv()
+    gathered = jnp.sum(plane_in[...], axis=0)
+    part_sum[...] = gathered
+    line_in[row] = gathered
+
+    def line_copy(number, dz, dc, slot):
+        return remote(
+            part_sum,
+            line_in.at[slot],
+            line_send.at[number],
+            line_recv.at[number],
+            (y * rows_count + line_row(dz, dc, 1), me),
+        )
+
+    for number, (dz, dc) in enumerate(line):
+        line_copy(number, dz, dc, row).start()
+    for number, (dz, dc) in enumerate(line):
+        line_copy(number, dz, dc, line_row(dz, dc, -1)).wait_recv()
+    total_ref[...] = jnp.sum(line_in[...], axis=0)
+    for step in range(1, split):
+        depth_copy(step, me).wait_send()
+        result_copy(step, behind(step)).wait_recv()
+        result_copy(step, me).wait_send()
+    for number, (dx, dy) in enumerate(plane):
+        plane_copy(number, dx, dy, me * YS + y).wait_send()
+    for number, (dz, dc) in enumerate(line):
+        line_copy(number, dz, dc, row).wait_send()
+
+
+def decode(far, own, weights, head_rows, depth_tiles, pose_own, pose_far, partner_tile, pairs):
     width = own.shape[1]
     tokens = far.shape[0] // pairs
     own_count = own.shape[0] // tokens
+    split = depth_tiles.shape[0]
     vmem = pl.BlockSpec(memory_space=pltpu.VMEM)
+    result_rows = 4 * pairs + 8
     return pl.pallas_call(
         decode_kernel,
-        out_shape=jax.ShapeDtypeStruct((pairs, head_rows.shape[0], tokens), jnp.float32),
-        in_specs=[vmem] * 4,
-        out_specs=vmem,
+        out_shape=(
+            jax.ShapeDtypeStruct((split, result_rows, 128), jnp.float32),
+            jax.ShapeDtypeStruct((16, 128), jnp.float32),
+        ),
+        in_specs=[vmem] * 8,
+        out_specs=(vmem, vmem),
         scratch_shapes=[
             pltpu.VMEM((own_count, width // 128, 2 * tokens, 128), jnp.bfloat16),
             pltpu.VMEM(far.shape, jnp.bfloat16),
             pltpu.VMEM(far.shape, jnp.bfloat16),
             pltpu.VMEM(far.shape, jnp.bfloat16),
+            pltpu.VMEM((pairs, head_rows.shape[0], tokens), jnp.float32),
+            pltpu.VMEM(depth_tiles.shape, jnp.float32),
+            pltpu.VMEM((split, result_rows, 128), jnp.float32),
+            pltpu.VMEM((YS, 16, 128), jnp.float32),
+            pltpu.VMEM((split * YS, 16, 128), jnp.float32),
+            pltpu.VMEM((16, 128), jnp.float32),
+            pltpu.VMEM((2 * ZS, 16, 128), jnp.float32),
+            pltpu.SemaphoreType.DMA((2 * split,)),
+            pltpu.SemaphoreType.DMA((2 * split,)),
+            pltpu.SemaphoreType.DMA((split * YS,)),
+            pltpu.SemaphoreType.DMA((split * YS,)),
+            pltpu.SemaphoreType.DMA((2 * ZS,)),
+            pltpu.SemaphoreType.DMA((2 * ZS,)),
         ],
-        compiler_params=pltpu.CompilerParams(vmem_limit_bytes=48 * 2**20),
+        compiler_params=pltpu.CompilerParams(
+            collective_id=1, has_side_effects=True, vmem_limit_bytes=48 * 2**20
+        ),
         name="decode",
-    )(far, own, weights, head_rows)
+    )(far, own, weights, head_rows, depth_tiles, pose_own, pose_far, partner_tile)
 
 
 def shards(
@@ -876,48 +950,36 @@
         split,
     )
     head_rows = jnp.pad(head_weight.T, ((0, 12), (0, 0)))
-    head_own = decode(
-        far_rows.reshape(pair_count // split * tokens, dec_width),
+    own_pairs = pair_count // split
+    depth_mask = jnp.stack([depths, valid_mask.astype(jnp.float32)], axis=0)
+    depth_tiles = depth_mask.reshape(2, split, own_count, token_share).transpose(1, 0, 2, 3)
+    depth_tiles = jnp.pad(
+        depth_tiles.reshape(split, 2 * own_count, token_share),
+        ((0, 0), (0, 8 - 2 * own_count), (0, 128 - token_share)),
+    )
+    pose_own = lax.dynamic_slice_in_dim(camera_poses, place * own_count, own_count, 1)
+    pose_own = jnp.pad(jnp.repeat(pose_own.T, K, axis=0), ((0, 0), (0, 116)))
+    own_partner = lax.dynamic_slice_in_dim(flat_partner, place * own_pairs, own_pairs, 0)
+    partner_tile = jnp.broadcast_to(own_partner[:, None], (own_pairs, 128))
+    picked_pose = pose_tiles[own_partner // images, :12, :images].astype(jnp.float32)
+    local = (own_partner % images)[:, None, None] == jnp.arange(images, dtype=jnp.int32)
+    pose_far = jnp.pad(jnp.sum(jnp.where(local, picked_pose, 0.0), axis=2), ((0, 0), (0, 116)))
+    results, total = decode(
+        far_rows.reshape(own_pairs * tokens, dec_width),
         own_rows.reshape(own_count * tokens, dec_width),
         weights_full.reshape(4, dec_width, dec_width),
         head_rows,
-        pair_count // split,
+        depth_tiles,
+        pose_own,
+        pose_far,
+        partner_tile,
+        own_pairs,
     )
-    head_own = head_own[:, :4].transpose(1, 0, 2)
-    moved = lax.all_to_all(head_own, "mp", split_axis=2, concat_axis=1, tiled=True)
-    points = moved[:3]
-    confidence = 1.0 + jnp.exp(moved[3])
-    pointmap = jnp.concatenate([points, confidence[None]], axis=0)
-    ray_dirs = make_rays(first_token + jnp.arange(token_share, dtype=jnp.int32), tokens // 16)
-    weight = valid_mask.astype(jnp.float32)
-    pose_table = pose_tiles[:, :12, :images].transpose(1, 0, 2).reshape(12, groups * images)
-    pose_far = pose_table[:, flat_partner].astype(jnp.float32).reshape(12, images, K)
-    point_grid = points.reshape(3, images, K, token_share)
-    conf_grid = confidence.reshape(images, K, token_share)
-
-    def loss_fn(depth_map, pose_own, pose_other):
-        return align_loss(
-            depth_map, pose_own, pose_other, point_grid, conf_grid, weight, ray_dirs, 1.0 / tokens
-        )
-
-    loss_value, pullback = jax.vjp(loss_fn, depths, camera_poses, pose_far)
-    grad_depth, grad_own, grad_far = pullback(jnp.ones_like(loss_value))
-    grad_far_flat = grad_far.reshape(12, pair_count)
-    total_images = groups * images
-    base_image = lax.axis_index("img") * images
-    image_ids = jnp.arange(total_images, dtype=jnp.int32)
-    partner_hits = (flat_partner[:, None] == image_ids[None, :]).astype(jnp.float32)
-    own_hits = (
-        (base_image + jnp.arange(images, dtype=jnp.int32))[:, None] == image_ids[None, :]
-    ).astype(jnp.float32)
-    dense_grad = jnp.dot(grad_far_flat, partner_hits, precision=lax.Precision.HIGHEST) + jnp.dot(
-        grad_own, own_hits, precision=lax.Precision.HIGHEST
-    )
-    dense_rows = dense_grad.reshape(12, groups, images).transpose(1, 0, 2).reshape(groups, 1, -1)
-    dense_rows = jnp.pad(dense_rows, ((0, 0), (0, 7), (0, 128 - 12 * images)))
-    total = reduce_poses(dense_rows.reshape(YS, 2 * ZS, 8, 128), split)
-    grad_pose = total[0, : 12 * images].reshape(12, images)
-    new_depths = depths - depth_step * grad_depth
+    pointmap = results[:, : 4 * own_pairs, :token_share].reshape(split, 4, own_pairs, token_share)
+    pointmap = pointmap.transpose(1, 0, 2, 3).reshape(4, pair_count, token_share)
+    new_depths = results[:, 4 * own_pairs : 4 * own_pairs + own_count, :token_share]
+    new_depths = new_depths.reshape(images, token_share)
+    grad_pose = lax.dynamic_slice(total, (0, here % (2 * ZS) * images), (12, images))
     new_poses = camera_poses - pose_step * grad_pose
     return (pointmap, new_depths, new_poses)
 

time: 210 us -> 227 us (1.081)
  local copies, waits for them, and re-layouts: 20.4 us -> 53.3 us
  Pallas kernels: 177 us -> 170 us
  starting transfers between devices: 4.14 us -> 0 us
  other arithmetic: 6.15 us -> 2.13 us
    gather x1 -> x48, local copies, waits for them, and re-layouts: 0.64 us -> 41.8 us  [shards(): pose_table[:, flat_partner].astype(jnp.float32).reshape(12, images, K)]
    pallas_call x2 -> x1, Pallas kernels: 47.6 us -> 40.6 us  [decode(): pl.pallas_call(decode_kernel, out_shape=(jax.ShapeDtypeStruct((split, res...]
    all_to_all x1 -> x0, starting transfers between devices: 4.14 us -> none  [shards(): lax.all_to_all(head_own, 'mp', split_axis=2, concat_axis=1, tiled=True)]
    unnamed x26 -> x20, local copies, waits for them, and re-layouts: 6.17 us -> 5.82 us
  transfers between devices with their start and end apart: 1 -> 0, of which waited for: 0 -> 0; matrix products, arithmetic and copies ran while one was open for 2% -> 0% of each run, Pallas kernels for 0% -> 0%
where the time goes in v4:
time: 227 us; the launch traced here: 226 us
  Pallas kernels  170 us (75%)
  local copies, waits for them, and re-layouts  53.3 us (23%)
    pallas_call x1, Pallas kernels, exchange(): pl.pallas_call(exchange_kernel, out_shape=(jax.ShapeDtypeStruct((per_dev,...  129 us
    gather x48, local copies, waits for them, and re-layouts  41.8 us
    pallas_call x1, Pallas kernels, decode(): pl.pallas_call(decode_kernel, out_shape=(jax.ShapeDtypeStruct((split, res...  40.6 us
    unnamed x20, local copies, waits for them, and re-layouts  5.82 us

profile of v4, /device:TPU:1, one launch (start us, length us, event | category | flops | bytes accessed | tf_op | source)
XLA Modules:
  0.0 226.3 jit_solution(16031108528565178319)
XLA Ops:
  0.7 0.8 reshape.66
  1.4 0.6 fusion.2.pick_ref
  2.0 1.8 constant_dynamic-slice_fusion.1.patch_own_ref
  3.8 1.7 copy.30
  5.5 1.7 copy.32.enc_proj_ref
  7.2 1.2 pad_maximum_fusion.weights_ref
  8.5 0.6 pad.20.pose_ref
  9.1 129.5 %exchange.1 = (bf16[16,4,24,768]{3,2,1,0:T(8,128)(2,1)}, bf16[2,4,24,768]{3,2,1,0:T(8,128)(2,1)}, bf16[4,4,192,768]{3,2,1,0:T(8,128)(2,1)}, bf16[64,16,128]{2,1,0:T(8,128)(2,1)S(1)}) custom-call(s32[64]{0:T(128)} %fusion.2.pick_ref, bf16[768,1024]{1,0:T(8,128)(2,1)} %bitcast.41, bf16[8,24,1024]{2,1,0:T(8,128)(2,1)} %constant_dynamic-slice_fusion.1.patch_own_ref, ...), custom_call_target="tpu_custom_call" | custom-call | tf_op jit(solution)/shard_map/exchange/pallas_call | solution.py:530
  138.7 41.8 %while.1 = (s32[]{:T(128)}, bf16[64,16,128]{2,1,0:T(8,128)(2,1)S(1)}, s32[16,3]{0,1:T(4,128)S(1)}, bf16[16,12,8]{2,1,0:T(8,128)(2,1)S(1)}, s32[]{:T(128)}) while((s32[]{:T(128)}, bf16[64,16,128]{2,1,0:T(8,128)(2,1)S(1)}, s32[16,3]{0,1:T(4,128)S(1)}, bf16[16,12,8]{2,1,0:T(8,128)(2,1)S(1)}, s32[]{:T(128)}) %tuple.28), condition=%wide.while_cond, body=%wide.while_body.sunk | while | flops 2 | bytes 8321 | solution.py:964
  138.8 0.5 fusion.12
  139.3 2.0 dynamic-slice_dynamic-update-slice_fusion.2
  141.4 0.5 fusion.12
  142.0 2.0 dynamic-slice_dynamic-update-slice_fusion.2
  144.0 0.5 fusion.12
  144.6 2.0 dynamic-slice_dynamic-update-slice_fusion.2
  146.7 0.5 fusion.12
  147.2 2.0 dynamic-slice_dynamic-update-slice_fusion.2
  149.3 0.5 fusion.12
  149.8 2.0 dynamic-slice_dynamic-update-slice_fusion.2
  151.9 0.5 fusion.12
  152.4 2.0 dynamic-slice_dynamic-update-slice_fusion.2
  154.5 0.5 fusion.12
  155.0 2.0 dynamic-slice_dynamic-update-slice_fusion.2
  157.1 0.5 fusion.12
  157.6 2.0 dynamic-slice_dynamic-update-slice_fusion.2
  159.7 0.5 fusion.12
  160.3 2.0 dynamic-slice_dynamic-update-slice_fusion.2
  162.3 0.5 fusion.12
  162.9 2.0 dynamic-slice_dynamic-update-slice_fusion.2
  164.9 0.5 fusion.12
  165.5 2.0 dynamic-slice_dynamic-update-slice_fusion.2
  167.6 0.5 fusion.12
  168.1 2.0 dynamic-slice_dynamic-update-slice_fusion.2
  170.2 0.5 fusion.12
  170.7 2.0 dynamic-slice_dynamic-update-slice_fusion.2
  172.8 0.5 fusion.12
  173.3 2.0 dynamic-slice_dynamic-update-slice_fusion.2
  175.4 0.5 fusion.12
  175.9 2.0 dynamic-slice_dynamic-update-slice_fusion.2
  178.0 0.5 fusion.12
  178.6 2.0 dynamic-slice_dynamic-update-slice_fusion.2
  180.6 0.1 select_reduce_fusion
  180.9 1.7 copy-done
  182.6 1.0 copy-done.1
  183.6 40.6 %decode.1 = (f32[4,72,128]{2,1,0:T(8,128)S(1)}, f32[16,128]{1,0:T(8,128)S(1)}) custom-call(bf16[1536,768]{1,0:T(8,128)(2,1)S(1)} %bitcast.37, bf16[192,768]{1,0:T(8,128)(2,1)S(1)} %bitcast.38, bf16[4,768,768]{2,1,0:T(8,128)(2,1)} %bitcast.40, bf16[16,768]{1,0:T(8,128)(2,1)S(1)} %pad.21.head_ref, f32[4,8,128]{2,1,0:T(8,128)S(1)} %pad.22.depth_ref, ...), custom_call_target="tpu_custom_call" | custom-call | tf_op jit(solution)/shard_map/decode/pallas_call | solution.py:869
  224.2 0.7 copy.37
  225.1 0.7 copy.38
  225.8 0.6 slice.7
  (50 shorter events, 1.7 us)
Async XLA Ops:
  5.5 1.7 copy-start.2
  5.5 1.7 copy-start.3
  7.2 1.2 copy-start.4
  9.1 171.7 %copy-start.6 = (s32[8,24]{1,0:T(8,128)S(1)}, s32[8,24]{1,0:T(8,128)}, u32[]{:S(2)}) copy-start(s32[8,24]{1,0:T(8,128)} %param.21) | copy-start | bytes 2308
  9.1 171.8 %copy-start.7 = (f32[8,24]{1,0:T(8,128)S(1)}, f32[8,24]{1,0:T(8,128)}, u32[]{:S(2)}) copy-start(f32[8,24]{1,0:T(8,128)} %param.19) | copy-start | bytes 2308
  9.1 171.8 %copy-start.5 = (bf16[768,4]{0,1:T(4,128)(2,1)S(1)}, bf16[768,4]{0,1:T(4,128)(2,1)}, u32[]{:S(2)}) copy-start(bf16[768,4]{0,1:T(4,128)(2,1)} %param.17) | copy-start | bytes 18436
  180.9 1.7 copy-start
  182.6 1.0 copy-start.1

commit v5 on v4

--- a/solution.py
+++ b/solution.py
@@ -341,28 +341,42 @@
         normed = norm_rows(patches_ref[span, :].astype(jnp.float32))
         projected = jnp.dot(normed, enc_proj_ref[...], preferred_element_type=jnp.float32)
         projected = projected.astype(jnp.bfloat16)
-        for image in range(2):
+        places = [(image, first) for image in range(2) for first in range(0, local, 128)]
+
+        def take(kind, image, first):
             lines = slice(image * tokens, (image + 1) * tokens)
-            for first in range(0, local, 128):
-                query = projected[lines, first : first + 128] * jnp.bfloat16(HD ** (-0.5))
-                key = projected[lines, local + first : local + first + 128]
-                value = projected[lines, 2 * local + first : 2 * local + first + 128]
-                both = jnp.concatenate(
-                    [jnp.where(first_half, query, zero), jnp.where(first_half, zero, query)], axis=0
+            return projected[lines, kind * local + first : kind * local + first + 128]
+
+        scores = []
+        for image, first in places:
+            query = take(0, image, first) * jnp.bfloat16(HD ** (-0.5))
+            both = jnp.concatenate(
+                [jnp.where(first_half, query, zero), jnp.where(first_half, zero, query)], axis=0
+            )
+            scores.append(
+                lax.dot_general(
+                    both, take(1, image, first), last, preferred_element_type=jnp.float32
                 )
-                scores = lax.dot_general(both, key, last, preferred_element_type=jnp.float32)
-                expos = jnp.exp(scores - jnp.max(scores, axis=1, keepdims=True))
-                got = jnp.dot(
-                    expos.astype(jnp.bfloat16),
-                    jnp.concatenate([value, ones], axis=1),
-                    preferred_element_type=jnp.float32,
-                )
-                got = got[:, :128] / got[:, 128:]
-                got = jnp.where(first_half, got[:tokens], got[tokens:])
-                for place in range(split):
-                    mixed[place, pair * 2 + image, :, first : first + 128] = got[
-                        place * share : (place + 1) * share
-                    ].astype(jnp.bfloat16)
+            )
+        expos = [
+            jnp.exp(each - jnp.max(each, axis=1, keepdims=True)).astype(jnp.bfloat16)
+            for each in scores
+        ]
+        sums = [
+            jnp.dot(
+                each,
+                jnp.concatenate([take(2, image, first), ones], axis=1),
+                preferred_element_type=jnp.float32,
+            )
+            for each, (image, first) in zip(expos, places)
+        ]
+        for each, (image, first) in zip(sums, places):
+            got = each[:, :128] / each[:, 128:]
+            got = jnp.where(first_half, got[:tokens], got[tokens:])
+            for place in range(split):
+                mixed[place, pair * 2 + image, :, first : first + 128] = got[
+                    place * share : (place + 1) * share
+                ].astype(jnp.bfloat16)
         return carry
 
     lax.fori_loop(0, images // 4, encode, 0)
@@ -573,8 +587,9 @@
     head_ref,
     depth_ref,
     pose_own_ref,
-    pose_far_ref,
+    pose_all_ref,
     partner_ref,
+    partner_row_ref,
     result_ref,
     total_ref,
     queries,
@@ -672,7 +687,7 @@
         ).astype(jnp.bfloat16)
         return carry
 
-    lax.fori_loop(0, pairs // 4, project, 0)
+    lax.fori_loop(0, pairs // 4, project, 0, unroll=2)
     pl.semaphore_wait(barrier, len(plane) + len(line))
 
     def depth_copy(step, slot):
@@ -688,26 +703,60 @@
         depth_copy(step, me).start()
     depth_all[me] = depth_ref[me]
     staging[...] = jnp.zeros_like(staging)
+    members = own_count * split
+    group_count, pose_rows, _ = pose_all_ref.shape
+    lane_ids = lax.broadcasted_iota(jnp.int32, (pairs, 128), 1)
+    chosen = (lane_ids == lax.rem(partner_ref[...], members)).astype(jnp.bfloat16)
+    candidates = lax.dot_general(
+        pose_all_ref[...].reshape(group_count * pose_rows, 128),
+        chosen,
+        last,
+        preferred_element_type=jnp.float32,
+    ).reshape(group_count, pose_rows, pairs)
+    owners = lax.broadcasted_iota(jnp.int32, (group_count, pose_rows, pairs), 0)
+    held_by = lax.div(partner_row_ref[:1, :pairs], members)
+    turned = jnp.sum(jnp.where(owners == held_by[None], candidates, 0.0), axis=0)
+    same = lax.broadcasted_iota(jnp.int32, (pose_rows, pose_rows), 0) == lax.broadcasted_iota(
+        jnp.int32, (pose_rows, pose_rows), 1
+    )
+    far_pose = lax.dot_general(
+        turned.astype(jnp.bfloat16),
+        same.astype(jnp.bfloat16),
+        (((0,), (0,)), ((), ())),
+        preferred_element_type=jnp.float32,
+    )
     ones = jnp.ones((tokens, 128), jnp.bfloat16)
 
     def attend(pair, carry):
         span = pl.ds(pl.multiple_of(pair * tokens, tokens), tokens)
         image = pair // per_image
-        for block in range(blocks):
-            columns = slice(block * 128, (block + 1) * 128)
-            scores = lax.dot_general(
-                queries[image, block], keys[span, columns], last, preferred_element_type=jnp.float32
+        columns = [slice(block * 128, (block + 1) * 128) for block in range(blocks)]
+        scores = [
+            lax.dot_general(
+                queries[image, block], keys[span, part], last, preferred_element_type=jnp.float32
             )
-            expos = jnp.exp(scores - jnp.max(scores, axis=1, keepdims=True)).astype(jnp.bfloat16)
-            both = jnp.concatenate([values[span, columns], ones], axis=1)
-            got = jnp.dot(expos, both, preferred_element_type=jnp.float32)
-            got = got[:, :128] / got[:, 128:]
-            mixed[span, columns] = jnp.where(first_half, got[:tokens], got[tokens:]).astype(
+            for block, part in enumerate(columns)
+        ]
+        expos = [
+            jnp.exp(each - jnp.max(each, axis=1, keepdims=True)).astype(jnp.bfloat16)
+            for each in scores
+        ]
+        sums = [
+            jnp.dot(
+                each,
+                jnp.concatenate([values[span, part], ones], axis=1),
+                preferred_element_type=jnp.float32,
+            )
+            for each, part in zip(expos, columns)
+        ]
+        for each, part in zip(sums, columns):
+            got = each[:, :128] / each[:, 128:]
+            mixed[span, part] = jnp.where(first_half, got[:tokens], got[tokens:]).astype(
                 jnp.bfloat16
             )
         return carry
 
-    lax.fori_loop(0, pairs, attend, 0)
+    lax.fori_loop(0, pairs, attend, 0, unroll=2)
 
     def finish(step, carry):
         span = pl.ds(pl.multiple_of(step * chunk, chunk), chunk)
@@ -722,7 +771,7 @@
             heads_all[step * 4 + part] = heads[:, part * tokens : (part + 1) * tokens]
         return carry
 
-    lax.fori_loop(0, pairs // 4, finish, 0)
+    lax.fori_loop(0, pairs // 4, finish, 0, unroll=2)
     for step in range(1, split):
         depth_copy(step, behind(step)).wait_recv()
 
@@ -747,7 +796,7 @@
     points = [heads_all[:, component, :] for component in range(3)]
     confidence = 1.0 + jnp.exp(heads_all[:, 3, :])
     weight = valid * confidence * (2.0 / tokens)
-    own_pose, far_pose = pose_own_ref[...], pose_far_ref[...]
+    own_pose = pose_own_ref[...]
     lane128 = lax.broadcasted_iota(jnp.int32, (pairs, 128), 1)
     own_grad = jnp.zeros((pairs, 128), jnp.float32)
     far_grad = jnp.zeros((pairs, 128), jnp.float32)
@@ -859,7 +908,9 @@
         line_copy(number, dz, dc, row).wait_send()
 
 
-def decode(far, own, weights, head_rows, depth_tiles, pose_own, pose_far, partner_tile, pairs):
+def decode(
+    far, own, weights, head_rows, depth_tiles, pose_own, poses, partner_tile, partner_row, pairs
+):
     width = own.shape[1]
     tokens = far.shape[0] // pairs
     own_count = own.shape[0] // tokens
@@ -872,7 +923,7 @@
             jax.ShapeDtypeStruct((split, result_rows, 128), jnp.float32),
             jax.ShapeDtypeStruct((16, 128), jnp.float32),
         ),
-        in_specs=[vmem] * 8,
+        in_specs=[vmem] * 9,
         out_specs=(vmem, vmem),
         scratch_shapes=[
             pltpu.VMEM((own_count, width // 128, 2 * tokens, 128), jnp.bfloat16),
@@ -897,7 +948,7 @@
             collective_id=1, has_side_effects=True, vmem_limit_bytes=48 * 2**20
         ),
         name="decode",
-    )(far, own, weights, head_rows, depth_tiles, pose_own, pose_far, partner_tile)
+    )(far, own, weights, head_rows, depth_tiles, pose_own, poses, partner_tile, partner_row)
 
 
 def shards(
@@ -961,9 +1012,7 @@
     pose_own = jnp.pad(jnp.repeat(pose_own.T, K, axis=0), ((0, 0), (0, 116)))
     own_partner = lax.dynamic_slice_in_dim(flat_partner, place * own_pairs, own_pairs, 0)
     partner_tile = jnp.broadcast_to(own_partner[:, None], (own_pairs, 128))
-    picked_pose = pose_tiles[own_partner // images, :12, :images].astype(jnp.float32)
-    local = (own_partner % images)[:, None, None] == jnp.arange(images, dtype=jnp.int32)
-    pose_far = jnp.pad(jnp.sum(jnp.where(local, picked_pose, 0.0), axis=2), ((0, 0), (0, 116)))
+    partner_row = jnp.broadcast_to(jnp.pad(own_partner, (0, 128 - own_pairs))[None], (8, 128))
     results, total = decode(
         far_rows.reshape(own_pairs * tokens, dec_width),
         own_rows.reshape(own_count * tokens, dec_width),
@@ -971,8 +1020,9 @@
         head_rows,
         depth_tiles,
         pose_own,
-        pose_far,
+        pose_tiles,
         partner_tile,
+        partner_row,
         own_pairs,
     )
     pointmap = results[:, : 4 * own_pairs, :token_share].reshape(split, 4, own_pairs, token_share)

time: 227 us -> 178 us (0.78)
  local copies, waits for them, and re-layouts: 53.3 us -> 12.5 us
  Pallas kernels: 170 us -> 162 us
    gather x48 -> x0, local copies, waits for them, and re-layouts: 41.8 us -> none
    pallas_call x1, Pallas kernels: 40.6 us -> 32.5 us  [decode(): pl.pallas_call(decode_kernel, out_shape=(jax.ShapeDtypeStruct((split, res...]
    unnamed x20 -> x22, local copies, waits for them, and re-layouts: 5.82 us -> 6.77 us
where the time goes in v5:
time: 178 us; the launch traced here: 177 us
  Pallas kernels  162 us (91%)
  local copies, waits for them, and re-layouts  12.5 us (7%)
  other arithmetic  1.86 us (1%)
    pallas_call x1, Pallas kernels, exchange(): pl.pallas_call(exchange_kernel, out_shape=(jax.ShapeDtypeStruct((per_dev,...  130 us
    pallas_call x1, Pallas kernels, decode(): pl.pallas_call(decode_kernel, out_shape=(jax.ShapeDtypeStruct((split, res...  32.5 us
    unnamed x22, local copies, waits for them, and re-layouts  6.77 us

profile of v5, /device:TPU:1, one launch (start us, length us, event | category | flops | bytes accessed | tf_op | source)
XLA Modules:
  0.0 177.2 jit_solution(8364943997539048973)
XLA Ops:
  0.7 0.8 reshape.46
  1.4 0.6 fusion.2.pick_ref
  2.0 1.8 constant_dynamic-slice_fusion.patch_own_ref
  3.8 1.7 copy.30
  5.5 0.0 copy-start.3
  5.5 0.0 copy-start.4
  5.5 1.7 copy.32.enc_proj_ref
  7.2 0.0 copy-start.5
  7.2 0.0 copy-done.3
  7.2 0.0 copy-done.4
  7.2 1.2 pad_maximum_fusion.weights_ref
  8.4 0.0 copy-done.5
  8.4 0.1 copy.31
  8.5 0.6 pad.20.pose_ref
  9.1 0.0 copy-start.7
  9.1 0.0 copy-start.8
  9.1 0.0 copy-start.6
  9.1 129.6 %exchange.1 = (bf16[16,4,24,768]{3,2,1,0:T(8,128)(2,1)}, bf16[2,4,24,768]{3,2,1,0:T(8,128)(2,1)}, bf16[4,4,192,768]{3,2,1,0:T(8,128)(2,1)}, bf16[64,16,128]{2,1,0:T(8,128)(2,1)}) custom-call(s32[64]{0:T(128)} %fusion.2.pick_ref, bf16[768,1024]{1,0:T(8,128)(2,1)} %bitcast.30, bf16[8,24,1024]{2,1,0:T(8,128)(2,1)} %constant_dynamic-slice_fusion.patch_own_ref, ...), custom_call_target="tpu_custom_call" | custom-call | tf_op jit(solution)/shard_map/exchange/pallas_call | solution.py:544
  138.7 0.1 dynamic_slice.14
  138.8 0.1 broadcast_in_dim.20.partner_ref
  138.9 0.0 copy-done.7
  138.9 0.0 copy-done.8
  138.9 0.0 copy-done.6
  139.0 0.0 copy-start
  139.0 1.7 copy-done
  140.6 0.0 copy-start.1
  140.6 1.0 copy-done.1
  141.6 0.0 copy-start.2
  141.6 0.9 copy-done.2
  142.5 32.5 %decode.1 = (f32[4,72,128]{2,1,0:T(8,128)S(1)}, f32[16,128]{1,0:T(8,128)S(1)}) custom-call(bf16[1536,768]{1,0:T(8,128)(2,1)S(1)} %bitcast.26, bf16[192,768]{1,0:T(8,128)(2,1)S(1)} %bitcast.27, bf16[4,768,768]{2,1,0:T(8,128)(2,1)} %bitcast.29, bf16[16,768]{1,0:T(8,128)(2,1)S(1)} %pad.21.head_ref, f32[4,8,128]{2,1,0:T(8,128)S(1)} %pad.22.depth_ref, ...), custom_call_target="tpu_custom_call" | custom-call | tf_op jit(solution)/shard_map/decode/pallas_call | solution.py:920
  175.1 0.7 copy.37
  175.8 0.1 copy.36
  175.9 0.1 multiply_subtract_fusion
  175.9 0.7 copy.38
  176.6 0.6 slice.7
  (12 shorter events, 0.1 us)
Async XLA Ops:
  5.5 1.7 copy-start.3
  5.5 1.7 copy-start.4
  7.2 1.2 copy-start.5
  9.1 129.8 %copy-start.7 = (s32[8,24]{1,0:T(8,128)S(1)}, s32[8,24]{1,0:T(8,128)}, u32[]{:S(2)}) copy-start(s32[8,24]{1,0:T(8,128)} %param.21) | copy-start | bytes 2308
  9.1 129.8 %copy-start.8 = (f32[8,24]{1,0:T(8,128)S(1)}, f32[8,24]{1,0:T(8,128)}, u32[]{:S(2)}) copy-start(f32[8,24]{1,0:T(8,128)} %param.19) | copy-start | bytes 2308
  9.1 129.8 %copy-start.6 = (bf16[768,4]{0,1:T(4,128)(2,1)S(1)}, bf16[768,4]{0,1:T(4,128)(2,1)}, u32[]{:S(2)}) copy-start(bf16[768,4]{0,1:T(4,128)(2,1)} %param.17) | copy-start | bytes 18436
  139.0 1.7 copy-start
  140.6 1.0 copy-start.1
  141.6 0.9 copy-start.2

commit v6 on v5

--- a/solution.py
+++ b/solution.py
@@ -109,7 +109,6 @@
 def exchange_kernel(
     pick_ref,
     patches_ref,
-    patch_own_ref,
     enc_proj_ref,
     enc_out_ref,
     embed_ref,
@@ -309,11 +308,30 @@
 
     def out_copy(step, slot):
         return remote(
-            enc_out_ref,
-            enc_out_all.at[slot],
+            enc_out_ref.at[pl.ds(2 * core, 2)],
+            enc_out_all.at[slot, pl.ds(2 * core, 2)],
             enc_send.at[step],
             enc_recv.at[step],
             mate(step),
+        )
+
+    def out_relay(step, slot):
+        part = pl.ds(2 * core + (0 if step == 1 else 1), 1)
+        return remote(
+            enc_out_all.at[slot, part],
+            enc_out_all.at[slot, part],
+            enc_send.at[3 * split + step],
+            enc_recv.at[3 * split + step],
+            mate(step),
+        )
+
+    def out_twin(step, half, slot):
+        return remote(
+            enc_out_all.at[slot, pl.ds(2 * half, 2)],
+            enc_out_all.at[slot, pl.ds(2 * half, 2)],
+            enc_send.at[4 * split + step],
+            enc_recv.at[4 * split + step],
+            twin,
         )
 
     def mixed_copy(part, step, slot):
@@ -326,26 +344,30 @@
             mate(step),
         )
 
-    for step in range(1, split):
+    for step in (1, 3):
         out_copy(step, me).start()
     enc_out_all[me] = enc_out_ref[...]
     tokens = share * split
-    local = enc_out_ref.shape[0]
+    local = enc_out_ref.shape[0] * enc_out_ref.shape[1]
     last = (((1,), (1,)), ((), ()))
     first_half = lax.broadcasted_iota(jnp.int32, (1, 128), 1) < HD
     zero = jnp.zeros((), jnp.bfloat16)
     ones = jnp.ones((tokens, 128), jnp.bfloat16)
 
     def encode(pair, carry):
-        span = pl.ds(pl.multiple_of(pair * 2 * tokens, 2 * tokens), 2 * tokens)
-        normed = norm_rows(patches_ref[span, :].astype(jnp.float32))
-        projected = jnp.dot(normed, enc_proj_ref[...], preferred_element_type=jnp.float32)
-        projected = projected.astype(jnp.bfloat16)
+        picture = patches_ref[pl.ds(2 * pair, 2)].astype(jnp.float32)
+        normed = norm_rows(picture.reshape(2 * tokens, -1))
+        projected = [
+            jnp.dot(normed, enc_proj_ref[kind], preferred_element_type=jnp.float32).astype(
+                jnp.bfloat16
+            )
+            for kind in range(3)
+        ]
         places = [(image, first) for image in range(2) for first in range(0, local, 128)]
 
         def take(kind, image, first):
             lines = slice(image * tokens, (image + 1) * tokens)
-            return projected[lines, kind * local + first : kind * local + first + 128]
+            return projected[kind][lines, first : first + 128]
 
         scores = []
         for image, first in places:
@@ -382,22 +404,29 @@
     lax.fori_loop(0, images // 4, encode, 0)
     for step in range(1, split):
         mixed_copy(0, step, me).start()
+    for step in (1, 3):
+        out_copy(step, behind(step)).wait_recv()
+        out_relay(step, behind(step)).start()
+        out_twin(step, core, behind(step)).start()
     lax.fori_loop(images // 4, images // 2, encode, 0)
     for step in range(1, split):
         mixed_copy(1, step, me).start()
     for step in (1, 3):
+        out_relay(step, behind(2)).wait_recv()
+    out_twin(2, core, behind(2)).start()
+    for step in (1, 3):
         weight_copy(step, me).start()
     mixed_all[me] = mixed[me]
-    encoded = patch_own_ref[...].astype(jnp.float32).reshape(images * share, -1)
+    encoded = patches_ref[:, me].astype(jnp.float32).reshape(images * share, -1)
     for step in range(split):
         source = behind(step)
         if step:
-            out_copy(step, source).wait_recv()
+            out_twin(step, 1 - core, source).wait_recv()
             mixed_copy(0, step, source).wait_recv()
             mixed_copy(1, step, source).wait_recv()
         part = mixed_all[source].astype(jnp.float32).reshape(images * share, local)
         encoded = encoded + jnp.dot(
-            part.astype(jnp.bfloat16), enc_out_all[source], preferred_element_type=jnp.float32
+            part.astype(jnp.bfloat16), enc_out_all[source].reshape(local, -1), preferred_element_type=jnp.float32
         )
     embedded = jnp.dot(norm_rows(encoded), embed_ref[...], preferred_element_type=jnp.float32)
     embedded = embedded.astype(jnp.bfloat16).astype(jnp.float32)
@@ -516,12 +545,14 @@
     for dy in range(1, YS):
         pose_cross(dy, y).wait_send()
     for step in range(1, split):
-        out_copy(step, me).wait_send()
+        out_twin(step, core, behind(step)).wait_send()
         mixed_copy(0, step, me).wait_send()
         mixed_copy(1, step, me).wait_send()
         own_copy(step, me).wait_send()
         weight_twin(step, core, behind(step)).wait_send()
     for step in (1, 3):
+        out_copy(step, me).wait_send()
+        out_relay(step, behind(step)).wait_send()
         weight_copy(step, me).wait_send()
         weight_relay(step, behind(step)).wait_send()
     for chunk in range(chunks):
@@ -534,8 +565,9 @@
             far_onward(chunk, step, behind(step)).wait_send()
 
 
-def exchange(pick, patches, patch_own, enc_proj, enc_out, embed, weights, pose, pairs, groups, split):
-    images, share, _ = patch_own.shape
+def exchange(pick, patches, enc_proj, enc_out, embed, weights, pose, pairs, groups, split):
+    images, _, share, _ = patches.shape
+    local = enc_out.shape[0] * enc_out.shape[1]
     width = embed.shape[1]
     chunks = len(WIDTHS)
     count = len(link_plan(images, WIDTHS)[1])
@@ -549,18 +581,18 @@
             jax.ShapeDtypeStruct((4, split) + weights.shape[1:], jnp.bfloat16),
             jax.ShapeDtypeStruct((groups,) + pose.shape, jnp.bfloat16),
         ),
-        in_specs=[pl.BlockSpec(memory_space=pltpu.SMEM)] + [vmem] * 7,
+        in_specs=[pl.BlockSpec(memory_space=pltpu.SMEM)] + [vmem] * 6,
         out_specs=(vmem,) * 4,
         scratch_shapes=[pltpu.VMEM((groups * images, share, w), jnp.bfloat16) for w in WIDTHS]
         + [pltpu.VMEM((pairs, share, w), jnp.bfloat16) for w in WIDTHS]
         + [pltpu.VMEM((2, per_dev // 2, share, w), jnp.bfloat16) for w in WIDTHS]
         + [
-            pltpu.VMEM((split, images, share, enc_out.shape[0]), jnp.bfloat16),
-            pltpu.VMEM((split, images, share, enc_out.shape[0]), jnp.bfloat16),
+            pltpu.VMEM((split, images, share, local), jnp.bfloat16),
+            pltpu.VMEM((split, images, share, local), jnp.bfloat16),
             pltpu.VMEM((split,) + enc_out.shape, jnp.bfloat16),
             pltpu.VMEM((images, share, width), jnp.bfloat16),
-            pltpu.SemaphoreType.DMA((3 * split,)),
-            pltpu.SemaphoreType.DMA((3 * split,)),
+            pltpu.SemaphoreType.DMA((5 * split,)),
+            pltpu.SemaphoreType.DMA((5 * split,)),
             pltpu.SemaphoreType.DMA((count,)),
             pltpu.SemaphoreType.DMA((count,)),
             pltpu.SemaphoreType.DMA((count + chunks,)),
@@ -577,7 +609,7 @@
             collective_id=0, has_side_effects=True, vmem_limit_bytes=56 * 2**20
         ),
         name="exchange",
-    )(pick, patches, patch_own, enc_proj, enc_out, embed, weights, pose)
+    )(pick, patches, enc_proj, enc_out, embed, weights, pose)
 
 
 def decode_kernel(
@@ -980,8 +1012,6 @@
     )
 
     token_share = tokens // split
-    first_token = place * token_share
-    patch_own = lax.dynamic_slice_in_dim(patches, first_token, token_share, 1)
     owner = flat_partner // images
     shift_y = (here // (2 * ZS) - owner // (2 * ZS)) % YS
     shift_z = ((here // 2) % ZS - (owner // 2) % ZS) % ZS
@@ -989,10 +1019,9 @@
     pick = ((shift_core * YS + shift_y) * ZS + shift_z) * images + flat_partner % images
     far_rows, own_rows, weights_full, pose_tiles = exchange(
         pick,
-        patches.reshape(images * tokens, model_width),
-        patch_own,
-        encoder_proj.reshape(model_width, 3 * enc_local),
-        encoder_out,
+        patches.reshape(images, split, token_share, model_width),
+        jnp.transpose(encoder_proj, (1, 0, 2)),
+        encoder_out.reshape(4, enc_local // 4, model_width),
         decoder_embed,
         weights,
         pose_tile,

time: 178 us -> 160 us (0.90)
  Pallas kernels: 162 us -> 148 us
  local copies, waits for them, and re-layouts: 12.5 us -> 7.32 us
    pallas_call x1, Pallas kernels: 130 us -> 117 us  [exchange(): pl.pallas_call(exchange_kernel, out_shape=(jax.ShapeDtypeStruct((per_dev,...]
    unnamed x22 -> x17, local copies, waits for them, and re-layouts: 6.77 us -> 5.05 us
where the time goes in v6:
time: 160 us; the launch traced here: 159 us
  Pallas kernels  148 us (92%)
  local copies, waits for them, and re-layouts  7.32 us (5%)
  other arithmetic  3.04 us (2%)
    pallas_call x1, Pallas kernels, exchange(): pl.pallas_call(exchange_kernel, out_shape=(jax.ShapeDtypeStruct((per_dev,...  117 us
    pallas_call x1, Pallas kernels, decode(): pl.pallas_call(decode_kernel, out_shape=(jax.ShapeDtypeStruct((split, res...  31.1 us
    unnamed x17, local copies, waits for them, and re-layouts  5.05 us

profile of v6, /device:TPU:1, one launch (start us, length us, event | category | flops | bytes accessed | tf_op | source)
XLA Modules:
  0.0 159.5 jit_solution(15044445408633824415)
XLA Ops:
  0.6 0.0 copy-start.3
  0.7 0.8 reshape.46
  1.4 0.6 fusion.2.pick_ref
  2.0 2.4 %pad_maximum_fusion.weights_ref = bf16[4,192,768]{2,1,0:T(8,128)(2,1)} fusion(bf16[1,192,768]{2,1,0:T(8,128)(2,1)} %bitcast.36, bf16[3,192,768]{2,1,0:T(8,128)(2,1)} %bitcast.32), kind=kLoop, calls=%fused_computation | loop fusion | flops 589824 | bytes 2359296 | tf_op jit(solution)/shard_map/concatenate | solution.py:1009
  4.4 0.0 copy-done.3
  4.4 0.1 copy.27
  4.5 0.6 pad.20.pose_ref
  5.1 0.0 copy-start.5
  5.1 0.0 copy-start.6
  5.1 0.0 copy-start.4
  5.1 117.2 %exchange.1 = (bf16[16,4,24,768]{3,2,1,0:T(8,128)(2,1)}, bf16[2,4,24,768]{3,2,1,0:T(8,128)(2,1)}, bf16[4,4,192,768]{3,2,1,0:T(8,128)(2,1)}, bf16[64,16,128]{2,1,0:T(8,128)(2,1)}) custom-call(s32[64]{0:T(128)} %fusion.2.pick_ref, bf16[8,4,24,1024]{3,2,1,0:T(8,128)(2,1)} %bitcast.30, bf16[3,1024,256]{2,1,0:T(8,128)(2,1)} %bitcast.31, ...), custom_call_target="tpu_custom_call" | custom-call | tf_op jit(solution)/shard_map/exchange/pallas_call | solution.py:576
  122.3 0.1 dynamic_slice.10
  122.4 0.1 broadcast_in_dim.20.partner_ref
  122.5 0.0 copy-done.5
  122.5 0.0 copy-done.6
  122.5 0.0 copy-done.4
  122.6 0.0 copy-start
  122.6 1.7 %copy-done = bf16[16,4,24,768]{3,2,1,0:T(8,128)(2,1)S(1)} copy-done((bf16[16,4,24,768]{3,2,1,0:T(8,128)(2,1)S(1)}, bf16[16,4,24,768]{3,2,1,0:T(8,128)(2,1)}, u32[]{:S(2)}) %copy-start) | copy-done | bytes 2359320
  124.2 0.0 copy-start.1
  124.2 1.0 copy-done.1
  125.2 0.0 copy-start.2
  125.2 0.9 copy-done.2
  126.1 31.1 %decode.1 = (f32[4,72,128]{2,1,0:T(8,128)S(1)}, f32[16,128]{1,0:T(8,128)S(1)}) custom-call(bf16[1536,768]{1,0:T(8,128)(2,1)S(1)} %bitcast.27, bf16[192,768]{1,0:T(8,128)(2,1)S(1)} %bitcast.28, bf16[4,768,768]{2,1,0:T(8,128)(2,1)} %bitcast.29, bf16[16,768]{1,0:T(8,128)(2,1)S(1)} %pad.21.head_ref, f32[4,8,128]{2,1,0:T(8,128)S(1)} %pad.22.depth_ref, ...), custom_call_target="tpu_custom_call" | custom-call | tf_op jit(solution)/shard_map/decode/pallas_call | solution.py:952
  157.3 0.7 copy.32
  158.0 0.1 copy.31
  158.1 0.1 multiply_subtract_fusion
  158.2 0.7 copy.33
  158.9 0.6 slice.7
  (12 shorter events, 0.1 us)
Async XLA Ops:
  0.6 3.8 %copy-start.3 = (f32[12,8]{0,1:T(8,128)S(1)}, f32[12,8]{0,1:T(8,128)}, u32[]{:S(2)}) copy-start(f32[12,8]{0,1:T(8,128)} %param.20) | copy-start | bytes 1156
  5.1 117.4 %copy-start.5 = (s32[8,24]{1,0:T(8,128)S(1)}, s32[8,24]{1,0:T(8,128)}, u32[]{:S(2)}) copy-start(s32[8,24]{1,0:T(8,128)} %param.21) | copy-start | bytes 2308
  5.1 117.4 %copy-start.6 = (f32[8,24]{1,0:T(8,128)S(1)}, f32[8,24]{1,0:T(8,128)}, u32[]{:S(2)}) copy-start(f32[8,24]{1,0:T(8,128)} %param.19) | copy-start | bytes 2308
  5.1 117.4 %copy-start.4 = (bf16[768,4]{0,1:T(4,128)(2,1)S(1)}, bf16[768,4]{0,1:T(4,128)(2,1)}, u32[]{:S(2)}) copy-start(bf16[768,4]{0,1:T(4,128)(2,1)} %param.17) | copy-start | bytes 18436
  122.6 1.7 %copy-start = (bf16[16,4,24,768]{3,2,1,0:T(8,128)(2,1)S(1)}, bf16[16,4,24,768]{3,2,1,0:T(8,128)(2,1)}, u32[]{:S(2)}) copy-start(bf16[16,4,24,768]{3,2,1,0:T(8,128)(2,1)} %get-tuple-element.9) | copy-start | bytes 7077892
  124.2 1.0 copy-start.1
  125.2 0.9 copy-start.2

commit v7 on v6

--- a/solution.py
+++ b/solution.py
@@ -114,12 +114,20 @@
     embed_ref,
     weights_ref,
     pose_ref,
+    head_ref,
+    depth_ref,
+    pose_own_ref,
+    partner_ref,
+    partner_row_ref,
+    result_ref,
+    total_ref,
     far_ref,
     own_ref,
     weights_all,
     pose_all,
     *scratch,
 ):
+    finish, scratch = scratch[:17], scratch[17:]
     chunks = len(WIDTHS)
     held, scratch = scratch[:chunks], scratch[chunks:]
     staged, scratch = scratch[:chunks], scratch[chunks:]
@@ -180,8 +188,12 @@
 
     barrier = pltpu.get_barrier_semaphore()
     peers = [line_peer(dz, dc, 1) for dz, dc in line]
-    peers += [y_peer(dy, 1) for dy in range(1, YS)]
-    peers += [mate(step) for step in range(1, split)]
+    peers += [
+        (spot(lax.rem(y + dy, YS), z, core)[0], lax.rem(me + dx, split))
+        for dx in range(split)
+        for dy in range(YS)
+        if dx or dy
+    ]
     for peer in peers:
         pl.semaphore_signal(barrier, inc=1, device_id=peer, device_id_type=MESH)
     pose_all[here] = pose_ref[...]
@@ -563,56 +575,23 @@
             far_direct(chunk, step, me).wait_send()
             far_onward(chunk, step, behind(2)).wait_recv()
             far_onward(chunk, step, behind(step)).wait_send()
-
-
-def exchange(pick, patches, enc_proj, enc_out, embed, weights, pose, pairs, groups, split):
-    images, _, share, _ = patches.shape
-    local = enc_out.shape[0] * enc_out.shape[1]
-    width = embed.shape[1]
-    chunks = len(WIDTHS)
-    count = len(link_plan(images, WIDTHS)[1])
-    vmem = pl.BlockSpec(memory_space=pltpu.VMEM)
-    per_dev = pairs // split
-    return pl.pallas_call(
-        exchange_kernel,
-        out_shape=(
-            jax.ShapeDtypeStruct((per_dev, split, share, width), jnp.bfloat16),
-            jax.ShapeDtypeStruct((images // split, split, share, width), jnp.bfloat16),
-            jax.ShapeDtypeStruct((4, split) + weights.shape[1:], jnp.bfloat16),
-            jax.ShapeDtypeStruct((groups,) + pose.shape, jnp.bfloat16),
-        ),
-        in_specs=[pl.BlockSpec(memory_space=pltpu.SMEM)] + [vmem] * 6,
-        out_specs=(vmem,) * 4,
-        scratch_shapes=[pltpu.VMEM((groups * images, share, w), jnp.bfloat16) for w in WIDTHS]
-        + [pltpu.VMEM((pairs, share, w), jnp.bfloat16) for w in WIDTHS]
-        + [pltpu.VMEM((2, per_dev // 2, share, w), jnp.bfloat16) for w in WIDTHS]
-        + [
-            pltpu.VMEM((split, images, share, local), jnp.bfloat16),
-            pltpu.VMEM((split, images, share, local), jnp.bfloat16),
-            pltpu.VMEM((split,) + enc_out.shape, jnp.bfloat16),
-            pltpu.VMEM((images, share, width), jnp.bfloat16),
-            pltpu.SemaphoreType.DMA((5 * split,)),
-            pltpu.SemaphoreType.DMA((5 * split,)),
-            pltpu.SemaphoreType.DMA((count,)),
-            pltpu.SemaphoreType.DMA((count,)),
-            pltpu.SemaphoreType.DMA((count + chunks,)),
-            pltpu.SemaphoreType.DMA((count + chunks,)),
-            pltpu.SemaphoreType.DMA((4 * split,)),
-            pltpu.SemaphoreType.DMA((4 * split,)),
-            pltpu.SemaphoreType.DMA((2 * ZS + YS,)),
-            pltpu.SemaphoreType.DMA((2 * ZS + YS,)),
-            pltpu.SemaphoreType.DMA((chunks, 3 * split)),
-            pltpu.SemaphoreType.DMA((chunks, 3 * split)),
-            pltpu.SemaphoreType.DMA((2 + chunks,)),
-        ],
-        compiler_params=pltpu.CompilerParams(
-            collective_id=0, has_side_effects=True, vmem_limit_bytes=56 * 2**20
-        ),
-        name="exchange",
-    )(pick, patches, enc_proj, enc_out, embed, weights, pose)
-
-
-def decode_kernel(
+    decode_part(
+        far_ref,
+        own_ref,
+        weights_all,
+        head_ref,
+        depth_ref,
+        pose_own_ref,
+        pose_all,
+        partner_ref,
+        partner_row_ref,
+        result_ref,
+        total_ref,
+        *finish,
+    )
+
+
+def decode_part(
     far_ref,
     own_ref,
     weights_ref,
@@ -642,7 +621,7 @@
     line_send,
     line_recv,
 ):
-    width = own_ref.shape[1]
+    width = own_ref.shape[3]
     pairs, _, tokens = heads_all.shape
     split = depth_all.shape[0]
     share = tokens // split
@@ -680,24 +659,18 @@
             device_id_type=MESH,
         )
 
-    barrier = pltpu.get_barrier_semaphore()
-    for dx, dy in plane:
-        pl.semaphore_signal(
-            barrier, inc=1, device_id=plane_peer(dx, dy, 1), device_id_type=MESH
-        )
-    for dz, dc in line:
-        pl.semaphore_signal(
-            barrier, inc=1, device_id=(y * rows_count + line_row(dz, dc, 1), me), device_id_type=MESH
-        )
     blocks = width // 128
-    own_count = own_ref.shape[0] // tokens
+    own_count = own_ref.shape[0]
     per_image = pairs // own_count
     last = (((1,), (1,)), ((), ()))
     lane = lax.broadcasted_iota(jnp.int32, (1, 128), 1)
     first_half = lane < HD
 
-    rows = norm_rows(own_ref[...].astype(jnp.float32))
-    projected = lax.dot_general(rows, weights_ref[0], last, preferred_element_type=jnp.float32)
+    def weight(kind):
+        return weights_ref[kind].reshape(width, width)
+
+    rows = norm_rows(own_ref[...].astype(jnp.float32).reshape(own_count * tokens, width))
+    projected = lax.dot_general(rows, weight(0), last, preferred_element_type=jnp.float32)
     projected = projected.astype(jnp.bfloat16) * jnp.bfloat16(HD ** (-0.5))
     zero = jnp.zeros((), jnp.bfloat16)
     for image in range(own_count):
@@ -710,18 +683,17 @@
 
     def project(step, carry):
         span = pl.ds(pl.multiple_of(step * chunk, chunk), chunk)
-        part = far_ref[span, :]
+        part = far_ref[pl.ds(step * 4, 4)].astype(jnp.float32)
+        part = part.reshape(chunk, width).astype(jnp.bfloat16)
         keys[span, :] = lax.dot_general(
-            part, weights_ref[1], last, preferred_element_type=jnp.float32
+            part, weight(1), last, preferred_element_type=jnp.float32
         ).astype(jnp.bfloat16)
         values[span, :] = lax.dot_general(
-            part, weights_ref[2], last, preferred_element_type=jnp.float32
+            part, weight(2), last, preferred_element_type=jnp.float32
         ).astype(jnp.bfloat16)
         return carry
 
     lax.fori_loop(0, pairs // 4, project, 0, unroll=2)
-    pl.semaphore_wait(barrier, len(plane) + len(line))
-
     def depth_copy(step, slot):
         return remote(
             depth_ref.at[lax.rem(me + step, split)],
@@ -793,8 +765,8 @@
     def finish(step, carry):
         span = pl.ds(pl.multiple_of(step * chunk, chunk), chunk)
         image = step * 4 // per_image
-        own = own_ref[pl.ds(pl.multiple_of(image * tokens, tokens), tokens), :].astype(jnp.float32)
-        settled = jnp.dot(mixed[span, :], weights_ref[3], preferred_element_type=jnp.float32)
+        own = own_ref[image].astype(jnp.float32).reshape(tokens, width)
+        settled = jnp.dot(mixed[span, :], weight(3), preferred_element_type=jnp.float32)
         settled = settled + jnp.concatenate([own] * 4, axis=0)
         heads = lax.dot_general(
             head_ref[...], norm_rows(settled), last, preferred_element_type=jnp.float32
@@ -940,47 +912,105 @@
         line_copy(number, dz, dc, row).wait_send()
 
 
-def decode(
-    far, own, weights, head_rows, depth_tiles, pose_own, poses, partner_tile, partner_row, pairs
+def pair_step(
+    pick,
+    patches,
+    enc_proj,
+    enc_out,
+    embed,
+    weights,
+    pose,
+    head_rows,
+    depth_tiles,
+    pose_own,
+    partner_tile,
+    partner_row,
+    pairs,
+    groups,
 ):
-    width = own.shape[1]
-    tokens = far.shape[0] // pairs
-    own_count = own.shape[0] // tokens
-    split = depth_tiles.shape[0]
+    images, split, share, _ = patches.shape
+    tokens = share * split
+    own_count = images // split
+    local = enc_out.shape[0] * enc_out.shape[1]
+    width = embed.shape[1]
+    chunks = len(WIDTHS)
+    count = len(link_plan(images, WIDTHS)[1])
     vmem = pl.BlockSpec(memory_space=pltpu.VMEM)
-    result_rows = 4 * pairs + 8
+    per_dev = pairs // split
+    result_rows = 4 * per_dev + 8
+    rows = per_dev * tokens
+    b16, f32, dma = jnp.bfloat16, jnp.float32, pltpu.SemaphoreType.DMA
     return pl.pallas_call(
-        decode_kernel,
+        exchange_kernel,
         out_shape=(
-            jax.ShapeDtypeStruct((split, result_rows, 128), jnp.float32),
-            jax.ShapeDtypeStruct((16, 128), jnp.float32),
+            jax.ShapeDtypeStruct((split, result_rows, 128), f32),
+            jax.ShapeDtypeStruct((16, 128), f32),
         ),
-        in_specs=[vmem] * 9,
+        in_specs=[pl.BlockSpec(memory_space=pltpu.SMEM)] + [vmem] * 11,
         out_specs=(vmem, vmem),
         scratch_shapes=[
-            pltpu.VMEM((own_count, width // 128, 2 * tokens, 128), jnp.bfloat16),
-            pltpu.VMEM(far.shape, jnp.bfloat16),
-            pltpu.VMEM(far.shape, jnp.bfloat16),
-            pltpu.VMEM(far.shape, jnp.bfloat16),
-            pltpu.VMEM((pairs, head_rows.shape[0], tokens), jnp.float32),
-            pltpu.VMEM(depth_tiles.shape, jnp.float32),
-            pltpu.VMEM((split, result_rows, 128), jnp.float32),
-            pltpu.VMEM((YS, 16, 128), jnp.float32),
-            pltpu.VMEM((split * YS, 16, 128), jnp.float32),
-            pltpu.VMEM((16, 128), jnp.float32),
-            pltpu.VMEM((2 * ZS, 16, 128), jnp.float32),
-            pltpu.SemaphoreType.DMA((2 * split,)),
-            pltpu.SemaphoreType.DMA((2 * split,)),
-            pltpu.SemaphoreType.DMA((split * YS,)),
-            pltpu.SemaphoreType.DMA((split * YS,)),
-            pltpu.SemaphoreType.DMA((2 * ZS,)),
-            pltpu.SemaphoreType.DMA((2 * ZS,)),
+            pltpu.VMEM((per_dev, split, share, width), b16),
+            pltpu.VMEM((own_count, split, share, width), b16),
+            pltpu.VMEM((4, split) + weights.shape[1:], b16),
+            pltpu.VMEM((groups,) + pose.shape, b16),
+            pltpu.VMEM((own_count, width // 128, 2 * tokens, 128), b16),
+            pltpu.VMEM((rows, width), b16),
+            pltpu.VMEM((rows, width), b16),
+            pltpu.VMEM((rows, width), b16),
+            pltpu.VMEM((per_dev, head_rows.shape[0], tokens), f32),
+            pltpu.VMEM(depth_tiles.shape, f32),
+            pltpu.VMEM((split, result_rows, 128), f32),
+            pltpu.VMEM((YS, 16, 128), f32),
+            pltpu.VMEM((split * YS, 16, 128), f32),
+            pltpu.VMEM((16, 128), f32),
+            pltpu.VMEM((2 * ZS, 16, 128), f32),
+            dma((2 * split,)),
+            dma((2 * split,)),
+            dma((split * YS,)),
+            dma((split * YS,)),
+            dma((2 * ZS,)),
+            dma((2 * ZS,)),
+        ]
+        + [pltpu.VMEM((groups * images, share, w), b16) for w in WIDTHS]
+        + [pltpu.VMEM((pairs, share, w), b16) for w in WIDTHS]
+        + [pltpu.VMEM((2, per_dev // 2, share, w), b16) for w in WIDTHS]
+        + [
+            pltpu.VMEM((split, images, share, local), b16),
+            pltpu.VMEM((split, images, share, local), b16),
+            pltpu.VMEM((split,) + enc_out.shape, b16),
+            pltpu.VMEM((images, share, width), b16),
+            dma((5 * split,)),
+            dma((5 * split,)),
+            dma((count,)),
+            dma((count,)),
+            dma((count + chunks,)),
+            dma((count + chunks,)),
+            dma((4 * split,)),
+            dma((4 * split,)),
+            dma((2 * ZS + YS,)),
+            dma((2 * ZS + YS,)),
+            dma((chunks, 3 * split)),
+            dma((chunks, 3 * split)),
+            dma((2 + chunks,)),
         ],
         compiler_params=pltpu.CompilerParams(
-            collective_id=1, has_side_effects=True, vmem_limit_bytes=48 * 2**20
+            collective_id=0, has_side_effects=True, vmem_limit_bytes=61 * 2**20
         ),
-        name="decode",
-    )(far, own, weights, head_rows, depth_tiles, pose_own, poses, partner_tile, partner_row)
+        name="pair_step",
+    )(
+        pick,
+        patches,
+        enc_proj,
+        enc_out,
+        embed,
+        weights,
+        pose,
+        head_rows,
+        depth_tiles,
+        pose_own,
+        partner_tile,
+        partner_row,
+    )
 
 
 def shards(
@@ -1017,7 +1047,20 @@
     shift_z = ((here // 2) % ZS - (owner // 2) % ZS) % ZS
     shift_core = (here - owner) % 2
     pick = ((shift_core * YS + shift_y) * ZS + shift_z) * images + flat_partner % images
-    far_rows, own_rows, weights_full, pose_tiles = exchange(
+    head_rows = jnp.pad(head_weight.T, ((0, 12), (0, 0)))
+    own_pairs = pair_count // split
+    depth_mask = jnp.stack([depths, valid_mask.astype(jnp.float32)], axis=0)
+    depth_tiles = depth_mask.reshape(2, split, own_count, token_share).transpose(1, 0, 2, 3)
+    depth_tiles = jnp.pad(
+        depth_tiles.reshape(split, 2 * own_count, token_share),
+        ((0, 0), (0, 8 - 2 * own_count), (0, 128 - token_share)),
+    )
+    pose_own = lax.dynamic_slice_in_dim(camera_poses, place * own_count, own_count, 1)
+    pose_own = jnp.pad(jnp.repeat(pose_own.T, K, axis=0), ((0, 0), (0, 116)))
+    own_partner = lax.dynamic_slice_in_dim(flat_partner, place * own_pairs, own_pairs, 0)
+    partner_tile = jnp.broadcast_to(own_partner[:, None], (own_pairs, 128))
+    partner_row = jnp.broadcast_to(jnp.pad(own_partner, (0, 128 - own_pairs))[None], (8, 128))
+    results, total = pair_step(
         pick,
         patches.reshape(images, split, token_share, model_width),
         jnp.transpose(encoder_proj, (1, 0, 2)),
@@ -1025,34 +1068,13 @@
         decoder_embed,
         weights,
         pose_tile,
-        pair_count,
-        groups,
-        split,
-    )
-    head_rows = jnp.pad(head_weight.T, ((0, 12), (0, 0)))
-    own_pairs = pair_count // split
-    depth_mask = jnp.stack([depths, valid_mask.astype(jnp.float32)], axis=0)
-    depth_tiles = depth_mask.reshape(2, split, own_count, token_share).transpose(1, 0, 2, 3)
-    depth_tiles = jnp.pad(
-        depth_tiles.reshape(split, 2 * own_count, token_share),
-        ((0, 0), (0, 8 - 2 * own_count), (0, 128 - token_share)),
-    )
-    pose_own = lax.dynamic_slice_in_dim(camera_poses, place * own_count, own_count, 1)
-    pose_own = jnp.pad(jnp.repeat(pose_own.T, K, axis=0), ((0, 0), (0, 116)))
-    own_partner = lax.dynamic_slice_in_dim(flat_partner, place * own_pairs, own_pairs, 0)
-    partner_tile = jnp.broadcast_to(own_partner[:, None], (own_pairs, 128))
-    partner_row = jnp.broadcast_to(jnp.pad(own_partner, (0, 128 - own_pairs))[None], (8, 128))
-    results, total = decode(
-        far_rows.reshape(own_pairs * tokens, dec_width),
-        own_rows.reshape(own_count * tokens, dec_width),
-        weights_full.reshape(4, dec_width, dec_width),
         head_rows,
         depth_tiles,
         pose_own,
-        pose_tiles,
         partner_tile,
         partner_row,
-        own_pairs,
+        pair_count,
+        groups,
     )
     pointmap = results[:, : 4 * own_pairs, :token_share].reshape(split, 4, own_pairs, token_share)
     pointmap = pointmap.transpose(1, 0, 2, 3).reshape(4, pair_count, token_share)

time: 160 us -> 158 us (0.988)
  Pallas kernels: 148 us -> 144 us
  local copies, waits for them, and re-layouts: 7.32 us -> 9.04 us
    pallas_call x2 -> x1, Pallas kernels: 148 us -> 144 us  [pair_step(): pl.pallas_call(exchange_kernel, out_shape=(jax.ShapeDtypeStruct((split, r...]
    unnamed x17 -> x11, local copies, waits for them, and re-layouts: 5.05 us -> 1.48 us
where the time goes in v7:
time: 158 us
  Pallas kernels  144 us (91%)
  local copies, waits for them, and re-layouts  9.04 us (6%)
  other arithmetic  3.78 us (2%)
    pallas_call x1, Pallas kernels, pair_step(): pl.pallas_call(exchange_kernel, out_shape=(jax.ShapeDtypeStruct((split, r...  144 us

profile of v7, /device:TPU:1, one launch (start us, length us, event | category | flops | bytes accessed | tf_op | source)
XLA Modules:
  0.0 157.9 jit_solution(2115010811963671009)
XLA Ops:
  0.7 0.8 reshape.37
  1.4 0.6 fusion.2.pick_ref
  2.0 0.1 dynamic_slice.10
  2.1 0.7 broadcast_in_dim.20.partner_ref
  2.7 0.6 broadcast_in_dim.21.partner_row_ref
  3.3 0.7 dynamic-slice_bitcast_fusion
  4.0 0.6 pad.23.pose_own_ref
  4.6 0.0 copy-start.2
  4.6 0.0 copy-start.3
  4.6 0.0 copy-start.1
  4.6 0.0 copy-start
  4.6 2.4 %pad_maximum_fusion.weights_ref = bf16[4,192,768]{2,1,0:T(8,128)(2,1)} fusion(bf16[1,192,768]{2,1,0:T(8,128)(2,1)} %bitcast.30, bf16[3,192,768]{2,1,0:T(8,128)(2,1)} %bitcast.26), kind=kLoop, calls=%fused_computation | loop fusion | flops 589824 | bytes 2359296 | tf_op jit(solution)/shard_map/concatenate | solution.py:1039
  7.1 0.0 copy-done.2
  7.1 0.0 copy-done.3
  7.1 0.6 pad.22.depth_ref
  7.7 0.0 copy-done.1
  7.7 0.6 pad.21.head_ref
  8.3 0.0 copy-done
  8.3 0.1 copy.27
  8.4 0.6 pad.20.pose_ref
  9.0 144.4 %pair_step.1 = (f32[4,72,128]{2,1,0:T(8,128)}, f32[16,128]{1,0:T(8,128)}) custom-call(s32[64]{0:T(128)} %fusion.2.pick_ref, bf16[8,4,24,1024]{3,2,1,0:T(8,128)(2,1)} %bitcast.24, bf16[3,1024,256]{2,1,0:T(8,128)(2,1)} %bitcast.25, bf16[4,64,1024]{2,1,0:T(8,128)(2,1)} %bitcast.27, bf16[1024,768]{1,0:T(8,128)(2,1)} %embed_ref.1, ...), custom_call_target="tpu_custom_call" | custom-call | tf_op jit(solution)/shard_map/pair_step/pallas_call | solution.py:943
  153.4 0.9 slice.6
  154.4 0.7 copy.32
  155.1 0.1 copy.31
  155.1 0.8 multiply_subtract_fusion
  155.9 0.7 copy.33
  156.6 1.3 slice.7
  (6 shorter events, 0.0 us)
Async XLA Ops:
  4.6 2.4 %copy-start.2 = (s32[8,24]{1,0:T(8,128)S(1)}, s32[8,24]{1,0:T(8,128)}, u32[]{:S(2)}) copy-start(s32[8,24]{1,0:T(8,128)} %param.21) | copy-start | bytes 2308
  4.6 2.4 %copy-start.3 = (f32[8,24]{1,0:T(8,128)S(1)}, f32[8,24]{1,0:T(8,128)}, u32[]{:S(2)}) copy-start(f32[8,24]{1,0:T(8,128)} %param.19) | copy-start | bytes 2308
  4.6 3.1 %copy-start.1 = (bf16[768,4]{0,1:T(4,128)(2,1)S(1)}, bf16[768,4]{0,1:T(4,128)(2,1)}, u32[]{:S(2)}) copy-start(bf16[768,4]{0,1:T(4,128)(2,1)} %param.17) | copy-start | bytes 18436
  4.6 3.7 %copy-start = (f32[12,8]{0,1:T(8,128)S(1)}, f32[12,8]{0,1:T(8,128)}, u32[]{:S(2)}) copy-start(f32[12,8]{0,1:T(8,128)} %param.20) | copy-start | bytes 1156

commit v8 on v7

--- a/solution.py
+++ b/solution.py
@@ -113,12 +113,9 @@
     enc_out_ref,
     embed_ref,
     weights_ref,
-    pose_ref,
     head_ref,
-    depth_ref,
-    pose_own_ref,
-    partner_ref,
-    partner_row_ref,
+    floats_ref,
+    ints_ref,
     result_ref,
     total_ref,
     far_ref,
@@ -196,7 +193,7 @@
     ]
     for peer in peers:
         pl.semaphore_signal(barrier, inc=1, device_id=peer, device_id_type=MESH)
-    pose_all[here] = pose_ref[...]
+    pose_all[here] = floats_ref[2 * split].astype(jnp.bfloat16)
     pl.semaphore_wait(barrier, len(peers))
 
     def remote(source, target, send, recv, device):
@@ -567,6 +564,18 @@
         out_relay(step, behind(step)).wait_send()
         weight_copy(step, me).wait_send()
         weight_relay(step, behind(step)).wait_send()
+    rest = decode_part(
+        far_ref,
+        own_ref,
+        weights_all,
+        head_ref,
+        floats_ref,
+        pose_all,
+        ints_ref,
+        result_ref,
+        total_ref,
+        *finish,
+    )
     for chunk in range(chunks):
         far_local(chunk).wait()
         for step in (1, 3):
@@ -575,20 +584,7 @@
             far_direct(chunk, step, me).wait_send()
             far_onward(chunk, step, behind(2)).wait_recv()
             far_onward(chunk, step, behind(step)).wait_send()
-    decode_part(
-        far_ref,
-        own_ref,
-        weights_all,
-        head_ref,
-        depth_ref,
-        pose_own_ref,
-        pose_all,
-        partner_ref,
-        partner_row_ref,
-        result_ref,
-        total_ref,
-        *finish,
-    )
+    rest()
 
 
 def decode_part(
@@ -596,11 +592,9 @@
     own_ref,
     weights_ref,
     head_ref,
-    depth_ref,
-    pose_own_ref,
+    floats_ref,
     pose_all_ref,
-    partner_ref,
-    partner_row_ref,
+    ints_ref,
     result_ref,
     total_ref,
     queries,
@@ -679,24 +673,9 @@
             queries[image, block, :tokens] = jnp.where(first_half, part, zero)
             queries[image, block, tokens:] = jnp.where(first_half, zero, part)
 
-    chunk = 4 * tokens
-
-    def project(step, carry):
-        span = pl.ds(pl.multiple_of(step * chunk, chunk), chunk)
-        part = far_ref[pl.ds(step * 4, 4)].astype(jnp.float32)
-        part = part.reshape(chunk, width).astype(jnp.bfloat16)
-        keys[span, :] = lax.dot_general(
-            part, weight(1), last, preferred_element_type=jnp.float32
-        ).astype(jnp.bfloat16)
-        values[span, :] = lax.dot_general(
-            part, weight(2), last, preferred_element_type=jnp.float32
-        ).astype(jnp.bfloat16)
-        return carry
-
-    lax.fori_loop(0, pairs // 4, project, 0, unroll=2)
     def depth_copy(step, slot):
         return remote(
-            depth_ref.at[lax.rem(me + step, split)],
+            floats_ref.at[split + lax.rem(me + step, split)],
             depth_all.at[slot],
             x_send.at[step],
             x_recv.at[step],
@@ -705,12 +684,13 @@
 
     for step in range(1, split):
         depth_copy(step, me).start()
-    depth_all[me] = depth_ref[me]
+    depth_all[me] = floats_ref[split + me]
+    own_partner = ints_ref[me, :pairs]
     staging[...] = jnp.zeros_like(staging)
     members = own_count * split
     group_count, pose_rows, _ = pose_all_ref.shape
     lane_ids = lax.broadcasted_iota(jnp.int32, (pairs, 128), 1)
-    chosen = (lane_ids == lax.rem(partner_ref[...], members)).astype(jnp.bfloat16)
+    chosen = (lane_ids == lax.rem(own_partner, members)).astype(jnp.bfloat16)
     candidates = lax.dot_general(
         pose_all_ref[...].reshape(group_count * pose_rows, 128),
         chosen,
@@ -718,7 +698,7 @@
         preferred_element_type=jnp.float32,
     ).reshape(group_count, pose_rows, pairs)
     owners = lax.broadcasted_iota(jnp.int32, (group_count, pose_rows, pairs), 0)
-    held_by = lax.div(partner_row_ref[:1, :pairs], members)
+    held_by = lax.div(ints_ref[me, pairs : pairs + 1, :pairs], members)
     turned = jnp.sum(jnp.where(owners == held_by[None], candidates, 0.0), axis=0)
     same = lax.broadcasted_iota(jnp.int32, (pose_rows, pose_rows), 0) == lax.broadcasted_iota(
         jnp.int32, (pose_rows, pose_rows), 1
@@ -729,187 +709,206 @@
         (((0,), (0,)), ((), ())),
         preferred_element_type=jnp.float32,
     )
-    ones = jnp.ones((tokens, 128), jnp.bfloat16)
-
-    def attend(pair, carry):
-        span = pl.ds(pl.multiple_of(pair * tokens, tokens), tokens)
-        image = pair // per_image
-        columns = [slice(block * 128, (block + 1) * 128) for block in range(blocks)]
-        scores = [
-            lax.dot_general(
-                queries[image, block], keys[span, part], last, preferred_element_type=jnp.float32
+
+    def rest():
+        chunk = 4 * tokens
+
+        def project(step, carry):
+            span = pl.ds(pl.multiple_of(step * chunk, chunk), chunk)
+            part = far_ref[pl.ds(step * 4, 4)].astype(jnp.float32)
+            part = part.reshape(chunk, width).astype(jnp.bfloat16)
+            keys[span, :] = lax.dot_general(
+                part, weight(1), last, preferred_element_type=jnp.float32
+            ).astype(jnp.bfloat16)
+            values[span, :] = lax.dot_general(
+                part, weight(2), last, preferred_element_type=jnp.float32
+            ).astype(jnp.bfloat16)
+            return carry
+
+        lax.fori_loop(0, pairs // 4, project, 0, unroll=2)
+        ones = jnp.ones((tokens, 128), jnp.bfloat16)
+
+        def attend(pair, carry):
+            span = pl.ds(pl.multiple_of(pair * tokens, tokens), tokens)
+            image = pair // per_image
+            columns = [slice(block * 128, (block + 1) * 128) for block in range(blocks)]
+            scores = [
+                lax.dot_general(
+                    queries[image, block], keys[span, part], last, preferred_element_type=jnp.float32
+                )
+                for block, part in enumerate(columns)
+            ]
+            expos = [
+                jnp.exp(each - jnp.max(each, axis=1, keepdims=True)).astype(jnp.bfloat16)
+                for each in scores
+            ]
+            sums = [
+                jnp.dot(
+                    each,
+                    jnp.concatenate([values[span, part], ones], axis=1),
+                    preferred_element_type=jnp.float32,
+                )
+                for each, part in zip(expos, columns)
+            ]
+            for each, part in zip(sums, columns):
+                got = each[:, :128] / each[:, 128:]
+                mixed[span, part] = jnp.where(first_half, got[:tokens], got[tokens:]).astype(
+                    jnp.bfloat16
+                )
+            return carry
+
+        lax.fori_loop(0, pairs, attend, 0, unroll=2)
+
+        def finish(step, carry):
+            span = pl.ds(pl.multiple_of(step * chunk, chunk), chunk)
+            image = step * 4 // per_image
+            own = own_ref[image].astype(jnp.float32).reshape(tokens, width)
+            settled = jnp.dot(mixed[span, :], weight(3), preferred_element_type=jnp.float32)
+            settled = settled + jnp.concatenate([own] * 4, axis=0)
+            heads = lax.dot_general(
+                head_ref[...], norm_rows(settled), last, preferred_element_type=jnp.float32
             )
-            for block, part in enumerate(columns)
-        ]
-        expos = [
-            jnp.exp(each - jnp.max(each, axis=1, keepdims=True)).astype(jnp.bfloat16)
-            for each in scores
-        ]
-        sums = [
-            jnp.dot(
-                each,
-                jnp.concatenate([values[span, part], ones], axis=1),
-                preferred_element_type=jnp.float32,
+            for part in range(4):
+                heads_all[step * 4 + part] = heads[:, part * tokens : (part + 1) * tokens]
+            return carry
+
+        lax.fori_loop(0, pairs // 4, finish, 0, unroll=2)
+        for step in range(1, split):
+            depth_copy(step, behind(step)).wait_recv()
+
+        def widen(offset):
+            both = jnp.concatenate(
+                [depth_all[q, offset : offset + own_count, :share] for q in range(split)], axis=1
             )
-            for each, part in zip(expos, columns)
-        ]
-        for each, part in zip(sums, columns):
-            got = each[:, :128] / each[:, 128:]
-            mixed[span, part] = jnp.where(first_half, got[:tokens], got[tokens:]).astype(
-                jnp.bfloat16
+            return jnp.concatenate(
+                [
+                    jnp.broadcast_to(both[image : image + 1], (per_image, tokens))
+                    for image in range(own_count)
+                ],
+                axis=0,
             )
-        return carry
-
-    lax.fori_loop(0, pairs, attend, 0, unroll=2)
-
-    def finish(step, carry):
-        span = pl.ds(pl.multiple_of(step * chunk, chunk), chunk)
-        image = step * 4 // per_image
-        own = own_ref[image].astype(jnp.float32).reshape(tokens, width)
-        settled = jnp.dot(mixed[span, :], weight(3), preferred_element_type=jnp.float32)
-        settled = settled + jnp.concatenate([own] * 4, axis=0)
-        heads = lax.dot_general(
-            head_ref[...], norm_rows(settled), last, preferred_element_type=jnp.float32
-        )
-        for part in range(4):
-            heads_all[step * 4 + part] = heads[:, part * tokens : (part + 1) * tokens]
-        return carry
-
-    lax.fori_loop(0, pairs // 4, finish, 0, unroll=2)
-    for step in range(1, split):
-        depth_copy(step, behind(step)).wait_recv()
-
-    def widen(offset):
-        both = jnp.concatenate(
-            [depth_all[q, offset : offset + own_count, :share] for q in range(split)], axis=1
-        )
-        return jnp.concatenate(
+
+        depth = widen(0)
+        valid = widen(own_count)
+        token = lax.broadcasted_iota(jnp.int32, (1, tokens), 1)
+        ray_x = (lax.rem(token, 16).astype(jnp.float32) - 7.5) * 0.125
+        ray_y = (lax.div(token, 16).astype(jnp.float32) - (tokens // 16 - 1) * 0.5) * 0.125
+        rays = [ray_x, ray_y, jnp.ones_like(ray_x)]
+        points = [heads_all[:, component, :] for component in range(3)]
+        confidence = 1.0 + jnp.exp(heads_all[:, 3, :])
+        factor = valid * confidence * (2.0 / tokens)
+        own_pose = floats_ref[me]
+        lane128 = lax.broadcasted_iota(jnp.int32, (pairs, 128), 1)
+        own_grad = jnp.zeros((pairs, 128), jnp.float32)
+        far_grad = jnp.zeros((pairs, 128), jnp.float32)
+        depth_grad = jnp.zeros((pairs, tokens), jnp.float32)
+        for component in range(3):
+            base = 4 * component
+            direction = sum(own_pose[:, base + k : base + k + 1] * rays[k] for k in range(3))
+            world = own_pose[:, base + 3 : base + 4] + depth * direction
+            predicted = far_pose[:, base + 3 : base + 4] + sum(
+                far_pose[:, base + k : base + k + 1] * points[k] for k in range(3)
+            )
+            slope = factor * (world - predicted)
+            depth_grad = depth_grad + slope * direction
+            scaled = slope * depth
+            for k in range(4):
+                mine = scaled * rays[k] if k < 3 else slope
+                other = slope * points[k] if k < 3 else slope
+                mine = jnp.sum(mine, axis=1, keepdims=True)
+                other = jnp.sum(other, axis=1, keepdims=True)
+                own_grad = jnp.where(lane128 == base + k, mine, own_grad)
+                far_grad = jnp.where(lane128 == base + k, -other, far_grad)
+        total_images = YS * 128
+        ids = lax.broadcasted_iota(jnp.int32, (pairs, total_images), 1)
+        pair_ids = lax.broadcasted_iota(jnp.int32, (pairs, total_images), 0)
+        own_ids = (here * split + me) * own_count + lax.div(pair_ids, per_image)
+        hits = jnp.concatenate([ids == own_ids, ids == own_partner[:, :1]], axis=0)
+        table = lax.dot_general(
+            jnp.concatenate([own_grad, far_grad], axis=0),
+            hits.astype(jnp.float32),
+            (((0,), (0,)), ((), ())),
+            precision=lax.Precision.HIGHEST,
+            preferred_element_type=jnp.float32,
+        )
+        for part in range(YS):
+            dense[part] = table[:16, part * 128 : (part + 1) * 128]
+
+        def plane_copy(number, dx, dy, slot):
+            return remote(
+                dense.at[lax.rem(y + dy, YS)],
+                plane_in.at[slot],
+                plane_send.at[number],
+                plane_recv.at[number],
+                plane_peer(dx, dy, 1),
+            )
+
+        for number, (dx, dy) in enumerate(plane):
+            plane_copy(number, dx, dy, me * YS + y).start()
+        plane_in[me * YS + y] = dense[y]
+
+        old = jnp.concatenate(
+            [depth[image * per_image : image * per_image + 1] for image in range(own_count)], axis=0
+        )
+        change = jnp.concatenate(
             [
-                jnp.broadcast_to(both[image : image + 1], (per_image, tokens))
+                jnp.sum(
+                    depth_grad[image * per_image : (image + 1) * per_image], axis=0, keepdims=True
+                )
                 for image in range(own_count)
             ],
             axis=0,
         )
-
-    depth = widen(0)
-    valid = widen(own_count)
-    token = lax.broadcasted_iota(jnp.int32, (1, tokens), 1)
-    ray_x = (lax.rem(token, 16).astype(jnp.float32) - 7.5) * 0.125
-    ray_y = (lax.div(token, 16).astype(jnp.float32) - (tokens // 16 - 1) * 0.5) * 0.125
-    rays = [ray_x, ray_y, jnp.ones_like(ray_x)]
-    points = [heads_all[:, component, :] for component in range(3)]
-    confidence = 1.0 + jnp.exp(heads_all[:, 3, :])
-    weight = valid * confidence * (2.0 / tokens)
-    own_pose = pose_own_ref[...]
-    lane128 = lax.broadcasted_iota(jnp.int32, (pairs, 128), 1)
-    own_grad = jnp.zeros((pairs, 128), jnp.float32)
-    far_grad = jnp.zeros((pairs, 128), jnp.float32)
-    depth_grad = jnp.zeros((pairs, tokens), jnp.float32)
-    for component in range(3):
-        base = 4 * component
-        direction = sum(own_pose[:, base + k : base + k + 1] * rays[k] for k in range(3))
-        world = own_pose[:, base + 3 : base + 4] + depth * direction
-        predicted = far_pose[:, base + 3 : base + 4] + sum(
-            far_pose[:, base + k : base + k + 1] * points[k] for k in range(3)
-        )
-        slope = weight * (world - predicted)
-        depth_grad = depth_grad + slope * direction
-        scaled = slope * depth
-        for k in range(4):
-            mine = scaled * rays[k] if k < 3 else slope
-            other = slope * points[k] if k < 3 else slope
-            mine = jnp.sum(mine, axis=1, keepdims=True)
-            other = jnp.sum(other, axis=1, keepdims=True)
-            own_grad = jnp.where(lane128 == base + k, mine, own_grad)
-            far_grad = jnp.where(lane128 == base + k, -other, far_grad)
-    total_images = YS * 128
-    ids = lax.broadcasted_iota(jnp.int32, (pairs, total_images), 1)
-    pair_ids = lax.broadcasted_iota(jnp.int32, (pairs, total_images), 0)
-    own_ids = (here * split + me) * own_count + lax.div(pair_ids, per_image)
-    hits = jnp.concatenate([ids == own_ids, ids == partner_ref[:, :1]], axis=0)
-    table = lax.dot_general(
-        jnp.concatenate([own_grad, far_grad], axis=0),
-        hits.astype(jnp.float32),
-        (((0,), (0,)), ((), ())),
-        precision=lax.Precision.HIGHEST,
-        preferred_element_type=jnp.float32,
-    )
-    for part in range(YS):
-        dense[part] = table[:16, part * 128 : (part + 1) * 128]
-
-    def plane_copy(number, dx, dy, slot):
-        return remote(
-            dense.at[lax.rem(y + dy, YS)],
-            plane_in.at[slot],
-            plane_send.at[number],
-            plane_recv.at[number],
-            plane_peer(dx, dy, 1),
-        )
-
-    for number, (dx, dy) in enumerate(plane):
-        plane_copy(number, dx, dy, me * YS + y).start()
-    plane_in[me * YS + y] = dense[y]
-
-    old = jnp.concatenate(
-        [depth[image * per_image : image * per_image + 1] for image in range(own_count)], axis=0
-    )
-    change = jnp.concatenate(
-        [
-            jnp.sum(
-                depth_grad[image * per_image : (image + 1) * per_image], axis=0, keepdims=True
+        moved = old - depth_step * change
+        for place in range(split):
+            span = slice(place * share, (place + 1) * share)
+            for component, values_now in enumerate(points + [confidence]):
+                staging[place, component * pairs : (component + 1) * pairs, :share] = values_now[:, span]
+            staging[place, 4 * pairs : 4 * pairs + own_count, :share] = moved[:, span]
+
+        def result_copy(step, slot):
+            return remote(
+                staging.at[lax.rem(me + step, split)],
+                result_ref.at[slot],
+                x_send.at[split + step],
+                x_recv.at[split + step],
+                mate(step),
             )
-            for image in range(own_count)
-        ],
-        axis=0,
-    )
-    moved = old - depth_step * change
-    for place in range(split):
-        span = slice(place * share, (place + 1) * share)
-        for component, values_now in enumerate(points + [confidence]):
-            staging[place, component * pairs : (component + 1) * pairs, :share] = values_now[:, span]
-        staging[place, 4 * pairs : 4 * pairs + own_count, :share] = moved[:, span]
-
-    def result_copy(step, slot):
-        return remote(
-            staging.at[lax.rem(me + step, split)],
-            result_ref.at[slot],
-            x_send.at[split + step],
-            x_recv.at[split + step],
-            mate(step),
-        )
-
-    for step in range(1, split):
-        result_copy(step, me).start()
-    result_ref[me] = staging[me]
-    for number, (dx, dy) in enumerate(plane):
-        source = lax.rem(me + split - dx, split) * YS + lax.rem(y + YS - dy, YS)
-        plane_copy(number, dx, dy, source).wait_recv()
-    gathered = jnp.sum(plane_in[...], axis=0)
-    part_sum[...] = gathered
-    line_in[row] = gathered
-
-    def line_copy(number, dz, dc, slot):
-        return remote(
-            part_sum,
-            line_in.at[slot],
-            line_send.at[number],
-            line_recv.at[number],
-            (y * rows_count + line_row(dz, dc, 1), me),
-        )
-
-    for number, (dz, dc) in enumerate(line):
-        line_copy(number, dz, dc, row).start()
-    for number, (dz, dc) in enumerate(line):
-        line_copy(number, dz, dc, line_row(dz, dc, -1)).wait_recv()
-    total_ref[...] = jnp.sum(line_in[...], axis=0)
-    for step in range(1, split):
-        depth_copy(step, me).wait_send()
-        result_copy(step, behind(step)).wait_recv()
-        result_copy(step, me).wait_send()
-    for number, (dx, dy) in enumerate(plane):
-        plane_copy(number, dx, dy, me * YS + y).wait_send()
-    for number, (dz, dc) in enumerate(line):
-        line_copy(number, dz, dc, row).wait_send()
+
+        for step in range(1, split):
+            result_copy(step, me).start()
+        result_ref[me] = staging[me]
+        for number, (dx, dy) in enumerate(plane):
+            source = lax.rem(me + split - dx, split) * YS + lax.rem(y + YS - dy, YS)
+            plane_copy(number, dx, dy, source).wait_recv()
+        gathered = jnp.sum(plane_in[...], axis=0)
+        part_sum[...] = gathered
+        line_in[row] = gathered
+
+        def line_copy(number, dz, dc, slot):
+            return remote(
+                part_sum,
+                line_in.at[slot],
+                line_send.at[number],
+                line_recv.at[number],
+                (y * rows_count + line_row(dz, dc, 1), me),
+            )
+
+        for number, (dz, dc) in enumerate(line):
+            line_copy(number, dz, dc, row).start()
+        for number, (dz, dc) in enumerate(line):
+            line_copy(number, dz, dc, line_row(dz, dc, -1)).wait_recv()
+        total_ref[...] = jnp.sum(line_in[...], axis=0)
+        for step in range(1, split):
+            depth_copy(step, me).wait_send()
+            result_copy(step, behind(step)).wait_recv()
+            result_copy(step, me).wait_send()
+        for number, (dx, dy) in enumerate(plane):
+            plane_copy(number, dx, dy, me * YS + y).wait_send()
+        for number, (dz, dc) in enumerate(line):
+            line_copy(number, dz, dc, row).wait_send()
+
+    return rest
 
 
 def pair_step(
@@ -919,12 +918,9 @@
     enc_out,
     embed,
     weights,
-    pose,
     head_rows,
-    depth_tiles,
-    pose_own,
-    partner_tile,
-    partner_row,
+    floats,
+    ints,
     pairs,
     groups,
 ):
@@ -946,19 +942,19 @@
             jax.ShapeDtypeStruct((split, result_rows, 128), f32),
             jax.ShapeDtypeStruct((16, 128), f32),
         ),
-        in_specs=[pl.BlockSpec(memory_space=pltpu.SMEM)] + [vmem] * 11,
+        in_specs=[pl.BlockSpec(memory_space=pltpu.SMEM)] + [vmem] * 8,
         out_specs=(vmem, vmem),
         scratch_shapes=[
             pltpu.VMEM((per_dev, split, share, width), b16),
             pltpu.VMEM((own_count, split, share, width), b16),
             pltpu.VMEM((4, split) + weights.shape[1:], b16),
-            pltpu.VMEM((groups,) + pose.shape, b16),
+            pltpu.VMEM((groups, 16, 128), b16),
             pltpu.VMEM((own_count, width // 128, 2 * tokens, 128), b16),
             pltpu.VMEM((rows, width), b16),
             pltpu.VMEM((rows, width), b16),
             pltpu.VMEM((rows, width), b16),
             pltpu.VMEM((per_dev, head_rows.shape[0], tokens), f32),
-            pltpu.VMEM(depth_tiles.shape, f32),
+            pltpu.VMEM((split, 16, 128), f32),
             pltpu.VMEM((split, result_rows, 128), f32),
             pltpu.VMEM((YS, 16, 128), f32),
             pltpu.VMEM((split * YS, 16, 128), f32),
@@ -1004,12 +1000,9 @@
         enc_out,
         embed,
         weights,
-        pose,
         head_rows,
-        depth_tiles,
-        pose_own,
-        partner_tile,
-        partner_row,
+        floats,
+        ints,
     )
 
 
@@ -1030,17 +1023,12 @@
     dec_width = decoder_embed.shape[1]
     enc_local = encoder_proj.shape[2]
     split = lax.axis_size("mp")
-    place = lax.axis_index("mp")
     own_count = images // split
     flat_partner = partners.reshape(-1)
     pair_count = flat_partner.shape[0]
     groups = lax.axis_size("img")
     here = lax.axis_index("img")
     weights = jnp.concatenate([jnp.transpose(decoder_proj, (1, 2, 0)), decoder_out[None]], axis=0)
-    pose_tile = jnp.pad(
-        camera_poses.astype(jnp.bfloat16), ((0, 4), (0, 128 - camera_poses.shape[1]))
-    )
-
     token_share = tokens // split
     owner = flat_partner // images
     shift_y = (here // (2 * ZS) - owner // (2 * ZS)) % YS
@@ -1053,13 +1041,16 @@
     depth_tiles = depth_mask.reshape(2, split, own_count, token_share).transpose(1, 0, 2, 3)
     depth_tiles = jnp.pad(
         depth_tiles.reshape(split, 2 * own_count, token_share),
-        ((0, 0), (0, 8 - 2 * own_count), (0, 128 - token_share)),
+        ((0, 0), (0, 16 - 2 * own_count), (0, 128 - token_share)),
     )
-    pose_own = lax.dynamic_slice_in_dim(camera_poses, place * own_count, own_count, 1)
-    pose_own = jnp.pad(jnp.repeat(pose_own.T, K, axis=0), ((0, 0), (0, 116)))
-    own_partner = lax.dynamic_slice_in_dim(flat_partner, place * own_pairs, own_pairs, 0)
-    partner_tile = jnp.broadcast_to(own_partner[:, None], (own_pairs, 128))
-    partner_row = jnp.broadcast_to(jnp.pad(own_partner, (0, 128 - own_pairs))[None], (8, 128))
+    pose_own = jnp.repeat(camera_poses.T, K, axis=0).reshape(split, own_pairs, 12)
+    pose_own = jnp.pad(pose_own, ((0, 0), (0, 0), (0, 116)))
+    pose_tile = jnp.pad(camera_poses, ((0, 4), (0, 128 - images)))[None]
+    floats = jnp.concatenate([pose_own, depth_tiles, pose_tile], axis=0)
+    parted = flat_partner.reshape(split, own_pairs)
+    columns = jnp.broadcast_to(parted[:, :, None], (split, own_pairs, 128))
+    lines = jnp.broadcast_to(jnp.pad(parted, ((0, 0), (0, 112)))[:, None], (split, 8, 128))
+    ints = jnp.concatenate([columns, lines], axis=1)
     results, total = pair_step(
         pick,
         patches.reshape(images, split, token_share, model_width),
@@ -1067,12 +1058,9 @@
         encoder_out.reshape(4, enc_local // 4, model_width),
         decoder_embed,
         weights,
-        pose_tile,
         head_rows,
-        depth_tiles,
-        pose_own,
-        partner_tile,
-        partner_row,
+        floats,
+        ints,
         pair_count,
         groups,
     )

time: 158 us -> 159 us (level)
  other arithmetic: 3.78 us -> 6.36 us
    pad x4 -> x1, local copies, waits for them, and re-layouts: 1.82 us -> 0.01 us  [shards(): jnp.pad(parted, ((0, 0), (0, 112)))[:, None]]
where the time goes in v8:
time: 159 us; the launch traced here: 158 us
  Pallas kernels  143 us (90%)
  local copies, waits for them, and re-layouts  7.99 us (5%)
  other arithmetic  6.36 us (4%)
    pallas_call x1, Pallas kernels, pair_step(): pl.pallas_call(exchange_kernel, out_shape=(jax.ShapeDtypeStruct((split, r...  143 us

profile of v8, /device:TPU:1, one launch (start us, length us, event | category | flops | bytes accessed | tf_op | source)
XLA Modules:
  0.0 158.5 jit_solution(16362130531871809872)
XLA Ops:
  0.7 0.8 reshape.34
  1.4 0.6 fusion.4.pick_ref
  2.0 0.8 broadcast_in_dim.25
  2.8 0.7 convert_element_type.11
  3.5 0.7 pad_maximum_fusion.1
  4.2 0.8 copy.22
  4.9 1.3 pad.20.head_ref
  6.2 0.1 broadcast_in_dim.26
  6.3 0.6 pad_add_fusion.ints_ref
  6.9 0.7 broadcast_in_dim.23
  7.6 0.6 fusion.floats_ref
  8.3 2.4 %pad_maximum_fusion.weights_ref = bf16[4,192,768]{2,1,0:T(8,128)(2,1)} fusion(bf16[1,192,768]{2,1,0:T(8,128)(2,1)} %bitcast.30, bf16[3,192,768]{2,1,0:T(8,128)(2,1)} %bitcast.26), kind=kLoop, calls=%fused_computation | loop fusion | flops 589824 | bytes 2359296 | tf_op jit(solution)/shard_map/concatenate | solution.py:1031
  10.6 143.4 %pair_step.1 = (f32[4,72,128]{2,1,0:T(8,128)}, f32[16,128]{1,0:T(8,128)}) custom-call(s32[64]{0:T(128)} %fusion.4.pick_ref, bf16[8,4,24,1024]{3,2,1,0:T(8,128)(2,1)} %bitcast.24, bf16[3,1024,256]{2,1,0:T(8,128)(2,1)} %bitcast.25, bf16[4,64,1024]{2,1,0:T(8,128)(2,1)} %bitcast.29, bf16[1024,768]{1,0:T(8,128)(2,1)} %embed_ref.1, ...), custom_call_target="tpu_custom_call" | custom-call | tf_op jit(solution)/shard_map/pair_step/pallas_call | solution.py:939
  154.0 0.8 multiply_subtract_fusion
  154.8 0.7 copy.26
  155.5 1.3 slice.7
  156.8 0.9 slice.6
  157.7 0.7 copy.25
  (4 shorter events, 0.0 us)

commit v9 on v8

--- a/solution.py
+++ b/solution.py
@@ -114,7 +114,9 @@
     embed_ref,
     weights_ref,
     head_ref,
-    floats_ref,
+    depth_ref,
+    valid_ref,
+    poses_ref,
     ints_ref,
     result_ref,
     total_ref,
@@ -125,6 +127,7 @@
     *scratch,
 ):
     finish, scratch = scratch[:17], scratch[17:]
+    floats_ref, scratch = scratch[0], scratch[1:]
     chunks = len(WIDTHS)
     held, scratch = scratch[:chunks], scratch[chunks:]
     staged, scratch = scratch[:chunks], scratch[chunks:]
@@ -193,7 +196,16 @@
     ]
     for peer in peers:
         pl.semaphore_signal(barrier, inc=1, device_id=peer, device_id_type=MESH)
-    pose_all[here] = floats_ref[2 * split].astype(jnp.bfloat16)
+    floats_ref[...] = jnp.zeros_like(floats_ref)
+    floats_ref[split, : poses_ref.shape[0], : poses_ref.shape[1]] = poses_ref[...]
+    pair_count = images // split
+    for quarter in range(split):
+        lines = slice(quarter * pair_count, (quarter + 1) * pair_count)
+        floats_ref[quarter, :pair_count, :share] = depth_ref[lines, :]
+        floats_ref[quarter, pair_count : 2 * pair_count, :share] = valid_ref[lines, :].astype(
+            jnp.float32
+        )
+    pose_all[here] = floats_ref[split].astype(jnp.bfloat16)
     pl.semaphore_wait(barrier, len(peers))
 
     def remote(source, target, send, recv, device):
@@ -675,7 +687,7 @@
 
     def depth_copy(step, slot):
         return remote(
-            floats_ref.at[split + lax.rem(me + step, split)],
+            floats_ref.at[lax.rem(me + step, split)],
             depth_all.at[slot],
             x_send.at[step],
             x_recv.at[step],
@@ -684,7 +696,7 @@
 
     for step in range(1, split):
         depth_copy(step, me).start()
-    depth_all[me] = floats_ref[split + me]
+    depth_all[me] = floats_ref[me]
     own_partner = ints_ref[me, :pairs]
     staging[...] = jnp.zeros_like(staging)
     members = own_count * split
@@ -797,8 +809,15 @@
         points = [heads_all[:, component, :] for component in range(3)]
         confidence = 1.0 + jnp.exp(heads_all[:, 3, :])
         factor = valid * confidence * (2.0 / tokens)
-        own_pose = floats_ref[me]
         lane128 = lax.broadcasted_iota(jnp.int32, (pairs, 128), 1)
+        mine_ids = me * own_count + lax.div(lax.broadcasted_iota(jnp.int32, (pairs, 128), 0), per_image)
+        own_pose = lax.dot_general(
+            (lane128 == mine_ids).astype(jnp.float32),
+            floats_ref[split],
+            last,
+            precision=lax.Precision.HIGHEST,
+            preferred_element_type=jnp.float32,
+        )
         own_grad = jnp.zeros((pairs, 128), jnp.float32)
         far_grad = jnp.zeros((pairs, 128), jnp.float32)
         depth_grad = jnp.zeros((pairs, tokens), jnp.float32)
@@ -919,7 +938,9 @@
     embed,
     weights,
     head_rows,
-    floats,
+    depths,
+    valid,
+    poses,
     ints,
     pairs,
     groups,
@@ -942,7 +963,7 @@
             jax.ShapeDtypeStruct((split, result_rows, 128), f32),
             jax.ShapeDtypeStruct((16, 128), f32),
         ),
-        in_specs=[pl.BlockSpec(memory_space=pltpu.SMEM)] + [vmem] * 8,
+        in_specs=[pl.BlockSpec(memory_space=pltpu.SMEM)] + [vmem] * 10,
         out_specs=(vmem, vmem),
         scratch_shapes=[
             pltpu.VMEM((per_dev, split, share, width), b16),
@@ -967,6 +988,7 @@
             dma((2 * ZS,)),
             dma((2 * ZS,)),
         ]
+        + [pltpu.VMEM((split + 1, 16, 128), f32)]
         + [pltpu.VMEM((groups * images, share, w), b16) for w in WIDTHS]
         + [pltpu.VMEM((pairs, share, w), b16) for w in WIDTHS]
         + [pltpu.VMEM((2, per_dev // 2, share, w), b16) for w in WIDTHS]
@@ -1001,7 +1023,9 @@
         embed,
         weights,
         head_rows,
-        floats,
+        depths,
+        valid,
+        poses,
         ints,
     )
 
@@ -1037,16 +1061,6 @@
     pick = ((shift_core * YS + shift_y) * ZS + shift_z) * images + flat_partner % images
     head_rows = jnp.pad(head_weight.T, ((0, 12), (0, 0)))
     own_pairs = pair_count // split
-    depth_mask = jnp.stack([depths, valid_mask.astype(jnp.float32)], axis=0)
-    depth_tiles = depth_mask.reshape(2, split, own_count, token_share).transpose(1, 0, 2, 3)
-    depth_tiles = jnp.pad(
-        depth_tiles.reshape(split, 2 * own_count, token_share),
-        ((0, 0), (0, 16 - 2 * own_count), (0, 128 - token_share)),
-    )
-    pose_own = jnp.repeat(camera_poses.T, K, axis=0).reshape(split, own_pairs, 12)
-    pose_own = jnp.pad(pose_own, ((0, 0), (0, 0), (0, 116)))
-    pose_tile = jnp.pad(camera_poses, ((0, 4), (0, 128 - images)))[None]
-    floats = jnp.concatenate([pose_own, depth_tiles, pose_tile], axis=0)
     parted = flat_partner.reshape(split, own_pairs)
     columns = jnp.broadcast_to(parted[:, :, None], (split, own_pairs, 128))
     lines = jnp.broadcast_to(jnp.pad(parted, ((0, 0), (0, 112)))[:, None], (split, 8, 128))
@@ -1059,7 +1073,9 @@
         decoder_embed,
         weights,
         head_rows,
-        floats,
+        depths,
+        valid_mask,
+        camera_poses,
         ints,
         pair_count,
         groups,

time: 159 us -> 157 us (0.987)
  other arithmetic: 6.36 us -> 4.33 us
where the time goes in v9:
time: 157 us; the launch traced here: 156 us
  Pallas kernels  144 us (92%)
  local copies, waits for them, and re-layouts  7.89 us (5%)
  other arithmetic  4.33 us (3%)
    pallas_call x1, Pallas kernels, pair_step(): pl.pallas_call(exchange_kernel, out_shape=(jax.ShapeDtypeStruct((split, r...  144 us

profile of v9, /device:TPU:1, one launch (start us, length us, event | category | flops | bytes accessed | tf_op | source)
XLA Modules:
  0.0 156.5 jit_solution(12972900907259572510)
XLA Ops:
  0.7 0.8 reshape.26
  1.4 0.6 fusion.2.pick_ref
  2.0 0.8 broadcast_in_dim.17
  2.8 1.4 copy.18.poses_ref
  4.1 1.3 pad.8.head_ref
  5.4 0.1 broadcast_in_dim.18
  5.5 0.6 pad_add_fusion.ints_ref
  6.1 2.4 %pad_maximum_fusion.weights_ref = bf16[4,192,768]{2,1,0:T(8,128)(2,1)} fusion(bf16[1,192,768]{2,1,0:T(8,128)(2,1)} %bitcast.17, bf16[3,192,768]{2,1,0:T(8,128)(2,1)} %bitcast.13), kind=kLoop, calls=%fused_computation | loop fusion | flops 589824 | bytes 2359296 | tf_op jit(solution)/shard_map/concatenate | solution.py:1055
  8.5 0.0 copy-start
  8.5 143.5 %pair_step.1 = (f32[4,72,128]{2,1,0:T(8,128)}, f32[16,128]{1,0:T(8,128)}) custom-call(s32[64]{0:T(128)} %fusion.2.pick_ref, bf16[8,4,24,1024]{3,2,1,0:T(8,128)(2,1)} %bitcast.11, bf16[3,1024,256]{2,1,0:T(8,128)(2,1)} %bitcast.12, bf16[4,64,1024]{2,1,0:T(8,128)(2,1)} %bitcast.14, bf16[1024,768]{1,0:T(8,128)(2,1)} %embed_ref.1, ...), custom_call_target="tpu_custom_call" | custom-call | tf_op jit(solution)/shard_map/pair_step/pallas_call | solution.py:960
  152.0 0.0 copy-done
  152.1 0.8 multiply_subtract_fusion
  152.8 0.7 copy.22
  153.5 1.3 slice.7
  154.8 0.9 slice.6
  155.8 0.7 copy.21
  (3 shorter events, 0.0 us)
Async XLA Ops:
  8.5 143.5 %copy-start = (f32[12,8]{1,0:T(8,128)S(1)}, f32[12,8]{1,0:T(8,128)}, u32[]{:S(2)}) copy-start(f32[12,8]{1,0:T(8,128)} %copy.18.poses_ref) | copy-start | bytes 1156
